TPU v7x, 256 devices: a whole 4x4x8 slice. The times are simulated.
256 devices in a mesh: grp: 16 (over z, core), mem: 16 (over x, y).
Axes of the slice: x: 4, y: 4, z: 8, core: 2. Of those that a mesh axis runs over, the one named last changes fastest.
Arguments:
- tokens: bfloat16 [16384, 1024], P(('grp', 'mem')), may hold values from -6 to 6
- in_weight: bfloat16 [1024, 4096], replicated, may hold values from -0.1875 to 0.1875
- out_weight: bfloat16 [1024, 1024], replicated, may hold values from -0.1875 to 0.1875
- history_pool: bfloat16 [224, 512, 2048], P('grp', 'mem'), may hold values from -6 to 6
- position_bias: float32 [8, 14], replicated, may hold values from -2 to 2
- self_bias: float32 [8], replicated, may hold values from 2 to 6
- history_length: int32 [16], P('grp'), may hold values from 5633 to 7168, as said below
- candidate_count: int32 [16], P('grp'), may hold values from 256 to 1024, as said below
- block_slots: int32 [16, 16, 2], P('grp'), may hold values from -1 to 13, as said below
- block_position: int32 [16, 16, 2], P('grp'), may hold values from -1 to 13, as said below
Outputs:
- scored: bfloat16 [16384, 1024], P(('grp', 'mem'))
Inputs may be any that keep to these rules, and one draw needn't show every extreme that they name: `history_length`: the group with the longest history reaches 7168 tokens. `candidate_count`: some group has all 1024 slots real. `block_slots`: entries are indices into the 14 blocks owned by group o, or -1 for an empty slot; every pool block is listed at most once; at most 2 blocks go from one owner group to one scoring group, and in every draw some owner sends exactly 2; a group reads at most 14 blocks, and some group reads exactly 14. `block_position`: -1 exactly where block_slots is -1; for group d the positions 0 to ceil(history_length[d] / 512) - 1 each appear exactly once and no others.
All inputs are finite; a program needn't handle non-finite values.
Results may differ from a plain program's by a relative error of at most 0.014.
Values may be sent and summed in bfloat16 or wider, within the bound.
No kernel may reach another device: no remote copies, remote signals or barrier semaphores. Data moves between devices by JAX's collectives and lax.ppermute only.
A program may use at most 128 MiB of HBM per device.

v0:
```python
import jax
import jax.numpy as jnp
from jax import lax
from jax.sharding import PartitionSpec as P

epsilon = 1e-05


def layer_norm(values):
    center = values - jnp.mean(values, axis=-1, keepdims=True)
    spread = jnp.mean(center * center, axis=-1, keepdims=True)
    return center * lax.rsqrt(spread + epsilon)


def project(tokens, in_weight):
    normed = layer_norm(tokens.astype(jnp.float32)).astype(jnp.bfloat16)
    projected = jax.nn.silu(jnp.dot(normed, in_weight, preferred_element_type=jnp.float32))
    quarters = jnp.split(projected, 4, axis=1)
    return tuple((quarter.astype(jnp.bfloat16) for quarter in quarters))


def local(
    tokens,
    in_weight,
    out_weight,
    history_pool,
    position_bias,
    self_bias,
    history_length,
    candidate_count,
    block_slots,
    block_position,
):
    local_rows, model_width = tokens.shape
    head_count, block_count = position_bias.shape
    head_size = model_width // head_count
    score_scale = head_size ** (-0.5)
    gate_u, value_v, query_rows, key_new = project(tokens, in_weight)
    owned_blocks = history_pool.shape[0]
    slab_tokens = history_pool.shape[1]
    groups = lax.axis_size("grp")
    members = lax.axis_size("mem")
    my_slots = block_slots[0]
    my_positions = block_position[0]
    capacity = my_slots.shape[1]
    send_slots = lax.all_to_all(my_slots, "grp", split_axis=0, concat_axis=0, tiled=True)
    packed = history_pool[jnp.clip(send_slots, 0, owned_blocks - 1)]
    arrived = lax.all_to_all(packed, "grp", split_axis=0, concat_axis=0, tiled=True)
    arrived = arrived.reshape(groups * capacity, slab_tokens, 2 * model_width)
    positions = my_positions.reshape(groups * capacity)
    slot_count = arrived.shape[0]
    onehot = (positions[:, None] == jnp.arange(block_count, dtype=jnp.int32)[None, :]).astype(
        jnp.float32
    )
    slot_bias = jnp.dot(position_bias, onehot.T, precision=lax.Precision.HIGHEST)
    block_tokens = slab_tokens * members
    offsets = lax.axis_index("mem") * slab_tokens + jnp.arange(slab_tokens, dtype=jnp.int32)
    token_index = positions[:, None] * block_tokens + offsets[None, :]
    live_mask = (
        ((positions[:, None] >= 0) & (token_index < history_length[0]))
        .astype(jnp.float32)
        .reshape(slot_count * slab_tokens)
    )
    flattened = arrived.reshape(slot_count * slab_tokens, 2 * model_width)
    keys_hist = flattened[:, :model_width].reshape(-1, head_count, head_size)
    values_hist = flattened[:, model_width:].reshape(-1, head_count, head_size)
    token_bias = jnp.repeat(slot_bias, slab_tokens, axis=1)
    whole_query = lax.all_gather(query_rows, "mem", axis=0, tiled=True)
    row_count = local_rows * lax.axis_size("mem")
    block_query = whole_query.reshape(row_count, head_count, head_size)
    scores = jnp.einsum("nhd,khd->hnk", block_query, keys_hist, preferred_element_type=jnp.float32)
    weights = (
        jax.nn.silu(scores * score_scale + token_bias[:, None, :]) * live_mask[None, None, :]
    ).astype(jnp.bfloat16)
    combined = jnp.einsum("hnk,khd->nhd", weights, values_hist, preferred_element_type=jnp.float32)
    history_term = lax.psum_scatter(
        combined.reshape(row_count, model_width).astype(jnp.bfloat16),
        "mem",
        scatter_dimension=0,
        tiled=True,
    ).astype(jnp.float32)
    query_heads = query_rows.astype(jnp.float32).reshape(local_rows, head_count, head_size)
    key_heads = key_new.astype(jnp.float32).reshape(local_rows, head_count, head_size)
    value_heads = value_v.astype(jnp.float32).reshape(local_rows, head_count, head_size)
    self_weight = jax.nn.silu(
        jnp.sum(query_heads * key_heads, axis=2) * score_scale + self_bias[None, :]
    )
    attended = history_term + (self_weight[:, :, None] * value_heads).reshape(
        local_rows, model_width
    )
    gated = (layer_norm(attended) * gate_u.astype(jnp.float32)).astype(jnp.bfloat16)
    output = jnp.dot(gated, out_weight, preferred_element_type=jnp.float32) + tokens.astype(
        jnp.float32
    )
    row_index = lax.axis_index("mem") * local_rows + jnp.arange(local_rows, dtype=jnp.int32)
    return jnp.where(row_index[:, None] < candidate_count[0], output, 0.0).astype(jnp.bfloat16)


def solution(mesh):
    placed = (
        P(("grp", "mem"), None),
        P(),
        P(),
        P("grp", "mem", None),
        P(),
        P(),
        P("grp"),
        P("grp"),
        P("grp", None, None),
        P("grp", None, None),
    )
    return jax.shard_map(
        local, mesh=mesh, in_specs=placed, out_specs=P(("grp", "mem"), None), check_vma=False
    )
```

profile of v0, /device:TPU:2, one launch (start us, length us, event | category | flops | bytes accessed | tf_op | source)
XLA Modules:
  0.0 251.5 jit_solution(14958187405748815500)
XLA Ops:
  6.5 0.0 copy-start
  6.5 0.9 copy.42
  7.4 15.9 %all_to_all.14 = s32[16,1,2]{2,1,0:T(1,128)S(1)} all-to-all(s32[16,1,2]{2,1,0:T(1,128)S(1)} %copy.42), channel_id=1, replica_groups=mesh['grp'=16,'mem'=16] {'grp'}, dimensions={0} | all-to-all | bytes 256 | tf_op jit(solution)/shard_map/all_to_all | solution.py:46
  23.4 0.1 copy.43
  23.5 0.1 copy.44
  23.6 0.1 reshape.146
  23.7 4.3 %gather_fusion = bf16[32,32,2048]{2,1,0:T(8,128)(2,1)} fusion(bf16[14,32,2048]{2,1,0:T(8,128)(2,1)} %param.13, s32[1024]{0:T(1024)S(1)} %pad_clamp_fusion), kind=kCustom, calls=%fused_computation | custom fusion | bytes 8388736 | tf_op jit(solution)/shard_map/gather | solution.py:47
  27.9 0.0 copy-start.1
  27.9 4.7 %all-to-all-start.1 = ((bf16[16,2,32,2048]{3,2,1,0:T(8,128)(2,1)}), bf16[16,2,32,2048]{3,2,1,0:T(8,128)(2,1)}, u32[]{:S(2)}, u32[]{:S(2)}) async-start(bf16[16,2,32,2048]{3,2,1,0:T(8,128)(2,1)} %bitcast.49), calls=%async_computation.1 | async-start | bytes 8388608 | tf_op jit(solution)/shard_map/all_to_all | solution.py:48
  32.6 0.0 all-gather.2.cloned.1.call-start
  32.7 0.0 copy-done.1
  32.7 0.1 convert_reduce_fusion
  32.8 0.2 fusion.14
  33.0 0.0 copy-start.2
  33.0 0.0 copy-start.4
  33.0 5.1 %multiply_convert_fusion.4 = bf16[64,4096]{1,0:T(8,128)(2,1)S(1)} fusion(bf16[1024,4096]{1,0:T(8,128)(2,1)} %param.11, bf16[64,1024]{1,0:T(8,128)(2,1)S(1)} %copy-done.1, f32[64]{0:T(128)S(1)} %add_rsqrt_fusion.1, f32[64]{0:T(128)S(1)} %broadcast_multiply_fusion.2), kind=kOutput, calls=%fused_computation.11 | convolution fusion | flops 538443776 | bytes 9044480 | tf_op jit(solution)/shard_map/dot_general | solution.py:17
  38.1 0.7 split.20
  38.8 0.0 all-gather.2.cloned.1.call-update
  38.8 0.2 reduce-scatter.2.cloned.1.call-start
  39.7 0.0 copy-done.2
  39.7 0.1 copy.49
  39.8 0.1 eq.15
  39.9 0.1 fusion.27
  40.0 0.1 reshape.143
  40.1 0.0 copy-done.4
  40.1 0.2 convolution_bitcast_fusion
  40.2 0.1 broadcast_in_dim.11
  40.4 0.1 add.119
  40.5 86.4 %all-to-all-done.1 = bf16[16,2,32,2048]{3,2,1,0:T(8,128)(2,1)} async-done(((bf16[16,2,32,2048]{3,2,1,0:T(8,128)(2,1)}), bf16[16,2,32,2048]{3,2,1,0:T(8,128)(2,1)}, u32[]{:S(2)}, u32[]{:S(2)}) %all-to-all-start.1) | async-done | bytes 4194336 | tf_op jit(solution)/shard_map/all_to_all | solution.py:48
  126.9 4.6 %fusion.33 = (bf16[1024,1024]{1,0:T(8,128)(2,1)}, bf16[1024,1024]{1,0:T(8,128)(2,1)}) fusion(bf16[1024,2048]{1,0:T(8,128)(2,1)} %bitcast.4), kind=kLoop, calls=%fused_computation.48 | loop fusion | bytes 8388608 | tf_op jit(solution)/shard_map/slice | solution.py:65
  131.5 4.0 %copy.45 = bf16[1024,1024]{0,1:T(8,128)(2,1)} copy(bf16[1024,1024]{1,0:T(8,128)(2,1)} %get-tuple-element.6) | data formatting | bytes 4194304 | tf_op jit(solution)/shard_map/slice | solution.py:66
  135.5 4.0 %copy.46 = bf16[1024,1024]{0,1:T(8,128)(2,1)} copy(bf16[1024,1024]{1,0:T(8,128)(2,1)} %get-tuple-element.5) | data formatting | bytes 4194304 | tf_op jit(solution)/shard_map/slice | solution.py:65
  139.4 0.0 all-gather.2.cloned.1.call-done
  139.4 18.5 %fusion.7 = bf16[8,128,1024]{2,1,0:T(8,128)(2,1)} fusion(bf16[1024,8,128]{0,2,1:T(8,128)(2,1)} %bitcast.53, f32[1024]{0:T(1024)S(1)} %reshape.143, f32[8,1024]{1,0:T(8,128)S(1)} %add.119, bf16[1024,8,128]{0,2,1:T(8,128)(2,1)} %bitcast.54, bf16[1024,1024]{1,0:T(8,128)(2,1)} %all-gather.2.cloned.1.call-done), kind=kOutput, calls=%fused_computation.6 | convolution fusion | flops 4363124736 | bytes 8425472 | tf_op jit(solution)/shard_map/hnk,khd->nhd/dot_general | solution.py:75
  157.9 4.0 %copy.54 = bf16[1024,1024]{1,0:T(8,128)(2,1)} copy(bf16[1024,1024]{0,1:T(8,128)(2,1)} %bitcast.55) | data formatting | bytes 4194304 | tf_op jit(solution)/shard_map/convert_element_type | solution.py:77
  161.9 0.0 copy-start.3
  161.9 0.0 reduce-scatter.2.cloned.1.call-update
  162.0 0.1 reduce_sum.47
  162.1 0.1 copy.51
  162.2 0.3 copy-done.3
  162.5 0.1 divide_multiply_fusion
  162.6 0.1 copy.52
  163.4 76.8 %reduce-scatter.2.cloned.1.call-done = bf16[64,1024]{1,0:T(8,128)(2,1)} async-done(((bf16[1024,1024]{1,0:T(8,128)(2,1)}), bf16[64,1024]{1,0:T(8,128)(2,1)}) %reduce-scatter.2.cloned.1.call-update) | async-done | bytes 131088 | tf_op jit(solution)/shard_map/reduce_scatter | solution.py:76
  240.2 0.1 mul.117
  240.3 1.1 fusion.32
  241.4 1.1 multiply_reduce_fusion
  242.5 0.0 copy-done
  242.5 2.1 fusion.11
  (11 shorter events, 0.1 us)
Async XLA Ops:
  6.5 236.0 %copy-start = (bf16[1024,1024]{1,0:T(8,128)(2,1)S(1)}, bf16[1024,1024]{1,0:T(8,128)(2,1)}, u32[]{:S(2)}) copy-start(bf16[1024,1024]{1,0:T(8,128)(2,1)} %param.12) | copy-start | bytes 6291460
  27.9 4.7 %copy-start.1 = (bf16[64,1024]{1,0:T(8,128)(2,1)S(1)}, bf16[64,1024]{1,0:T(8,128)(2,1)}, u32[]{:S(2)}) copy-start(bf16[64,1024]{1,0:T(8,128)(2,1)} %param.10) | copy-start | bytes 393220
  27.9 98.9 %all-to-all-start.1 = ((bf16[16,2,32,2048]{3,2,1,0:T(8,128)(2,1)}), bf16[16,2,32,2048]{3,2,1,0:T(8,128)(2,1)}, u32[]{:S(2)}, u32[]{:S(2)}) async-start(bf16[16,2,32,2048]{3,2,1,0:T(8,128)(2,1)} %bitcast.49), calls=%async_computation.1 | async-start | bytes 8388608 | tf_op jit(solution)/shard_map/all_to_all | solution.py:48
  32.6 106.8 %all-gather.2.cloned.1.call-start = ((), (), s32[]{:S(2)}) async-start(), calls=%async_computation.3 | async-start | bytes 2228224 | tf_op jit(solution)/shard_map/all_gather | solution.py:68
  33.0 6.7 %copy-start.2 = (s32[1,16,2]{1,2,0:T(2,128)S(1)}, s32[1,16,2]{1,2,0:T(2,128)}, u32[]{:S(2)}) copy-start(s32[1,16,2]{1,2,0:T(2,128)} %param.19) | copy-start | bytes 388
  33.0 7.0 %copy-start.4 = (f32[8,14]{1,0:T(8,128)S(1)}, f32[8,14]{1,0:T(8,128)}, u32[]{:S(2)}) copy-start(f32[8,14]{1,0:T(8,128)} %param.14) | copy-start | bytes 1348
  38.8 201.4 %reduce-scatter.2.cloned.1.call-start = ((), (), s32[]{:S(2)}) async-start(), calls=%async_computation.4 | async-start | bytes 2228224 | tf_op jit(solution)/shard_map/reduce_scatter | solution.py:76
  161.9 0.7 copy-start.3
Sparse Core Ops, SparseCore 0:
  38.9 51.0 all-gather.1
  162.0 78.1 reduce-scatter.1
where the time goes:
time: 252 us
  waiting for transfers between devices  163 us (65%)
  matrix products  25.9 us (10%)
  local copies, waits for them, and re-layouts  23.7 us (9%)
  blocking collectives  15.9 us (6%)
  between operations  14.9 us (6%)
  starting transfers between devices  4.93 us (2%)
  other arithmetic  2.87 us (1%)
    all_to_all x1, waiting for transfers between devices, local(): lax.all_to_all(packed, 'grp', split_axis=0, concat_axis=0, tiled=True)  86.4 us
    reduce_scatter x1, waiting for transfers between devices, local(): lax.psum_scatter(combined.reshape(row_count, model_width).astype(jnp.bflo...  76.8 us
    dot_general x1, matrix products, local(): jnp.einsum('hnk,khd->nhd', weights, values_hist, preferred_element_type=j...  18.5 us
    all_to_all x1, blocking collectives, local(): lax.all_to_all(my_slots, 'grp', split_axis=0, concat_axis=0, tiled=True)  15.9 us
    slice x2, local copies, waits for them, and re-layouts, local(): keys_hist = flattened[:, :model_width].reshape(-1, head_count, head_size)  8.58 us
    dot_general x1, matrix products, project(): jnp.dot(normed, in_weight, preferred_element_type=jnp.float32)  5.07 us
  transfers between devices with their start and end apart: 3, of which 2 were waited for; matrix products, arithmetic and copies ran while one was open for 8% of the time, Pallas kernels for 0%

commit v1 on v0

v1 whole, which is shorter than its diff:
```python
import jax
import jax.numpy as jnp
from jax import lax
from jax.experimental import pallas as pl
from jax.experimental.pallas import tpu as pltpu
from jax.sharding import Mesh, PartitionSpec as P

D = 1024
HEADS = 8
HEAD = 128
BLOCK = 512
BLK = 14
CAP = 2
NZ = 8
NG = 16
NM = 16
SLAB = 32
ROWS = 64
HALF = 512
EPS = 1e-05
SCALE = HEAD**-0.5
G = ("z", "core")
M = ("x", "y")
VM = pl.BlockSpec(memory_space=pltpu.VMEM)
SM = pl.BlockSpec(memory_space=pltpu.SMEM)
ANY = pl.BlockSpec(memory_space=pl.ANY)


def params(mib):
    return pltpu.CompilerParams(vmem_limit_bytes=mib << 20)


def norm(values):
    center = values - jnp.mean(values, axis=-1, keepdims=True)
    spread = jnp.mean(center * center, axis=-1, keepdims=True)
    return center * lax.rsqrt(spread + EPS)


def silu(v):
    t = 0.5 * v
    return t + t * jnp.tanh(t)


def pack_kernel(pool, out, sems):
    copies = []
    for h in range(HEADS):
        for kv in range(2):
            for ch in range(2):
                copies.append(
                    pltpu.make_async_copy(
                        pool.at[:, :, pl.ds(kv * D + h * HEAD, HEAD)],
                        out.at[h * 2 + ch, kv],
                        sems.at[(h * 2 + kv) * 2 + ch],
                    )
                )
    for c in copies:
        c.start()
    for c in copies:
        c.wait()


def pack(pool):
    return pl.pallas_call(
        pack_kernel,
        out_shape=jax.ShapeDtypeStruct((NM, 2, BLK, SLAB, HEAD), jnp.bfloat16),
        in_specs=[ANY],
        out_specs=ANY,
        scratch_shapes=[pltpu.SemaphoreType.DMA((32,))],
        name="pack_history",
    )(pool)


def query_kernel(tokens, w, q_out, send_out):
    h2 = pl.program_id(0)
    normed = norm(tokens[...].astype(jnp.float32)).astype(jnp.bfloat16)
    q = silu(jnp.dot(normed, w[...], preferred_element_type=jnp.float32)).astype(jnp.bfloat16)
    q_out[...] = q
    for j in range(2):
        for ch in range(2):
            send_out[j * 2 + ch] = q[ch * 32 : ch * 32 + 32, j * HEAD : (j + 1) * HEAD]


def query(tokens, w):
    return pl.pallas_call(
        query_kernel,
        grid=(4,),
        out_shape=(
            jax.ShapeDtypeStruct((ROWS, D), jnp.bfloat16),
            jax.ShapeDtypeStruct((NM, 32, HEAD), jnp.bfloat16),
        ),
        in_specs=[
            pl.BlockSpec((ROWS, D), lambda i: (0, 0)),
            pl.BlockSpec((D, 256), lambda i: (0, 8 + i)),
        ],
        out_specs=(
            pl.BlockSpec((ROWS, 256), lambda i: (0, i)),
            pl.BlockSpec((4, 32, HEAD), lambda i: (i, 0, 0)),
        ),
        compiler_params=params(16),
        name="project_query",
    )(tokens, w)


def rest_kernel(tokens, wu, wv, wk, q, self_bias, gate_out, self_out):
    i = pl.program_id(0)
    normed = norm(tokens[...].astype(jnp.float32)).astype(jnp.bfloat16)

    def proj(w):
        return silu(jnp.dot(normed, w[...], preferred_element_type=jnp.float32)).astype(jnp.bfloat16)

    gate_out[...] = proj(wu)
    v = proj(wv).astype(jnp.float32)
    k = proj(wk).astype(jnp.float32)
    qk = q[...].astype(jnp.float32) * k
    for j in range(2):
        cols = slice(j * HEAD, (j + 1) * HEAD)
        s = jnp.sum(qk[:, cols], axis=1, keepdims=True) * SCALE + self_bias[i * 2 + j]
        self_out[:, cols] = silu(s) * v[:, cols]


def rest(tokens, w, q, self_bias):
    return pl.pallas_call(
        rest_kernel,
        grid=(4,),
        out_shape=(
            jax.ShapeDtypeStruct((ROWS, D), jnp.bfloat16),
            jax.ShapeDtypeStruct((ROWS, D), jnp.float32),
        ),
        in_specs=[
            pl.BlockSpec((ROWS, D), lambda i: (0, 0)),
            pl.BlockSpec((D, 256), lambda i: (0, i)),
            pl.BlockSpec((D, 256), lambda i: (0, 4 + i)),
            pl.BlockSpec((D, 256), lambda i: (0, 12 + i)),
            pl.BlockSpec((ROWS, 256), lambda i: (0, i)),
            SM,
        ],
        out_specs=(
            pl.BlockSpec((ROWS, 256), lambda i: (0, i)),
            pl.BlockSpec((ROWS, 256), lambda i: (0, i)),
        ),
        compiler_params=params(24),
        name="project_rest",
    )(tokens, w, w, w, q, self_bias)


def attend_kernel(tab, where, bias, q, kv, own, other, acc):
    z, core, h = where[0], where[1], where[2]
    o = z * 2 + core

    def one(d, out, s):
        acc[...] = jnp.zeros_like(acc)
        for c in range(CAP):
            slot = tab[d, o * CAP + c]

            @pl.when(slot >= 0)
            def _():
                p = tab[d, NG * CAP + o * CAP + c]
                limit = tab[d, 2 * NG * CAP] - p * BLOCK
                b = bias[h, p] * 0.5
                k = kv[:, 0, slot].reshape(BLOCK, HEAD)
                v = kv[:, 1, slot].reshape(BLOCK, HEAD)
                token = lax.broadcasted_iota(jnp.int32, (BLOCK, HEAD), 0)
                v = jnp.where(token < limit, v, jnp.zeros_like(v))
                for r in range(4):
                    rows = pl.ds(r * 128, 128)
                    scores = lax.dot_general(
                        q[d, rows], k, (((1,), (1,)), ((), ())), preferred_element_type=jnp.float32
                    )
                    t = scores * (0.5 * SCALE) + b
                    w = (t + t * jnp.tanh(t)).astype(jnp.bfloat16)
                    acc[rows] += jnp.dot(w, v, preferred_element_type=jnp.float32)

        out[s] = acc[...].astype(jnp.bfloat16)

    def step(s, carry):
        zz = lax.rem(z + s, NZ)
        one(zz * 2 + 1 - core, other, s)
        one(zz * 2 + core, own, s)
        return carry

    lax.fori_loop(0, NZ, step, 0)


def attend(tab, where, bias, q, kv):
    shape = jax.ShapeDtypeStruct((NZ, HALF, HEAD), jnp.bfloat16)
    return pl.pallas_call(
        attend_kernel,
        out_shape=(shape, shape),
        in_specs=[SM, SM, SM, VM, VM],
        out_specs=(VM, VM),
        scratch_shapes=[pltpu.VMEM((HALF, HEAD), jnp.float32)],
        compiler_params=params(32),
        name="attend",
    )(tab, where, bias, q, kv)


def pair_kernel(a, b, *outs):
    for s in range(NZ):
        outs[s][...] = (a[s].astype(jnp.float32) + b[s].astype(jnp.float32)).astype(jnp.bfloat16)


def pair(a, b):
    return pl.pallas_call(
        pair_kernel,
        out_shape=[jax.ShapeDtypeStruct((HALF, HEAD), jnp.bfloat16)] * NZ,
        in_specs=[VM, VM],
        out_specs=[VM] * NZ,
        compiler_params=params(16),
        name="add_pair",
    )(a, b)


def total_kernel(*refs):
    out = refs[-1]
    total = refs[0][...].astype(jnp.float32)
    for r in refs[1:-1]:
        total += r[...].astype(jnp.float32)
    out[...] = total.astype(jnp.bfloat16).reshape(NM, 32, HEAD)


def total(parts):
    return pl.pallas_call(
        total_kernel,
        out_shape=jax.ShapeDtypeStruct((NM, 32, HEAD), jnp.bfloat16),
        in_specs=[VM] * len(parts),
        out_specs=VM,
        compiler_params=params(16),
        name="add_groups",
    )(*parts)


def tail_kernel(hist, self_term, gate, tokens, w, where, count, out):
    cols = []
    for h in range(HEADS):
        cols.append(jnp.concatenate([hist[h * 2], hist[h * 2 + 1]], axis=0))
    attended = jnp.concatenate(cols, axis=1).astype(jnp.float32) + self_term[...]
    gated = (norm(attended) * gate[...].astype(jnp.float32)).astype(jnp.bfloat16)
    res = jnp.dot(gated, w[...], preferred_element_type=jnp.float32) + tokens[...].astype(jnp.float32)
    row = where[3] * ROWS + lax.broadcasted_iota(jnp.int32, (ROWS, D), 0)
    out[...] = jnp.where(row < count[0], res, 0.0).astype(jnp.bfloat16)


def tail(hist, self_term, gate, tokens, w, where, count):
    return pl.pallas_call(
        tail_kernel,
        out_shape=jax.ShapeDtypeStruct((ROWS, D), jnp.bfloat16),
        in_specs=[VM, VM, VM, VM, VM, SM, SM],
        out_specs=VM,
        compiler_params=params(16),
        name="output",
    )(hist, self_term, gate, tokens, w, where, count)


def local(
    tokens,
    in_weight,
    out_weight,
    history_pool,
    position_bias,
    self_bias,
    history_length,
    candidate_count,
    block_slots,
    block_position,
):
    z, core, m = lax.axis_index("z"), lax.axis_index("core"), lax.axis_index(M)
    where = jnp.stack([z, core, m // 2, m]).astype(jnp.int32)
    mine = jnp.concatenate(
        [
            block_slots.reshape(1, NG * CAP),
            block_position.reshape(1, NG * CAP),
            jnp.broadcast_to(history_length[:, None], (1, 64)),
        ],
        axis=1,
    )
    tab = lax.all_gather(mine, G, axis=0, tiled=True)
    packed = pack(history_pool)
    kv = lax.all_to_all(packed, M, split_axis=0, concat_axis=0, tiled=True)
    q, q_send = query(tokens, in_weight)
    q_mine = lax.all_to_all(q_send, M, split_axis=0, concat_axis=0, tiled=True)
    q_all = lax.all_gather(q_mine.reshape(1, HALF, HEAD), G, axis=0, tiled=True)
    gate, self_term = rest(tokens, in_weight, q, self_bias)
    own, other = attend(tab, where, position_bias, q_all, kv)
    other = lax.ppermute(other, "core", [(0, 1), (1, 0)])
    sums = pair(own, other)
    parts = [sums[0]]
    for s in range(1, NZ):
        parts.append(lax.ppermute(sums[s], "z", [(i, (i + s) % NZ) for i in range(NZ)]))
    hist = lax.all_to_all(total(parts), M, split_axis=0, concat_axis=0, tiled=True)
    return tail(hist, self_term, gate, tokens, out_weight, where, candidate_count)


def solution(mesh):
    fine = Mesh(mesh.devices.reshape(NZ, 2, 4, 4), ("z", "core", "x", "y"))
    placed = (
        P(("z", "core", "x", "y"), None),
        P(),
        P(),
        P(("z", "core"), ("x", "y"), None),
        P(),
        P(),
        P(("z", "core")),
        P(("z", "core")),
        P(("z", "core"), None, None),
        P(("z", "core"), None, None),
    )
    return jax.shard_map(
        local, mesh=fine, in_specs=placed, out_specs=P(("z", "core", "x", "y"), None), check_vma=False
    )
```

time: 252 us -> 270 us (1.071)
  Pallas kernels: 0 us -> 135 us
  waiting for transfers between devices: 163 us -> 42.3 us
  starting transfers between devices: 4.93 us -> 34 us
  matrix products: 25.9 us -> 0 us
  blocking collectives: 15.9 us -> 33.6 us
  local copies, waits for them, and re-layouts: 23.7 us -> 9.63 us
  other arithmetic: 2.87 us -> 0.15 us
    pallas_call x0 -> x7, Pallas kernels: none -> 135 us  [the longest x1 113 us: pack(): pl.pallas_call(pack_kernel, out_shape=jax.ShapeDtypeStruct((NM, 2, BLK, S...]
    reduce_scatter x1 -> x0, waiting for transfers between devices: 76.8 us -> none  [local(): lax.psum_scatter(combined.reshape(row_count, model_width).astype(jnp.bflo...]
    all_to_all x1 -> x2, waiting for transfers between devices: 86.4 us -> 23.5 us  [the longest x1 23.5 us: local(): kv = lax.all_to_all(packed, M, split_axis=0, concat_axis=0, tiled=True)]
    dot_general x4 -> x0, matrix products: 25.9 us -> none  [the longest x1 18.5 us: local(): jnp.einsum('hnk,khd->nhd', weights, values_hist, preferred_element_type=j...]
    ppermute x0 -> x8, starting transfers between devices: none -> 20.2 us  [the longest x7 20.1 us: local(): lax.ppermute(sums[s], 'z', [(i, (i + s) % NZ) for i in range(NZ)])]
    all_gather x0 -> x1, blocking collectives: none -> 19.9 us  [local(): tab = lax.all_gather(mine, G, axis=0, tiled=True)]
    ppermute x0 -> x8, waiting for transfers between devices: none -> 18.7 us  [the longest x7 16.1 us: local(): lax.ppermute(sums[s], 'z', [(i, (i + s) % NZ) for i in range(NZ)])]
    slice x3 -> x0, local copies, waits for them, and re-layouts: 12.5 us -> none  [the longest x2 8.58 us: local(): keys_hist = flattened[:, :model_width].reshape(-1, head_count, head_size)]
  transfers between devices with their start and end apart: 3 -> 11, of which waited for: 2 -> 7; matrix products, arithmetic and copies ran while one was open for 8% -> 0% of each run, Pallas kernels for 0% -> 43%
where the time goes in v1:
time: 270 us
  Pallas kernels  135 us (50%)
  waiting for transfers between devices  42.3 us (16%)
  starting transfers between devices  34 us (13%)
  blocking collectives  33.6 us (12%)
  between operations  14.9 us (6%)
  local copies, waits for them, and re-layouts  9.63 us (4%)
    pallas_call x1, Pallas kernels, pack(): pl.pallas_call(pack_kernel, out_shape=jax.ShapeDtypeStruct((NM, 2, BLK, S...  113 us
    all_to_all x1, waiting for transfers between devices, local(): kv = lax.all_to_all(packed, M, split_axis=0, concat_axis=0, tiled=True)  23.5 us
    ppermute x7, starting transfers between devices, local(): lax.ppermute(sums[s], 'z', [(i, (i + s) % NZ) for i in range(NZ)])  20.1 us
    all_gather x1, blocking collectives, local(): tab = lax.all_gather(mine, G, axis=0, tiled=True)  19.9 us
    ppermute x7, waiting for transfers between devices, local(): lax.ppermute(sums[s], 'z', [(i, (i + s) % NZ) for i in range(NZ)])  16.1 us
    all_to_all x1, blocking collectives, local(): q_mine = lax.all_to_all(q_send, M, split_axis=0, concat_axis=0, tiled=True)  13.8 us
    pallas_call x1, Pallas kernels, attend(): pl.pallas_call(attend_kernel, out_shape=(shape, shape), in_specs=[SM, SM,...  13.6 us
    unnamed x22, local copies, waits for them, and re-layouts  9.45 us
  transfers between devices with their start and end apart: 11, of which 7 were waited for; matrix products, arithmetic and copies ran while one was open for 0% of the time, Pallas kernels for 43%

profile of v1, /device:TPU:2, one launch (start us, length us, event | category | flops | bytes accessed | tf_op | source)
XLA Modules:
  0.0 269.5 jit_solution(4556631424399918486)
XLA Ops:
  6.5 0.0 all-gather.3.cloned.1.call-start
  6.5 3.4 %copy-done = bf16[1024,4096]{1,0:T(8,128)(2,1)S(1)} copy-done((bf16[1024,4096]{1,0:T(8,128)(2,1)S(1)}, bf16[1024,4096]{1,0:T(8,128)(2,1)}, u32[]{:S(2)}) %copy-start) | copy-done | bytes 8388632
  9.9 0.9 copy-done.4
  10.8 1.9 project_query.1
  12.7 13.8 %all_to_all.15 = bf16[16,32,128]{2,1,0:T(8,128)(2,1)} all-to-all(bf16[16,32,128]{2,1,0:T(8,128)(2,1)S(1)} %get-tuple-element.19), channel_id=1, replica_groups=mesh['z'=8,'core'=2,'x'=4,'y'=4] {'x','y'}, dimensions={0} | all-to-all | bytes 262144 | tf_op jit(solution)/shard_map/all_to_all | solution.py:280
  26.5 0.0 all-gather.3.cloned.1.call-update
  26.5 112.6 %pack_history.1 = bf16[16,2,14,32,128]{4,3,2,1,0:T(8,128)(2,1)} custom-call(bf16[14,32,2048]{2,1,0:T(8,128)(2,1)} %pool.1), custom_call_target="tpu_custom_call" | custom-call | tf_op jit(solution)/shard_map/pack_history/pallas_call | solution.py:63
  139.1 0.0 copy-start.8
  139.1 0.0 copy-start.9
  139.1 0.0 copy-start.6
  139.1 6.0 %all-to-all-start.1 = ((bf16[16,2,14,32,128]{4,3,2,1,0:T(8,128)(2,1)}), bf16[16,2,14,32,128]{4,3,2,1,0:T(8,128)(2,1)}, u32[]{:S(2)}, u32[]{:S(2)}) async-start(bf16[16,2,14,32,128]{4,3,2,1,0:T(8,128)(2,1)} %pack_history.1), calls=%async_computation.1 | async-start | bytes 7340032 | tf_op jit(solution)/shard_map/all_to_all | solution.py:278
  145.1 0.0 copy-done.8
  145.1 0.1 copy.17
  145.2 0.1 reshape.12
  145.3 0.0 copy-done.9
  145.3 0.1 copy.18
  145.4 0.1 reshape.13
  146.1 0.1 fusion
  146.2 19.9 %all-gather = s32[16,1,128]{2,1,0:T(1,128)S(1)} all-gather(s32[1,1,128]{2,1,0:T(1,128)S(1)} %fusion), channel_id=1, replica_groups=mesh['z'=8,'core'=2,'x'=4,'y'=4] {'z','core'}, dimensions={0}, use_global_device_ids=true | all-gather | bytes 8704 | tf_op jit(solution)/shard_map/all_gather | solution.py:276
  166.1 0.1 pad_add_fusion.where
  166.1 23.5 %all-to-all-done.1.kv = bf16[16,2,14,32,128]{4,3,2,1,0:T(8,128)(2,1)} async-done(((bf16[16,2,14,32,128]{4,3,2,1,0:T(8,128)(2,1)}), bf16[16,2,14,32,128]{4,3,2,1,0:T(8,128)(2,1)}, u32[]{:S(2)}, u32[]{:S(2)}) %all-to-all-start.1) | async-done | bytes 3670048 | tf_op jit(solution)/shard_map/all_to_all | solution.py:278
  189.7 0.0 copy-done.6
  189.7 1.6 copy-done.3
  191.3 13.6 %attend.1 = (bf16[8,512,128]{2,1,0:T(8,128)(2,1)S(1)}, bf16[8,512,128]{2,1,0:T(8,128)(2,1)S(1)}) custom-call(s32[16,128]{1,0:T(8,128)S(1)} %bitcast.14, s32[4]{0:T(128)S(1)} %pad_add_fusion.where, f32[8,14]{1,0:T(8,128)S(1)} %copy-done.6, bf16[16,512,128]{2,1,0:T(8,128)(2,1)S(1)} %copy-done.3, bf16[16,2,14,32,128]{4,3,2,1,0:T(8,128)(2,1)} %all-to-all-done.1.kv), custom_call_target="tpu_custom_call" | custom-call | tf_op jit(solution)/shard_map/attend/pallas_call | solution.py:186
  204.9 0.1 collective-permute-start
  205.0 2.6 collective-permute-done.b
  207.6 0.2 add_pair.1
  207.9 3.8 %collective-permute-start.1 = (bf16[512,128]{1,0:T(8,128)(2,1)S(1)}, bf16[512,128]{1,0:T(8,128)(2,1)S(1)}, u32[]{:S(2)}, u32[]{:S(2)}) collective-permute-start(bf16[512,128]{1,0:T(8,128)(2,1)S(1)} %get-tuple-element.23), channel_id=1, source_target_pairs={{0,32},{32,64},{64,96},{96,128},{128,160},{160,192},{192,224},{224... | collective-permute-start | bytes 393224 | tf_op jit(solution)/shard_map/ppermute | solution.py:288
  211.7 3.3 %collective-permute-start.2 = (bf16[512,128]{1,0:T(8,128)(2,1)S(1)}, bf16[512,128]{1,0:T(8,128)(2,1)S(1)}, u32[]{:S(2)}, u32[]{:S(2)}) collective-permute-start(bf16[512,128]{1,0:T(8,128)(2,1)S(1)} %get-tuple-element.24), channel_id=1, source_target_pairs={{0,64},{32,96},{64,128},{96,160},{128,192},{160,224},{192,0},{224,... | collective-permute-start | bytes 393224 | tf_op jit(solution)/shard_map/ppermute | solution.py:288
  215.0 3.1 %collective-permute-start.3 = (bf16[512,128]{1,0:T(8,128)(2,1)S(1)}, bf16[512,128]{1,0:T(8,128)(2,1)S(1)}, u32[]{:S(2)}, u32[]{:S(2)}) collective-permute-start(bf16[512,128]{1,0:T(8,128)(2,1)S(1)} %get-tuple-element.25), channel_id=1, source_target_pairs={{0,96},{32,128},{64,160},{96,192},{128,224},{160,0},{192,32},{224,... | collective-permute-start | bytes 393224 | tf_op jit(solution)/shard_map/ppermute | solution.py:288
  218.1 1.4 collective-permute-start.4
  219.4 5.0 %collective-permute-start.5 = (bf16[512,128]{1,0:T(8,128)(2,1)S(1)}, bf16[512,128]{1,0:T(8,128)(2,1)S(1)}, u32[]{:S(2)}, u32[]{:S(2)}) collective-permute-start(bf16[512,128]{1,0:T(8,128)(2,1)S(1)} %get-tuple-element.27), channel_id=1, source_target_pairs={{0,160},{32,192},{64,224},{96,0},{128,32},{160,64},{192,96},{224,1... | collective-permute-start | bytes 393224 | tf_op jit(solution)/shard_map/ppermute | solution.py:288
  224.5 0.0 collective-permute-done.1.refs_1_
  224.5 1.8 collective-permute-start.6
  226.3 2.6 collective-permute-done.2.refs_2_
  228.9 1.8 collective-permute-start.7
  230.6 5.5 %collective-permute-done.3.refs_3_ = bf16[512,128]{1,0:T(8,128)(2,1)S(1)} collective-permute-done((bf16[512,128]{1,0:T(8,128)(2,1)S(1)}, bf16[512,128]{1,0:T(8,128)(2,1)S(1)}, u32[]{:S(2)}, u32[]{:S(2)}) %collective-permute-start.3) | collective-permute-done | bytes 131104 | tf_op jit(solution)/shard_map/ppermute | solution.py:288
  236.2 0.0 collective-permute-done.4.refs_4_
  236.2 2.5 collective-permute-done.5.refs_5_
  238.7 4.0 %collective-permute-done.6.refs_6_ = bf16[512,128]{1,0:T(8,128)(2,1)S(1)} collective-permute-done((bf16[512,128]{1,0:T(8,128)(2,1)S(1)}, bf16[512,128]{1,0:T(8,128)(2,1)S(1)}, u32[]{:S(2)}, u32[]{:S(2)}) %collective-permute-start.6) | collective-permute-done | bytes 131104 | tf_op jit(solution)/shard_map/ppermute | solution.py:288
  242.7 1.3 collective-permute-done.7.refs_7_
  244.1 0.8 add_groups.1
  244.9 7.8 %all-to-all-start.2 = ((bf16[16,32,128]{2,1,0:T(8,128)(2,1)}), bf16[16,32,128]{2,1,0:T(8,128)(2,1)S(1)}, u32[]{:S(2)}, u32[]{:S(2)}) async-start(bf16[16,32,128]{2,1,0:T(8,128)(2,1)} %add_groups.1), calls=%async_computation.2 | async-start | bytes 262144 | tf_op jit(solution)/shard_map/all_to_all | solution.py:289
  253.4 0.0 copy-start.1
  253.4 3.4 %copy-done.1 = bf16[1024,4096]{1,0:T(8,128)(2,1)S(1)} copy-done((bf16[1024,4096]{1,0:T(8,128)(2,1)S(1)}, bf16[1024,4096]{1,0:T(8,128)(2,1)}, u32[]{:S(2)}) %copy-start.1) | copy-done | bytes 8388632
  256.8 4.0 %project_rest.1 = (bf16[64,1024]{1,0:T(8,128)(2,1)S(1)}, f32[64,1024]{1,0:T(8,128)S(1)}) custom-call(bf16[64,1024]{1,0:T(8,128)(2,1)S(1)} %copy-done.5, bf16[1024,4096]{1,0:T(8,128)(2,1)S(1)} %copy-done.1, bf16[1024,4096]{1,0:T(8,128)(2,1)S(1)} %copy-done.1, bf16[1024,4096]{1,0:T(8,128)(2,1)S(1)} %copy-done.1, bf16[64,1024]{1,0:T(8,128)(2,1)S(1)} %get-tuple-element.30.q, ...), custom_call_target="tpu_custom_call" | custom-call | tf_op jit(solution)/shard_map/project_rest/pallas_call | solution.py:122
  260.8 0.0 all-to-all-done.2.hist
  260.8 1.9 output.1
  (11 shorter events, 0.0 us)
Async XLA Ops:
  6.5 183.1 %all-gather.3.cloned.1.call-start = ((), (), s32[]{:S(2)}) async-start(), calls=%async_computation.3 | async-start | bytes 2228224 | tf_op jit(solution)/shard_map/all_gather | solution.py:281
  6.5 3.4 %copy-start = (bf16[1024,4096]{1,0:T(8,128)(2,1)S(1)}, bf16[1024,4096]{1,0:T(8,128)(2,1)}, u32[]{:S(2)}) copy-start(bf16[1024,4096]{1,0:T(8,128)(2,1)} %wk.1) | copy-start | bytes 25165828
  9.9 0.9 copy-start.4
  139.1 6.0 %copy-start.8 = (s32[1,16,2]{1,2,0:T(2,128)S(1)}, s32[1,16,2]{1,2,0:T(2,128)}, u32[]{:S(2)}) copy-start(s32[1,16,2]{1,2,0:T(2,128)} %param.18) | copy-start | bytes 388
  139.1 6.2 %copy-start.9 = (s32[1,16,2]{1,2,0:T(2,128)S(1)}, s32[1,16,2]{1,2,0:T(2,128)}, u32[]{:S(2)}) copy-start(s32[1,16,2]{1,2,0:T(2,128)} %param.19) | copy-start | bytes 388
  139.1 50.5 %copy-start.6 = (f32[8,14]{1,0:T(8,128)S(1)}, f32[8,14]{1,0:T(8,128)}, u32[]{:S(2)}) copy-start(f32[8,14]{1,0:T(8,128)} %bias.1) | copy-start | bytes 1348
  139.1 50.5 %all-to-all-start.1 = ((bf16[16,2,14,32,128]{4,3,2,1,0:T(8,128)(2,1)}), bf16[16,2,14,32,128]{4,3,2,1,0:T(8,128)(2,1)}, u32[]{:S(2)}, u32[]{:S(2)}) async-start(bf16[16,2,14,32,128]{4,3,2,1,0:T(8,128)(2,1)} %pack_history.1), calls=%async_computation.1 | async-start | bytes 7340032 | tf_op jit(solution)/shard_map/all_to_all | solution.py:278
  189.7 1.6 copy-start.3
  191.3 62.1 %copy-start.5 = (bf16[64,1024]{1,0:T(8,128)(2,1)S(1)}, bf16[64,1024]{1,0:T(8,128)(2,1)}, u32[]{:S(2)}) copy-start(bf16[64,1024]{1,0:T(8,128)(2,1)} %tokens.5) | copy-start | bytes 393220
  191.3 62.1 %copy-start.7 = (f32[8]{0:T(128)S(1)}, f32[8]{0:T(128)}, u32[]{:S(2)}) copy-start(f32[8]{0:T(128)} %self_bias.1) | copy-start | bytes 100
  204.9 2.7 %collective-permute-start = (bf16[8,512,128]{2,1,0:T(8,128)(2,1)S(1)}, bf16[8,512,128]{2,1,0:T(8,128)(2,1)S(1)}, u32[]{:S(2)}, u32[]{:S(2)}) collective-permute-start(bf16[8,512,128]{2,1,0:T(8,128)(2,1)S(1)} %get-tuple-element.21), channel_id=1, source_target_pairs={{0,16},{16,0},{1,17},{17,1},{2,18},{18,2},{3,19},{19,3},{4,20},{20... | collective-permute-start | bytes 3145736 | tf_op jit(solution)/shard_map/ppermute | solution.py:284
  207.9 16.6 %collective-permute-start.1 = (bf16[512,128]{1,0:T(8,128)(2,1)S(1)}, bf16[512,128]{1,0:T(8,128)(2,1)S(1)}, u32[]{:S(2)}, u32[]{:S(2)}) collective-permute-start(bf16[512,128]{1,0:T(8,128)(2,1)S(1)} %get-tuple-element.23), channel_id=1, source_target_pairs={{0,32},{32,64},{64,96},{96,128},{128,160},{160,192},{192,224},{224... | collective-permute-start | bytes 393224 | tf_op jit(solution)/shard_map/ppermute | solution.py:288
  211.7 17.2 %collective-permute-start.2 = (bf16[512,128]{1,0:T(8,128)(2,1)S(1)}, bf16[512,128]{1,0:T(8,128)(2,1)S(1)}, u32[]{:S(2)}, u32[]{:S(2)}) collective-permute-start(bf16[512,128]{1,0:T(8,128)(2,1)S(1)} %get-tuple-element.24), channel_id=1, source_target_pairs={{0,64},{32,96},{64,128},{96,160},{128,192},{160,224},{192,0},{224,... | collective-permute-start | bytes 393224 | tf_op jit(solution)/shard_map/ppermute | solution.py:288
  215.0 21.2 %collective-permute-start.3 = (bf16[512,128]{1,0:T(8,128)(2,1)S(1)}, bf16[512,128]{1,0:T(8,128)(2,1)S(1)}, u32[]{:S(2)}, u32[]{:S(2)}) collective-permute-start(bf16[512,128]{1,0:T(8,128)(2,1)S(1)} %get-tuple-element.25), channel_id=1, source_target_pairs={{0,96},{32,128},{64,160},{96,192},{128,224},{160,0},{192,32},{224,... | collective-permute-start | bytes 393224 | tf_op jit(solution)/shard_map/ppermute | solution.py:288
  218.1 18.1 %collective-permute-start.4 = (bf16[512,128]{1,0:T(8,128)(2,1)S(1)}, bf16[512,128]{1,0:T(8,128)(2,1)S(1)}, u32[]{:S(2)}, u32[]{:S(2)}) collective-permute-start(bf16[512,128]{1,0:T(8,128)(2,1)S(1)} %get-tuple-element.26), channel_id=1, source_target_pairs={{0,128},{32,160},{64,192},{96,224},{128,0},{160,32},{192,64},{224,... | collective-permute-start | bytes 393224 | tf_op jit(solution)/shard_map/ppermute | solution.py:288
  219.4 19.3 %collective-permute-start.5 = (bf16[512,128]{1,0:T(8,128)(2,1)S(1)}, bf16[512,128]{1,0:T(8,128)(2,1)S(1)}, u32[]{:S(2)}, u32[]{:S(2)}) collective-permute-start(bf16[512,128]{1,0:T(8,128)(2,1)S(1)} %get-tuple-element.27), channel_id=1, source_target_pairs={{0,160},{32,192},{64,224},{96,0},{128,32},{160,64},{192,96},{224,1... | collective-permute-start | bytes 393224 | tf_op jit(solution)/shard_map/ppermute | solution.py:288
  224.5 18.2 %collective-permute-start.6 = (bf16[512,128]{1,0:T(8,128)(2,1)S(1)}, bf16[512,128]{1,0:T(8,128)(2,1)S(1)}, u32[]{:S(2)}, u32[]{:S(2)}) collective-permute-start(bf16[512,128]{1,0:T(8,128)(2,1)S(1)} %get-tuple-element.28), channel_id=1, source_target_pairs={{0,192},{32,224},{64,0},{96,32},{128,64},{160,96},{192,128},{224,1... | collective-permute-start | bytes 393224 | tf_op jit(solution)/shard_map/ppermute | solution.py:288
  228.9 15.2 %collective-permute-start.7 = (bf16[512,128]{1,0:T(8,128)(2,1)S(1)}, bf16[512,128]{1,0:T(8,128)(2,1)S(1)}, u32[]{:S(2)}, u32[]{:S(2)}) collective-permute-start(bf16[512,128]{1,0:T(8,128)(2,1)S(1)} %get-tuple-element.29), channel_id=1, source_target_pairs={{0,224},{32,0},{64,32},{96,64},{128,96},{160,128},{192,160},{224,1... | collective-permute-start | bytes 393224 | tf_op jit(solution)/shard_map/ppermute | solution.py:288
  244.9 15.9 %all-to-all-start.2 = ((bf16[16,32,128]{2,1,0:T(8,128)(2,1)}), bf16[16,32,128]{2,1,0:T(8,128)(2,1)S(1)}, u32[]{:S(2)}, u32[]{:S(2)}) async-start(bf16[16,32,128]{2,1,0:T(8,128)(2,1)} %add_groups.1), calls=%async_computation.2 | async-start | bytes 262144 | tf_op jit(solution)/shard_map/all_to_all | solution.py:289
  253.4 3.4 %copy-start.1 = (bf16[1024,4096]{1,0:T(8,128)(2,1)S(1)}, bf16[1024,4096]{1,0:T(8,128)(2,1)}, u32[]{:S(2)}) copy-start(bf16[1024,4096]{1,0:T(8,128)(2,1)} %wk.1) | copy-start | bytes 25165828
  256.8 4.0 %copy-start.2 = (bf16[1024,1024]{1,0:T(8,128)(2,1)S(1)}, bf16[1024,1024]{1,0:T(8,128)(2,1)}, u32[]{:S(2)}) copy-start(bf16[1024,1024]{1,0:T(8,128)(2,1)} %w.3) | copy-start | bytes 6291460
Sparse Core Ops, SparseCore 0:
  26.7 116.4 all-gather.2

commit v2 on v1

v2 whole, which is shorter than its diff:
```python
import functools

import jax
import jax.numpy as jnp
from jax import lax
from jax.experimental import pallas as pl
from jax.experimental.pallas import tpu as pltpu
from jax.sharding import Mesh, PartitionSpec as P

D = 1024
HEADS = 8
HEAD = 128
BLOCK = 512
BLK = 14
CAP = 2
NZ = 8
NG = 16
NM = 16
SLAB = 32
ROWS = 64
HALF = 512
QROWS = 528
CUT = 256
EPS = 1e-05
SCALE = HEAD**-0.5
G = ("z", "core")
M = ("x", "y")
VM = pl.BlockSpec(memory_space=pltpu.VMEM)
SM = pl.BlockSpec(memory_space=pltpu.SMEM)
HB = pl.BlockSpec(memory_space=pltpu.HBM)


def params(mib):
    return pltpu.CompilerParams(vmem_limit_bytes=mib << 20)


def norm(values):
    center = values - jnp.mean(values, axis=-1, keepdims=True)
    spread = jnp.mean(center * center, axis=-1, keepdims=True)
    return center * lax.rsqrt(spread + EPS)


def silu(v):
    t = 0.5 * v
    return t + t * jnp.tanh(t)


def pack_kernel(pool, after, out):
    for h in range(HEADS):
        for kv in range(2):
            cols = pool[:, :, kv * D + h * HEAD : kv * D + (h + 1) * HEAD]
            for ch in range(2):
                out[h * 2 + ch, kv] = cols


def pack(pool, after):
    return pl.pallas_call(
        pack_kernel,
        out_shape=jax.ShapeDtypeStruct((NM, 2, BLK, SLAB, HEAD), jnp.bfloat16),
        in_specs=[VM, VM],
        out_specs=VM,
        compiler_params=params(16),
        name="pack_history",
    )(pool, after)


def query_kernel(tokens, w, q_out, send_out, buf, sems):
    copies = [
        pltpu.make_async_copy(w.at[:, pl.ds(2 * D + i * 256, 256)], buf.at[i], sems.at[i]) for i in range(4)
    ]
    for c in copies:
        c.start()
    normed = norm(tokens[...].astype(jnp.float32)).astype(jnp.bfloat16)
    for i in range(4):
        copies[i].wait()
        q = silu(jnp.dot(normed, buf[i], preferred_element_type=jnp.float32)).astype(jnp.bfloat16)
        q_out[:, i * 256 : (i + 1) * 256] = q
        for j in range(2):
            for ch in range(2):
                send_out[i * 4 + j * 2 + ch] = q[ch * 32 : ch * 32 + 32, j * HEAD : (j + 1) * HEAD]


def query(tokens, w):
    return pl.pallas_call(
        query_kernel,
        out_shape=(
            jax.ShapeDtypeStruct((ROWS, D), jnp.bfloat16),
            jax.ShapeDtypeStruct((NM, 32, HEAD), jnp.bfloat16),
        ),
        in_specs=[VM, HB],
        out_specs=(VM, VM),
        scratch_shapes=[pltpu.VMEM((4, D, 256), jnp.bfloat16), pltpu.SemaphoreType.DMA((4,))],
        compiler_params=params(16),
        name="project_query",
    )(tokens, pltpu.with_memory_space_constraint(w, pltpu.HBM))


def rest_kernel(tokens, w, q, self_bias, w2, gate_out, self_out, w2_out, buf, sems, sem):
    held = pltpu.make_async_copy(w2, w2_out, sem)
    held.start()
    copies = []
    for i in range(4):
        for j, base in enumerate((0, D, 3 * D)):
            n = i * 3 + j
            copies.append(
                pltpu.make_async_copy(w.at[:, pl.ds(base + i * 256, 256)], buf.at[n], sems.at[n])
            )
    for c in copies:
        c.start()
    normed = norm(tokens[...].astype(jnp.float32)).astype(jnp.bfloat16)

    def proj(n):
        copies[n].wait()
        return silu(jnp.dot(normed, buf[n], preferred_element_type=jnp.float32)).astype(jnp.bfloat16)

    for i in range(4):
        wide = slice(i * 256, (i + 1) * 256)
        gate_out[:, wide] = proj(i * 3)
        v = proj(i * 3 + 1).astype(jnp.float32)
        k = proj(i * 3 + 2).astype(jnp.float32)
        qk = q[:, wide].astype(jnp.float32) * k
        for j in range(2):
            cols = slice(j * HEAD, (j + 1) * HEAD)
            s = jnp.sum(qk[:, cols], axis=1, keepdims=True) * SCALE + self_bias[i * 2 + j]
            self_out[:, i * 256 + j * HEAD : i * 256 + (j + 1) * HEAD] = silu(s) * v[:, cols]
    held.wait()


def rest(tokens, w, q, self_bias, w2):
    return pl.pallas_call(
        rest_kernel,
        out_shape=(
            jax.ShapeDtypeStruct((ROWS, D), jnp.bfloat16),
            jax.ShapeDtypeStruct((ROWS, D), jnp.float32),
            pltpu.VMEM((D, D), jnp.bfloat16),
        ),
        in_specs=[VM, HB, VM, SM, HB],
        out_specs=(VM, VM, VM),
        scratch_shapes=[
            pltpu.VMEM((12, D, 256), jnp.bfloat16),
            pltpu.SemaphoreType.DMA((12,)),
            pltpu.SemaphoreType.DMA,
        ],
        compiler_params=params(20),
        name="project_rest",
    )(
        tokens,
        pltpu.with_memory_space_constraint(w, pltpu.HBM),
        q,
        self_bias,
        pltpu.with_memory_space_constraint(w2, pltpu.HBM),
    )


def stack_kernel(own, p1, m1, p2, m2, p3, m3, p4, m4, out):
    for s, piece in ((0, own), (7, p1), (1, m1), (6, p2), (2, m2), (5, p3), (3, m3)):
        out[s] = piece[...]
    out[4, :CUT] = p4[...]
    out[4, CUT:] = m4[...]


def stack(pieces):
    return pl.pallas_call(
        stack_kernel,
        out_shape=jax.ShapeDtypeStruct((NZ, QROWS, HEAD), jnp.bfloat16),
        in_specs=[VM] * 9,
        out_specs=VM,
        compiler_params=params(16),
        name="stack_queries",
    )(*pieces)


def table_kernel(q_own, q_other, tab, ints, sem):
    for i, q in enumerate((q_own, q_other)):
        for s in range(NZ):
            ints[i * NZ + s] = q[s, HALF:].astype(jnp.float32).astype(jnp.int32)[0:8]
    copy = pltpu.make_async_copy(ints.at[:, 0], tab, sem)
    copy.start()
    copy.wait()


def table(q_own, q_other):
    return pl.pallas_call(
        table_kernel,
        out_shape=jax.ShapeDtypeStruct((NG, 128), jnp.int32),
        in_specs=[VM, VM],
        out_specs=SM,
        scratch_shapes=[pltpu.VMEM((NG, 8, 128), jnp.int32), pltpu.SemaphoreType.DMA],
        compiler_params=params(16),
        name="read_tables",
    )(q_own, q_other)


def attend_kernel(first, count, base, tab, where, bias, q, kv, out, weights):
    h = where[2]
    o = where[0] * 2 + where[1]

    def weigh(i, carry):
        s = where[8 + first + i]
        row = base + s
        length = tab[row, 2 * NG * CAP] * 256 + tab[row, 2 * NG * CAP + 1]
        for c in range(CAP):
            slot = tab[row, o * CAP + c]

            @pl.when(slot >= 0)
            def _():
                p = tab[row, NG * CAP + o * CAP + c]
                b = bias[h, p] * 0.5
                keys = kv[:, 0, slot].reshape(BLOCK, HEAD)
                for j in range(4):
                    rows = pl.ds(j * 128, 128)
                    scores = lax.dot_general(
                        q[s, rows], keys, (((1,), (1,)), ((), ())), preferred_element_type=jnp.float32
                    )
                    t = scores * (0.5 * SCALE) + b
                    weights[slot, rows] = (t + t * jnp.tanh(t)).astype(jnp.bfloat16)
                limit = length - p * BLOCK

                @pl.when(limit < BLOCK)
                def _():
                    token = lax.broadcasted_iota(jnp.int32, (128, BLOCK), 1)
                    for j in range(4):
                        rows = pl.ds(j * 128, 128)
                        w = weights[slot, rows].astype(jnp.float32)
                        weights[slot, rows] = jnp.where(token < limit, w, 0.0).astype(jnp.bfloat16)

        return carry

    def blend(i, carry):
        row = base + where[8 + first + i]
        one, two = tab[row, o * CAP], tab[row, o * CAP + 1]

        def store(slots):
            values = [kv[:, 1, n].reshape(BLOCK, HEAD) for n in slots]
            for j in range(4):
                rows = pl.ds(j * 128, 128)
                total = jnp.zeros((128, HEAD), jnp.float32)
                for n, v in zip(slots, values):
                    total += jnp.dot(weights[n, rows], v, preferred_element_type=jnp.float32)
                out[i, rows] = total.astype(jnp.bfloat16)

        @pl.when((one >= 0) & (two >= 0))
        def _():
            store((one, two))

        @pl.when((one >= 0) & (two < 0))
        def _():
            store((one,))

        @pl.when((one < 0) & (two >= 0))
        def _():
            store((two,))

        @pl.when((one < 0) & (two < 0))
        def _():
            store(())

        return carry

    lax.fori_loop(0, count, weigh, 0)
    lax.fori_loop(0, count, blend, 0)


def attend(first, count, base, tab, where, bias, q, kv):
    return pl.pallas_call(
        functools.partial(attend_kernel, first, count, base),
        out_shape=jax.ShapeDtypeStruct((count, HALF, HEAD), jnp.bfloat16),
        in_specs=[SM, SM, SM, VM, VM],
        out_specs=VM,
        scratch_shapes=[pltpu.VMEM((BLK, HALF, BLOCK), jnp.bfloat16)],
        compiler_params=params(20),
        name=f"attend_{first}_{base}",
    )(tab, where, bias, q, kv)


def add(*refs):
    total = refs[0].astype(jnp.float32)
    for r in refs[1:]:
        total += r.astype(jnp.float32)
    return total


def far_kernel(a, b, up, down, up4, down4):
    for out, slots in ((up, (0, 1)), (down, (4, 3))):
        for i, n in enumerate(slots):
            out[i] = add(a[n], b[n]).astype(jnp.bfloat16)
    four = add(a[2], b[2]).astype(jnp.bfloat16)
    up4[...] = four[:256]
    down4[...] = four[256:]


def far(a, b):
    two = jax.ShapeDtypeStruct((2, HALF, HEAD), jnp.bfloat16)
    half = jax.ShapeDtypeStruct((256, HEAD), jnp.bfloat16)
    return pl.pallas_call(
        far_kernel,
        out_shape=(two, two, half, half),
        in_specs=[VM] * 2,
        out_specs=(VM,) * 4,
        compiler_params=params(16),
        name="add_far",
    )(a, b)


def near_kernel(a, b, up, down, up4, down4, here, next_up, next_down):
    here[...] = add(a[0], b[0], up[0], down[0])
    top, low = slice(0, 256), slice(256, 512)
    next_up[top] = add(a[1, top], b[1, top], up[1, top], up4[...]).astype(jnp.bfloat16)
    next_up[low] = add(a[1, low], b[1, low], up[1, low]).astype(jnp.bfloat16)
    next_down[top] = add(a[2, top], b[2, top], down[1, top]).astype(jnp.bfloat16)
    next_down[low] = add(a[2, low], b[2, low], down[1, low], down4[...]).astype(jnp.bfloat16)


def near(*args):
    part = jax.ShapeDtypeStruct((HALF, HEAD), jnp.bfloat16)
    return pl.pallas_call(
        near_kernel,
        out_shape=(jax.ShapeDtypeStruct((HALF, HEAD), jnp.float32), part, part),
        in_specs=[VM] * 6,
        out_specs=(VM,) * 3,
        compiler_params=params(16),
        name="add_near",
    )(*args)


def total_kernel(here, up, down, out):
    out[...] = add(here[...], up[...], down[...]).astype(jnp.bfloat16).reshape(NM, 32, HEAD)


def total(*parts):
    return pl.pallas_call(
        total_kernel,
        out_shape=jax.ShapeDtypeStruct((NM, 32, HEAD), jnp.bfloat16),
        in_specs=[VM] * 3,
        out_specs=VM,
        compiler_params=params(16),
        name="add_groups",
    )(*parts)


def tail_kernel(hist, self_term, gate, tokens, w, where, count, out):
    cols = []
    for h in range(HEADS):
        cols.append(jnp.concatenate([hist[h * 2], hist[h * 2 + 1]], axis=0))
    attended = jnp.concatenate(cols, axis=1).astype(jnp.float32) + self_term[...]
    gated = (norm(attended) * gate[...].astype(jnp.float32)).astype(jnp.bfloat16)
    res = jnp.dot(gated, w[...], preferred_element_type=jnp.float32) + tokens[...].astype(jnp.float32)
    row = where[3] * ROWS + lax.broadcasted_iota(jnp.int32, (ROWS, D), 0)
    out[...] = jnp.where(row < count[0], res, 0.0).astype(jnp.bfloat16)


def tail(hist, self_term, gate, tokens, w, where, count):
    return pl.pallas_call(
        tail_kernel,
        out_shape=jax.ShapeDtypeStruct((ROWS, D), jnp.bfloat16),
        in_specs=[VM, VM, VM, VM, VM, SM, SM],
        out_specs=VM,
        compiler_params=params(16),
        name="output",
    )(hist, self_term, gate, tokens, w, where, count)


def move(value, step):
    return lax.ppermute(value, "z", [(i, (i + step) % NZ) for i in range(NZ)])


def swap(value):
    return lax.ppermute(value, "core", [(0, 1), (1, 0)])


def local(
    tokens,
    in_weight,
    out_weight,
    history_pool,
    position_bias,
    self_bias,
    history_length,
    candidate_count,
    block_slots,
    block_position,
):
    z, core, m = lax.axis_index("z"), lax.axis_index("core"), lax.axis_index(M)
    where = jnp.concatenate(
        [jnp.stack([z, core, m // 2, m, 0, 0, 0, 0]), jnp.array([1, 3, 4, 5, 7, 0, 2, 6])]
    ).astype(jnp.int32)
    length = history_length[:, None]
    mine = jnp.concatenate(
        [
            block_slots.reshape(1, NG * CAP),
            block_position.reshape(1, NG * CAP),
            length // 256,
            length % 256,
            jnp.zeros((1, 62), jnp.int32),
        ],
        axis=1,
    ).astype(jnp.bfloat16)
    mine = jnp.broadcast_to(mine, (16, 128))
    q, q_send = query(tokens, in_weight)
    q_mine = lax.all_to_all(q_send, M, split_axis=0, concat_axis=0, tiled=True)
    packed = pack(history_pool, q)
    q_mine, packed = lax.optimization_barrier((q_mine, packed))
    kv = lax.all_to_all(packed, M, split_axis=0, concat_axis=0, tiled=True)
    gate, self_term, w2 = rest(tokens, in_weight, q, self_bias, out_weight)
    q_mine = jnp.concatenate([q_mine.reshape(HALF, HEAD), mine], axis=0)
    q_mine, gate, self_term, w2 = lax.optimization_barrier((q_mine, gate, self_term, w2))
    p1, m1, p2, m2 = (move(q_mine, s) for s in (1, -1, 2, -2))
    p3, m3, p4, m4 = move(p2, 1), move(m2, -1), move(p2[:CUT], 2), move(m2[CUT:], -2)
    q_own = stack([q_mine, p1, m1, p2, m2, p3, m3, p4, m4])
    q_other = swap(q_own)
    tab = table(q_own, q_other)
    sums = []
    for first, count in ((0, 5), (5, 3)):
        other = swap(attend(first, count, NZ, tab, where, position_bias, q_other, kv))
        own = attend(first, count, 0, tab, where, position_bias, q_own, kv)
        sums.append((own, other))
    up, down, up4, down4 = far(*sums[0])
    up, down, up4, down4 = move(up, 1), move(down, -1), move(up4, 2), move(down4, -2)
    here, up, down = near(*sums[1], up, down, up4, down4)
    hist = lax.all_to_all(total(here, move(up, 2), move(down, -2)), M, split_axis=0, concat_axis=0, tiled=True)
    return tail(hist, self_term, gate, tokens, w2, where, candidate_count)


def solution(mesh):
    fine = Mesh(mesh.devices.reshape(NZ, 2, 4, 4), ("z", "core", "x", "y"))
    placed = (
        P(("z", "core", "x", "y"), None),
        P(),
        P(),
        P(("z", "core"), ("x", "y"), None),
        P(),
        P(),
        P(("z", "core")),
        P(("z", "core")),
        P(("z", "core"), None, None),
        P(("z", "core"), None, None),
    )
    return jax.shard_map(
        local, mesh=fine, in_specs=placed, out_specs=P(("z", "core", "x", "y"), None), check_vma=False
    )
```

time: 270 us -> 128 us (0.47)
  Pallas kernels: 135 us -> 30.7 us
  blocking collectives: 33.6 us -> 0 us
  starting transfers between devices: 34 us -> 53.1 us
  between operations: 14.9 us -> 1.62 us
  waiting for transfers between devices: 42.3 us -> 36.3 us
  local copies, waits for them, and re-layouts: 9.63 us -> 4.87 us
    pallas_call x1, Pallas kernels: 113 us -> 0.51 us  [pack(): pl.pallas_call(pack_kernel, out_shape=jax.ShapeDtypeStruct((NM, 2, BLK, S...]
    all_gather x1 -> x0, blocking collectives: 19.9 us -> none  [local(): tab = lax.all_gather(mine, G, axis=0, tiled=True)]
    all_to_all x1, waiting for transfers between devices: 23.5 us -> 6.35 us  [local(): kv = lax.all_to_all(packed, M, split_axis=0, concat_axis=0, tiled=True)]
    all_to_all x1 -> x0, blocking collectives: 13.8 us -> none  [local(): q_mine = lax.all_to_all(q_send, M, split_axis=0, concat_axis=0, tiled=True)]
    ppermute x8 -> x17, starting transfers between devices: 20.2 us -> 31.9 us  [the longest x14 31.5 us: move(): return lax.ppermute(value, 'z', [(i, (i + step) % NZ) for i in range(NZ)])]
    all_to_all x1 -> x2, waiting for transfers between devices: 0.01 us -> 9.79 us  [the longest x1 5.74 us: local(): lax.all_to_all(total(here, move(up, 2), move(down, -2)), M, split_axis=0,...]
    pallas_call x4 -> x10, Pallas kernels: 19.8 us -> 27.7 us  [the longest x4 16.9 us: attend(): pl.pallas_call(functools.partial(attend_kernel, first, count, base), out_...]
    all_to_all x1 -> x2, starting transfers between devices: 7.84 us -> 15.3 us  [the longest x1 7.85 us: local(): lax.all_to_all(total(here, move(up, 2), move(down, -2)), M, split_axis=0,...]
  transfers between devices with their start and end apart: 11 -> 20, of which waited for: 7 -> 11; matrix products, arithmetic and copies ran while one was open for 0% -> 0% of each run, Pallas kernels for 43% -> 16%
where the time goes in v2:
time: 128 us; the launch traced here: 127 us
  starting transfers between devices  53.1 us (41%)
  waiting for transfers between devices  36.3 us (28%)
  Pallas kernels  30.7 us (24%)
  local copies, waits for them, and re-layouts  4.87 us (4%)
  between operations  1.62 us (1%)
    ppermute x14, starting transfers between devices, move(): return lax.ppermute(value, 'z', [(i, (i + step) % NZ) for i in range(NZ)])  31.5 us
    ppermute x14, waiting for transfers between devices, move(): return lax.ppermute(value, 'z', [(i, (i + step) % NZ) for i in range(NZ)])  17.6 us
    pallas_call x4, Pallas kernels, attend(): pl.pallas_call(functools.partial(attend_kernel, first, count, base), out_...  16.9 us
    all_to_all x1, starting transfers between devices, local(): lax.all_to_all(total(here, move(up, 2), move(down, -2)), M, split_axis=0,...  7.85 us
    all_to_all x1, starting transfers between devices, local(): q_mine = lax.all_to_all(q_send, M, split_axis=0, concat_axis=0, tiled=True)  7.49 us
    all_to_all x1, waiting for transfers between devices, local(): kv = lax.all_to_all(packed, M, split_axis=0, concat_axis=0, tiled=True)  6.35 us
    pallas_call x1, Pallas kernels, rest(): pl.pallas_call(rest_kernel, out_shape=(jax.ShapeDtypeStruct((ROWS, D), jn...  6.12 us
    all_to_all x1, starting transfers between devices, local(): kv = lax.all_to_all(packed, M, split_axis=0, concat_axis=0, tiled=True)  5.8 us
  transfers between devices with their start and end apart: 20, of which 11 were waited for; matrix products, arithmetic and copies ran while one was open for 0% of the time, Pallas kernels for 16%

profile of v2, /device:TPU:2, one launch (start us, length us, event | category | flops | bytes accessed | tf_op | source)
XLA Modules:
  0.0 126.6 jit_solution(6048539631018307052)
XLA Ops:
  0.0 1.0 copy-done.4
  1.0 2.9 %project_query.1 = (bf16[64,1024]{1,0:T(8,128)(2,1)S(1)}, bf16[16,32,128]{2,1,0:T(8,128)(2,1)}) custom-call(bf16[64,1024]{1,0:T(8,128)(2,1)S(1)} %copy-done.4, bf16[1024,4096]{1,0:T(8,128)(2,1)} %w.3), custom_call_target="tpu_custom_call" | custom-call | tf_op jit(solution)/shard_map/project_query/pallas_call | solution.py:84
  3.9 7.5 %all-to-all-start = ((bf16[16,32,128]{2,1,0:T(8,128)(2,1)}), bf16[16,32,128]{2,1,0:T(8,128)(2,1)S(1)}, u32[]{:S(2)}, u32[]{:S(2)}) async-start(bf16[16,32,128]{2,1,0:T(8,128)(2,1)} %get-tuple-element.23), calls=%async_computation | async-start | bytes 262144 | tf_op jit(solution)/shard_map/all_to_all | solution.py:400
  11.4 0.5 pack_history.1
  12.0 1.8 %copy-done = bf16[16,2,14,32,128]{4,3,2,1,0:T(8,128)(2,1)} copy-done((bf16[16,2,14,32,128]{4,3,2,1,0:T(8,128)(2,1)}, bf16[16,2,14,32,128]{4,3,2,1,0:T(8,128)(2,1)S(1)}, u32[]{:S(2)}) %copy-start) | copy-done | bytes 3670040
  13.8 4.0 %all-to-all-done = bf16[16,32,128]{2,1,0:T(8,128)(2,1)S(1)} async-done(((bf16[16,32,128]{2,1,0:T(8,128)(2,1)}), bf16[16,32,128]{2,1,0:T(8,128)(2,1)S(1)}, u32[]{:S(2)}, u32[]{:S(2)}) %all-to-all-start) | async-done | bytes 131104 | tf_op jit(solution)/shard_map/all_to_all | solution.py:400
  17.8 5.8 %all-to-all-start.1 = ((bf16[16,2,14,32,128]{4,3,2,1,0:T(8,128)(2,1)}), bf16[16,2,14,32,128]{4,3,2,1,0:T(8,128)(2,1)}, u32[]{:S(2)}, u32[]{:S(2)}) async-start(bf16[16,2,14,32,128]{4,3,2,1,0:T(8,128)(2,1)} %copy-done), calls=%async_computation.1 | async-start | bytes 7340032 | tf_op jit(solution)/shard_map/all_to_all | solution.py:403
  24.4 0.1 copy.15
  24.4 0.1 concatenate.24
  24.5 0.1 copy.14
  24.6 0.1 concatenate.23
  24.8 6.1 %project_rest.1 = (bf16[64,1024]{1,0:T(8,128)(2,1)S(1)}, f32[64,1024]{1,0:T(8,128)S(1)}, bf16[1024,1024]{1,0:T(8,128)(2,1)S(1)}) custom-call(bf16[64,1024]{1,0:T(8,128)(2,1)S(1)} %copy-done.5, bf16[1024,4096]{1,0:T(8,128)(2,1)} %w.3, bf16[64,1024]{1,0:T(8,128)(2,1)S(1)} %get-tuple-element.24.after.q, f32[8]{0:T(128)S(1)} %copy-done.7, bf16[1024,1024]{1,0:T(8,128)(2,1)} %w2.1), custom_call_target="tpu_custom_call" | custom-call | tf_op jit(solution)/shard_map/project_rest/pallas_call | solution.py:130
  30.9 1.4 %copy-done.1 = bf16[1024,1024]{1,0:T(8,128)(2,1)} copy-done((bf16[1024,1024]{1,0:T(8,128)(2,1)}, bf16[1024,1024]{1,0:T(8,128)(2,1)S(1)}, u32[]{:S(2)}) %copy-start.1) | copy-done | bytes 2097176
  32.3 0.1 concatenate.27
  32.4 6.4 %collective-permute-start.3 = (bf16[528,128]{1,0:T(8,128)(2,1)S(1)}, bf16[528,128]{1,0:T(8,128)(2,1)S(1)}, u32[]{:S(2)}, u32[]{:S(2)}) collective-permute-start(bf16[528,128]{1,0:T(8,128)(2,1)S(1)} %pad_maximum_fusion.own), channel_id=1, source_target_pairs={{0,192},{32,224},{64,0},{96,32},{128,64},{160,96},{192,128},{224,1... | collective-permute-start | bytes 405512 | tf_op jit(solution)/shard_map/ppermute | solution.py:364
  38.8 3.7 %collective-permute-start.1 = (bf16[528,128]{1,0:T(8,128)(2,1)S(1)}, bf16[528,128]{1,0:T(8,128)(2,1)S(1)}, u32[]{:S(2)}, u32[]{:S(2)}) collective-permute-start(bf16[528,128]{1,0:T(8,128)(2,1)S(1)} %pad_maximum_fusion.own), channel_id=1, source_target_pairs={{0,224},{32,0},{64,32},{96,64},{128,96},{160,128},{192,160},{224,1... | collective-permute-start | bytes 405512 | tf_op jit(solution)/shard_map/ppermute | solution.py:364
  42.5 1.6 %collective-permute-done.3.m2 = bf16[528,128]{1,0:T(8,128)(2,1)S(1)} collective-permute-done((bf16[528,128]{1,0:T(8,128)(2,1)S(1)}, bf16[528,128]{1,0:T(8,128)(2,1)S(1)}, u32[]{:S(2)}, u32[]{:S(2)}) %collective-permute-start.3) | collective-permute-done | bytes 135200 | tf_op jit(solution)/shard_map/ppermute | solution.py:364
  44.1 2.9 %collective-permute-start.5 = (bf16[528,128]{1,0:T(8,128)(2,1)S(1)}, bf16[528,128]{1,0:T(8,128)(2,1)S(1)}, u32[]{:S(2)}, u32[]{:S(2)}) collective-permute-start(bf16[528,128]{1,0:T(8,128)(2,1)S(1)} %collective-permute-done.3.m2), channel_id=1, source_target_pairs={{0,224},{32,0},{64,32},{96,64},{128,96},{160,128},{192,160},{224,1... | collective-permute-start | bytes 405512 | tf_op jit(solution)/shard_map/ppermute | solution.py:364
  47.0 1.6 %collective-permute-done.2.p2 = bf16[528,128]{1,0:T(8,128)(2,1)S(1)} collective-permute-done((bf16[528,128]{1,0:T(8,128)(2,1)S(1)}, bf16[528,128]{1,0:T(8,128)(2,1)S(1)}, u32[]{:S(2)}, u32[]{:S(2)}) %collective-permute-start.2) | collective-permute-done | bytes 135200 | tf_op jit(solution)/shard_map/ppermute | solution.py:364
  48.6 1.0 collective-permute-start.4
  49.5 1.3 %collective-permute-start.7 = (bf16[272,128]{1,0:T(8,128)(2,1)S(1)}, bf16[272,128]{1,0:T(8,128)(2,1)S(1)}, u32[]{:S(2)}, u32[]{:S(2)}) collective-permute-start(bf16[272,128]{1,0:T(8,128)(2,1)S(1)} %slice.9), channel_id=1, source_target_pairs={{0,192},{32,224},{64,0},{96,32},{128,64},{160,96},{192,128},{224,1... | collective-permute-start | bytes 208904 | tf_op jit(solution)/shard_map/ppermute | solution.py:364
  50.9 1.7 %collective-permute-start.6 = (bf16[256,128]{1,0:T(8,128)(2,1)S(1)}, bf16[256,128]{1,0:T(8,128)(2,1)S(1)}, u32[]{:S(2)}, u32[]{:S(2)}) collective-permute-start(bf16[256,128]{1,0:T(8,128)(2,1)S(1)} %slice.8), channel_id=1, source_target_pairs={{0,64},{32,96},{64,128},{96,160},{128,192},{160,224},{192,0},{224,... | collective-permute-start | bytes 196616 | tf_op jit(solution)/shard_map/ppermute | solution.py:364
  52.6 5.0 %collective-permute-done.6.p4 = bf16[256,128]{1,0:T(8,128)(2,1)S(1)} collective-permute-done((bf16[256,128]{1,0:T(8,128)(2,1)S(1)}, bf16[256,128]{1,0:T(8,128)(2,1)S(1)}, u32[]{:S(2)}, u32[]{:S(2)}) %collective-permute-start.6) | collective-permute-done | bytes 65568 | tf_op jit(solution)/shard_map/ppermute | solution.py:364
  57.6 0.1 collective-permute-start.8
  57.9 2.6 %collective-permute-done.8.q_other.q = bf16[8,528,128]{2,1,0:T(8,128)(2,1)S(1)} collective-permute-done((bf16[8,528,128]{2,1,0:T(8,128)(2,1)S(1)}, bf16[8,528,128]{2,1,0:T(8,128)(2,1)S(1)}, u32[]{:S(2)}, u32[]{:S(2)}) %collective-permute-start.8) | collective-permute-done | bytes 1081376 | tf_op jit(solution)/shard_map/ppermute | solution.py:368
  60.4 1.4 %read_tables.1.tab = s32[16,128]{1,0:T(8,128)S(1)} custom-call(bf16[8,528,128]{2,1,0:T(8,128)(2,1)S(1)} %stack_queries.1.q_own.q, bf16[8,528,128]{2,1,0:T(8,128)(2,1)S(1)} %collective-permute-done.8.q_other.q), custom_call_target="tpu_custom_call" | custom-call | tf_op jit(solution)/shard_map/read_tables/pallas_call | solution.py:183
  61.8 6.4 %all-to-all-done.1.kv = bf16[16,2,14,32,128]{4,3,2,1,0:T(8,128)(2,1)} async-done(((bf16[16,2,14,32,128]{4,3,2,1,0:T(8,128)(2,1)}), bf16[16,2,14,32,128]{4,3,2,1,0:T(8,128)(2,1)}, u32[]{:S(2)}, u32[]{:S(2)}) %all-to-all-start.1) | async-done | bytes 3670048 | tf_op jit(solution)/shard_map/all_to_all | solution.py:403
  68.2 4.7 %attend_0_8.1 = bf16[5,512,128]{2,1,0:T(8,128)(2,1)S(1)} custom-call(s32[16,128]{1,0:T(8,128)S(1)} %read_tables.1.tab, s32[16]{0:T(128)S(1)} %concatenate.29.where, f32[8,14]{1,0:T(8,128)S(1)} %copy-done.6, bf16[8,528,128]{2,1,0:T(8,128)(2,1)S(1)} %collective-permute-done.8.q_other.q, bf16[16,2,14,32,128]{4,3,2,1,0:T(8,128)(2,1)} %all-to-all-done.1.kv), custom_call_target="tpu_custom_call" | custom-call | tf_op jit(solution)/shard_map/attend_0_8/pallas_call | solution.py:265
  72.9 0.3 collective-permute-start.10
  73.2 4.5 %attend_5_8.1 = bf16[3,512,128]{2,1,0:T(8,128)(2,1)S(1)} custom-call(s32[16,128]{1,0:T(8,128)S(1)} %read_tables.1.tab, s32[16]{0:T(128)S(1)} %concatenate.29.where, f32[8,14]{1,0:T(8,128)S(1)} %copy-done.6, bf16[8,528,128]{2,1,0:T(8,128)(2,1)S(1)} %collective-permute-done.8.q_other.q, bf16[16,2,14,32,128]{4,3,2,1,0:T(8,128)(2,1)} %all-to-all-done.1.kv), custom_call_target="tpu_custom_call" | custom-call | tf_op jit(solution)/shard_map/attend_5_8/pallas_call | solution.py:265
  77.7 0.1 collective-permute-start.9
  77.8 3.6 %attend_0_0.1.a = bf16[5,512,128]{2,1,0:T(8,128)(2,1)S(1)} custom-call(s32[16,128]{1,0:T(8,128)S(1)} %read_tables.1.tab, s32[16]{0:T(128)S(1)} %concatenate.29.where, f32[8,14]{1,0:T(8,128)S(1)} %copy-done.6, bf16[8,528,128]{2,1,0:T(8,128)(2,1)S(1)} %stack_queries.1.q_own.q, bf16[16,2,14,32,128]{4,3,2,1,0:T(8,128)(2,1)} %all-to-all-done.1.kv), custom_call_target="tpu_custom_call" | custom-call | tf_op jit(solution)/shard_map/attend_0_0/pallas_call | solution.py:265
  81.4 0.2 add_far.1
  81.6 2.6 %collective-permute-start.11 = (bf16[2,512,128]{2,1,0:T(8,128)(2,1)S(1)}, bf16[2,512,128]{2,1,0:T(8,128)(2,1)S(1)}, u32[]{:S(2)}, u32[]{:S(2)}) collective-permute-start(bf16[2,512,128]{2,1,0:T(8,128)(2,1)S(1)} %get-tuple-element.31), channel_id=1, source_target_pairs={{0,32},{32,64},{64,96},{96,128},{128,160},{160,192},{192,224},{224... | collective-permute-start | bytes 786440 | tf_op jit(solution)/shard_map/ppermute | solution.py:364
  84.2 3.5 %collective-permute-start.12 = (bf16[2,512,128]{2,1,0:T(8,128)(2,1)S(1)}, bf16[2,512,128]{2,1,0:T(8,128)(2,1)S(1)}, u32[]{:S(2)}, u32[]{:S(2)}) collective-permute-start(bf16[2,512,128]{2,1,0:T(8,128)(2,1)S(1)} %get-tuple-element.32), channel_id=1, source_target_pairs={{0,224},{32,0},{64,32},{96,64},{128,96},{160,128},{192,160},{224,1... | collective-permute-start | bytes 786440 | tf_op jit(solution)/shard_map/ppermute | solution.py:364
  87.7 4.1 %collective-permute-start.14 = (bf16[256,128]{1,0:T(8,128)(2,1)S(1)}, bf16[256,128]{1,0:T(8,128)(2,1)S(1)}, u32[]{:S(2)}, u32[]{:S(2)}) collective-permute-start(bf16[256,128]{1,0:T(8,128)(2,1)S(1)} %get-tuple-element.34), channel_id=1, source_target_pairs={{0,192},{32,224},{64,0},{96,32},{128,64},{160,96},{192,128},{224,1... | collective-permute-start | bytes 196616 | tf_op jit(solution)/shard_map/ppermute | solution.py:364
  91.9 4.0 %attend_5_0.1.a = bf16[3,512,128]{2,1,0:T(8,128)(2,1)S(1)} custom-call(s32[16,128]{1,0:T(8,128)S(1)} %read_tables.1.tab, s32[16]{0:T(128)S(1)} %concatenate.29.where, f32[8,14]{1,0:T(8,128)S(1)} %copy-done.6, bf16[8,528,128]{2,1,0:T(8,128)(2,1)S(1)} %stack_queries.1.q_own.q, bf16[16,2,14,32,128]{4,3,2,1,0:T(8,128)(2,1)} %all-to-all-done.1.kv), custom_call_target="tpu_custom_call" | custom-call | tf_op jit(solution)/shard_map/attend_5_0/pallas_call | solution.py:265
  95.9 1.3 %collective-permute-done.13.up4 = bf16[256,128]{1,0:T(8,128)(2,1)S(1)} collective-permute-done((bf16[256,128]{1,0:T(8,128)(2,1)S(1)}, bf16[256,128]{1,0:T(8,128)(2,1)S(1)}, u32[]{:S(2)}, u32[]{:S(2)}) %collective-permute-start.13) | collective-permute-done | bytes 65568 | tf_op jit(solution)/shard_map/ppermute | solution.py:364
  97.2 0.2 collective-permute-done.14.down4
  97.4 0.2 add_near.1
  97.6 3.5 %collective-permute-start.15 = (bf16[512,128]{1,0:T(8,128)(2,1)S(1)}, bf16[512,128]{1,0:T(8,128)(2,1)S(1)}, u32[]{:S(2)}, u32[]{:S(2)}) collective-permute-start(bf16[512,128]{1,0:T(8,128)(2,1)S(1)} %get-tuple-element.36), channel_id=1, source_target_pairs={{0,64},{32,96},{64,128},{96,160},{128,192},{160,224},{192,0},{224,... | collective-permute-start | bytes 393224 | tf_op jit(solution)/shard_map/ppermute | solution.py:364
  101.1 0.7 collective-permute-start.16
  101.8 4.1 %collective-permute-done.15.up = bf16[512,128]{1,0:T(8,128)(2,1)S(1)} collective-permute-done((bf16[512,128]{1,0:T(8,128)(2,1)S(1)}, bf16[512,128]{1,0:T(8,128)(2,1)S(1)}, u32[]{:S(2)}, u32[]{:S(2)}) %collective-permute-start.15) | collective-permute-done | bytes 131104 | tf_op jit(solution)/shard_map/ppermute | solution.py:364
  105.9 3.9 %collective-permute-done.16.down = bf16[512,128]{1,0:T(8,128)(2,1)S(1)} collective-permute-done((bf16[512,128]{1,0:T(8,128)(2,1)S(1)}, bf16[512,128]{1,0:T(8,128)(2,1)S(1)}, u32[]{:S(2)}, u32[]{:S(2)}) %collective-permute-start.16) | collective-permute-done | bytes 131104 | tf_op jit(solution)/shard_map/ppermute | solution.py:364
  109.8 0.7 add_groups.1
  110.5 7.9 %all-to-all-start.2 = ((bf16[16,32,128]{2,1,0:T(8,128)(2,1)}), bf16[16,32,128]{2,1,0:T(8,128)(2,1)S(1)}, u32[]{:S(2)}, u32[]{:S(2)}) async-start(bf16[16,32,128]{2,1,0:T(8,128)(2,1)} %add_groups.1), calls=%async_computation.2 | async-start | bytes 262144 | tf_op jit(solution)/shard_map/all_to_all | solution.py:420
  119.0 5.7 %all-to-all-done.2.hist = bf16[16,32,128]{2,1,0:T(8,128)(2,1)S(1)} async-done(((bf16[16,32,128]{2,1,0:T(8,128)(2,1)}), bf16[16,32,128]{2,1,0:T(8,128)(2,1)S(1)}, u32[]{:S(2)}, u32[]{:S(2)}) %all-to-all-start.2) | async-done | bytes 131104 | tf_op jit(solution)/shard_map/all_to_all | solution.py:420
  124.8 1.9 %output.1 = bf16[64,1024]{1,0:T(8,128)(2,1)} custom-call(bf16[16,32,128]{2,1,0:T(8,128)(2,1)S(1)} %all-to-all-done.2.hist, f32[64,1024]{1,0:T(8,128)S(1)} %get-tuple-element.38.self_term, bf16[64,1024]{1,0:T(8,128)(2,1)S(1)} %get-tuple-element.39.gate, bf16[64,1024]{1,0:T(8,128)(2,1)S(1)} %copy-done.5, bf16[1024,1024]{1,0:T(8,128)(2,1)S(1)} %copy-done.2, ...), custom_call_target="tpu_custom_call" | custom-call | tf_op jit(solution)/shard_map/output/pallas_call | solution.py:353
  (41 shorter events, 0.3 us)
Async XLA Ops:
  0.0 11.4 %copy-start.3 = (bf16[14,32,2048]{2,1,0:T(8,128)(2,1)S(1)}, bf16[14,32,2048]{2,1,0:T(8,128)(2,1)}, u32[]{:S(2)}) copy-start(bf16[14,32,2048]{2,1,0:T(8,128)(2,1)} %pool.1) | copy-start | bytes 5505028
  0.0 1.0 copy-start.4
  3.9 13.9 %all-to-all-start = ((bf16[16,32,128]{2,1,0:T(8,128)(2,1)}), bf16[16,32,128]{2,1,0:T(8,128)(2,1)S(1)}, u32[]{:S(2)}, u32[]{:S(2)}) async-start(bf16[16,32,128]{2,1,0:T(8,128)(2,1)} %get-tuple-element.23), calls=%async_computation | async-start | bytes 262144 | tf_op jit(solution)/shard_map/all_to_all | solution.py:400
  11.9 1.8 %copy-start = (bf16[16,2,14,32,128]{4,3,2,1,0:T(8,128)(2,1)}, bf16[16,2,14,32,128]{4,3,2,1,0:T(8,128)(2,1)S(1)}, u32[]{:S(2)}) copy-start(bf16[16,2,14,32,128]{4,3,2,1,0:T(8,128)(2,1)S(1)} %pack_history.1) | copy-start | bytes 11010052
  13.8 10.6 %copy-start.9 = (s32[1,16,2]{1,2,0:T(2,128)S(1)}, s32[1,16,2]{1,2,0:T(2,128)}, u32[]{:S(2)}) copy-start(s32[1,16,2]{1,2,0:T(2,128)} %param.19) | copy-start | bytes 388
  13.8 10.6 %copy-start.10 = (s32[1,16,2]{1,2,0:T(2,128)S(1)}, s32[1,16,2]{1,2,0:T(2,128)}, u32[]{:S(2)}) copy-start(s32[1,16,2]{1,2,0:T(2,128)} %param.20) | copy-start | bytes 388
  13.8 11.0 %copy-start.5 = (bf16[64,1024]{1,0:T(8,128)(2,1)S(1)}, bf16[64,1024]{1,0:T(8,128)(2,1)}, u32[]{:S(2)}) copy-start(bf16[64,1024]{1,0:T(8,128)(2,1)} %tokens.5) | copy-start | bytes 393220
  13.8 11.0 %copy-start.7 = (f32[8]{0:T(128)S(1)}, f32[8]{0:T(128)}, u32[]{:S(2)}) copy-start(f32[8]{0:T(128)} %self_bias.1) | copy-start | bytes 100
  17.8 50.4 %all-to-all-start.1 = ((bf16[16,2,14,32,128]{4,3,2,1,0:T(8,128)(2,1)}), bf16[16,2,14,32,128]{4,3,2,1,0:T(8,128)(2,1)}, u32[]{:S(2)}, u32[]{:S(2)}) async-start(bf16[16,2,14,32,128]{4,3,2,1,0:T(8,128)(2,1)} %copy-done), calls=%async_computation.1 | async-start | bytes 7340032 | tf_op jit(solution)/shard_map/all_to_all | solution.py:403
  30.9 1.4 %copy-start.1 = (bf16[1024,1024]{1,0:T(8,128)(2,1)}, bf16[1024,1024]{1,0:T(8,128)(2,1)S(1)}, u32[]{:S(2)}) copy-start(bf16[1024,1024]{1,0:T(8,128)(2,1)S(1)} %get-tuple-element.40.w) | copy-start | bytes 6291460
  32.3 25.5 %copy-start.8 = (s32[8]{0:T(128)S(1)}, s32[8]{0:T(128)}, u32[]{:S(2)}) copy-start(s32[8]{0:T(128)} %constant.75.clone) | copy-start | bytes 100
  32.4 11.7 %collective-permute-start.3 = (bf16[528,128]{1,0:T(8,128)(2,1)S(1)}, bf16[528,128]{1,0:T(8,128)(2,1)S(1)}, u32[]{:S(2)}, u32[]{:S(2)}) collective-permute-start(bf16[528,128]{1,0:T(8,128)(2,1)S(1)} %pad_maximum_fusion.own), channel_id=1, source_target_pairs={{0,192},{32,224},{64,0},{96,32},{128,64},{160,96},{192,128},{224,1... | collective-permute-start | bytes 405512 | tf_op jit(solution)/shard_map/ppermute | solution.py:364
  38.8 9.8 %collective-permute-start.2 = (bf16[528,128]{1,0:T(8,128)(2,1)S(1)}, bf16[528,128]{1,0:T(8,128)(2,1)S(1)}, u32[]{:S(2)}, u32[]{:S(2)}) collective-permute-start(bf16[528,128]{1,0:T(8,128)(2,1)S(1)} %pad_maximum_fusion.own), channel_id=1, source_target_pairs={{0,64},{32,96},{64,128},{96,160},{128,192},{160,224},{192,0},{224,... | collective-permute-start | bytes 405512 | tf_op jit(solution)/shard_map/ppermute | solution.py:364
  38.8 12.1 %collective-permute-start.1 = (bf16[528,128]{1,0:T(8,128)(2,1)S(1)}, bf16[528,128]{1,0:T(8,128)(2,1)S(1)}, u32[]{:S(2)}, u32[]{:S(2)}) collective-permute-start(bf16[528,128]{1,0:T(8,128)(2,1)S(1)} %pad_maximum_fusion.own), channel_id=1, source_target_pairs={{0,224},{32,0},{64,32},{96,64},{128,96},{160,128},{192,160},{224,1... | collective-permute-start | bytes 405512 | tf_op jit(solution)/shard_map/ppermute | solution.py:364
  42.5 10.1 %collective-permute-start = (bf16[528,128]{1,0:T(8,128)(2,1)S(1)}, bf16[528,128]{1,0:T(8,128)(2,1)S(1)}, u32[]{:S(2)}, u32[]{:S(2)}) collective-permute-start(bf16[528,128]{1,0:T(8,128)(2,1)S(1)} %pad_maximum_fusion.own), channel_id=1, source_target_pairs={{0,32},{32,64},{64,96},{96,128},{128,160},{160,192},{192,224},{224... | collective-permute-start | bytes 405512 | tf_op jit(solution)/shard_map/ppermute | solution.py:364
  44.1 13.5 %collective-permute-start.5 = (bf16[528,128]{1,0:T(8,128)(2,1)S(1)}, bf16[528,128]{1,0:T(8,128)(2,1)S(1)}, u32[]{:S(2)}, u32[]{:S(2)}) collective-permute-start(bf16[528,128]{1,0:T(8,128)(2,1)S(1)} %collective-permute-done.3.m2), channel_id=1, source_target_pairs={{0,224},{32,0},{64,32},{96,64},{128,96},{160,128},{192,160},{224,1... | collective-permute-start | bytes 405512 | tf_op jit(solution)/shard_map/ppermute | solution.py:364
  48.6 9.0 %collective-permute-start.4 = (bf16[528,128]{1,0:T(8,128)(2,1)S(1)}, bf16[528,128]{1,0:T(8,128)(2,1)S(1)}, u32[]{:S(2)}, u32[]{:S(2)}) collective-permute-start(bf16[528,128]{1,0:T(8,128)(2,1)S(1)} %collective-permute-done.2.p2), channel_id=1, source_target_pairs={{0,32},{32,64},{64,96},{96,128},{128,160},{160,192},{192,224},{224... | collective-permute-start | bytes 405512 | tf_op jit(solution)/shard_map/ppermute | solution.py:364
  49.5 8.0 %collective-permute-start.7 = (bf16[272,128]{1,0:T(8,128)(2,1)S(1)}, bf16[272,128]{1,0:T(8,128)(2,1)S(1)}, u32[]{:S(2)}, u32[]{:S(2)}) collective-permute-start(bf16[272,128]{1,0:T(8,128)(2,1)S(1)} %slice.9), channel_id=1, source_target_pairs={{0,192},{32,224},{64,0},{96,32},{128,64},{160,96},{192,128},{224,1... | collective-permute-start | bytes 208904 | tf_op jit(solution)/shard_map/ppermute | solution.py:364
  50.9 17.3 %copy-start.6 = (f32[8,14]{1,0:T(8,128)S(1)}, f32[8,14]{1,0:T(8,128)}, u32[]{:S(2)}) copy-start(f32[8,14]{1,0:T(8,128)} %bias.7) | copy-start | bytes 1348
  50.9 6.7 %collective-permute-start.6 = (bf16[256,128]{1,0:T(8,128)(2,1)S(1)}, bf16[256,128]{1,0:T(8,128)(2,1)S(1)}, u32[]{:S(2)}, u32[]{:S(2)}) collective-permute-start(bf16[256,128]{1,0:T(8,128)(2,1)S(1)} %slice.8), channel_id=1, source_target_pairs={{0,64},{32,96},{64,128},{96,160},{128,192},{160,224},{192,0},{224,... | collective-permute-start | bytes 196616 | tf_op jit(solution)/shard_map/ppermute | solution.py:364
  57.6 2.8 %collective-permute-start.8 = (bf16[8,528,128]{2,1,0:T(8,128)(2,1)S(1)}, bf16[8,528,128]{2,1,0:T(8,128)(2,1)S(1)}, u32[]{:S(2)}, u32[]{:S(2)}) collective-permute-start(bf16[8,528,128]{2,1,0:T(8,128)(2,1)S(1)} %stack_queries.1.q_own.q), channel_id=1, source_target_pairs={{0,16},{16,0},{1,17},{17,1},{2,18},{18,2},{3,19},{19,3},{4,20},{20... | collective-permute-start | bytes 3244040 | tf_op jit(solution)/shard_map/ppermute | solution.py:368
  72.9 8.5 %collective-permute-start.10 = (bf16[5,512,128]{2,1,0:T(8,128)(2,1)S(1)}, bf16[5,512,128]{2,1,0:T(8,128)(2,1)S(1)}, u32[]{:S(2)}, u32[]{:S(2)}) collective-permute-start(bf16[5,512,128]{2,1,0:T(8,128)(2,1)S(1)} %attend_0_8.1), channel_id=1, source_target_pairs={{0,16},{16,0},{1,17},{17,1},{2,18},{18,2},{3,19},{19,3},{4,20},{20... | collective-permute-start | bytes 1966088 | tf_op jit(solution)/shard_map/ppermute | solution.py:368
  77.7 18.2 %collective-permute-start.9 = (bf16[3,512,128]{2,1,0:T(8,128)(2,1)S(1)}, bf16[3,512,128]{2,1,0:T(8,128)(2,1)S(1)}, u32[]{:S(2)}, u32[]{:S(2)}) collective-permute-start(bf16[3,512,128]{2,1,0:T(8,128)(2,1)S(1)} %attend_5_8.1), channel_id=1, source_target_pairs={{0,16},{16,0},{1,17},{17,1},{2,18},{18,2},{3,19},{19,3},{4,20},{20... | collective-permute-start | bytes 1179656 | tf_op jit(solution)/shard_map/ppermute | solution.py:368
  81.6 15.8 %collective-permute-start.11 = (bf16[2,512,128]{2,1,0:T(8,128)(2,1)S(1)}, bf16[2,512,128]{2,1,0:T(8,128)(2,1)S(1)}, u32[]{:S(2)}, u32[]{:S(2)}) collective-permute-start(bf16[2,512,128]{2,1,0:T(8,128)(2,1)S(1)} %get-tuple-element.31), channel_id=1, source_target_pairs={{0,32},{32,64},{64,96},{96,128},{128,160},{160,192},{192,224},{224... | collective-permute-start | bytes 786440 | tf_op jit(solution)/shard_map/ppermute | solution.py:364
  84.2 13.2 %collective-permute-start.12 = (bf16[2,512,128]{2,1,0:T(8,128)(2,1)S(1)}, bf16[2,512,128]{2,1,0:T(8,128)(2,1)S(1)}, u32[]{:S(2)}, u32[]{:S(2)}) collective-permute-start(bf16[2,512,128]{2,1,0:T(8,128)(2,1)S(1)} %get-tuple-element.32), channel_id=1, source_target_pairs={{0,224},{32,0},{64,32},{96,64},{128,96},{160,128},{192,160},{224,1... | collective-permute-start | bytes 786440 | tf_op jit(solution)/shard_map/ppermute | solution.py:364
  87.7 9.5 %collective-permute-start.13 = (bf16[256,128]{1,0:T(8,128)(2,1)S(1)}, bf16[256,128]{1,0:T(8,128)(2,1)S(1)}, u32[]{:S(2)}, u32[]{:S(2)}) collective-permute-start(bf16[256,128]{1,0:T(8,128)(2,1)S(1)} %get-tuple-element.33), channel_id=1, source_target_pairs={{0,64},{32,96},{64,128},{96,160},{128,192},{160,224},{192,0},{224,... | collective-permute-start | bytes 196616 | tf_op jit(solution)/shard_map/ppermute | solution.py:364
  87.7 9.7 %collective-permute-start.14 = (bf16[256,128]{1,0:T(8,128)(2,1)S(1)}, bf16[256,128]{1,0:T(8,128)(2,1)S(1)}, u32[]{:S(2)}, u32[]{:S(2)}) collective-permute-start(bf16[256,128]{1,0:T(8,128)(2,1)S(1)} %get-tuple-element.34), channel_id=1, source_target_pairs={{0,192},{32,224},{64,0},{96,32},{128,64},{160,96},{192,128},{224,1... | collective-permute-start | bytes 196616 | tf_op jit(solution)/shard_map/ppermute | solution.py:364
  95.9 28.9 %copy-start.2 = (bf16[1024,1024]{1,0:T(8,128)(2,1)S(1)}, bf16[1024,1024]{1,0:T(8,128)(2,1)}, u32[]{:S(2)}) copy-start(bf16[1024,1024]{1,0:T(8,128)(2,1)} %copy-done.1) | copy-start | bytes 6291460
  97.6 8.3 %collective-permute-start.15 = (bf16[512,128]{1,0:T(8,128)(2,1)S(1)}, bf16[512,128]{1,0:T(8,128)(2,1)S(1)}, u32[]{:S(2)}, u32[]{:S(2)}) collective-permute-start(bf16[512,128]{1,0:T(8,128)(2,1)S(1)} %get-tuple-element.36), channel_id=1, source_target_pairs={{0,64},{32,96},{64,128},{96,160},{128,192},{160,224},{192,0},{224,... | collective-permute-start | bytes 393224 | tf_op jit(solution)/shard_map/ppermute | solution.py:364
  101.1 8.7 %collective-permute-start.16 = (bf16[512,128]{1,0:T(8,128)(2,1)S(1)}, bf16[512,128]{1,0:T(8,128)(2,1)S(1)}, u32[]{:S(2)}, u32[]{:S(2)}) collective-permute-start(bf16[512,128]{1,0:T(8,128)(2,1)S(1)} %get-tuple-element.37), channel_id=1, source_target_pairs={{0,192},{32,224},{64,0},{96,32},{128,64},{160,96},{192,128},{224,1... | collective-permute-start | bytes 393224 | tf_op jit(solution)/shard_map/ppermute | solution.py:364
  110.5 14.2 %all-to-all-start.2 = ((bf16[16,32,128]{2,1,0:T(8,128)(2,1)}), bf16[16,32,128]{2,1,0:T(8,128)(2,1)S(1)}, u32[]{:S(2)}, u32[]{:S(2)}) async-start(bf16[16,32,128]{2,1,0:T(8,128)(2,1)} %add_groups.1), calls=%async_computation.2 | async-start | bytes 262144 | tf_op jit(solution)/shard_map/all_to_all | solution.py:420

commit v3 on v2

v3 whole, which is shorter than its diff:
```python
import functools

import jax
import jax.numpy as jnp
from jax import lax
from jax.experimental import pallas as pl
from jax.experimental.pallas import tpu as pltpu
from jax.sharding import Mesh, PartitionSpec as P

D = 1024
HEADS = 8
HEAD = 128
BLOCK = 512
BLK = 14
CAP = 2
NZ = 8
NG = 16
NM = 16
SLAB = 32
ROWS = 64
HALF = 512
QROWS = 528
CUT = 256
EPS = 1e-05
SCALE = HEAD**-0.5
G = ("z", "core")
M = ("x", "y")
VM = pl.BlockSpec(memory_space=pltpu.VMEM)
SM = pl.BlockSpec(memory_space=pltpu.SMEM)
HB = pl.BlockSpec(memory_space=pltpu.HBM)


def params(mib):
    return pltpu.CompilerParams(vmem_limit_bytes=mib << 20)


def norm(values):
    center = values - jnp.mean(values, axis=-1, keepdims=True)
    spread = jnp.mean(center * center, axis=-1, keepdims=True)
    return center * lax.rsqrt(spread + EPS)


def silu(v):
    t = 0.5 * v
    return t + t * jnp.tanh(t)


def pack_kernel(pool, after, out):
    for h in range(HEADS):
        for kv in range(2):
            cols = pool[:, :, kv * D + h * HEAD : kv * D + (h + 1) * HEAD]
            for ch in range(2):
                out[h * 2 + ch, kv] = cols


def pack(pool, after):
    return pl.pallas_call(
        pack_kernel,
        out_shape=jax.ShapeDtypeStruct((NM, 2, BLK, SLAB, HEAD), jnp.bfloat16),
        in_specs=[VM, VM],
        out_specs=VM,
        compiler_params=params(12),
        name="pack_history",
    )(pool, after)


def query_kernel(tokens, w, q_out, send_out, rows, buf, sems):
    first = pltpu.make_async_copy(tokens, rows, sems.at[4])
    first.start()
    copies = [
        pltpu.make_async_copy(w.at[:, pl.ds(2 * D + i * 256, 256)], buf.at[i], sems.at[i]) for i in range(4)
    ]
    for c in copies:
        c.start()
    first.wait()
    normed = norm(rows[...].astype(jnp.float32)).astype(jnp.bfloat16)
    for i in range(4):
        copies[i].wait()
        q = silu(jnp.dot(normed, buf[i], preferred_element_type=jnp.float32)).astype(jnp.bfloat16)
        q_out[:, i * 256 : (i + 1) * 256] = q
        for j in range(2):
            for ch in range(2):
                send_out[i * 4 + j * 2 + ch] = q[ch * 32 : ch * 32 + 32, j * HEAD : (j + 1) * HEAD]


def query(tokens, w):
    return pl.pallas_call(
        query_kernel,
        out_shape=(
            jax.ShapeDtypeStruct((ROWS, D), jnp.bfloat16),
            jax.ShapeDtypeStruct((NM, 32, HEAD), jnp.bfloat16),
        ),
        in_specs=[HB, HB],
        out_specs=(VM, VM),
        scratch_shapes=[
            pltpu.VMEM((ROWS, D), jnp.bfloat16),
            pltpu.VMEM((4, D, 256), jnp.bfloat16),
            pltpu.SemaphoreType.DMA((5,)),
        ],
        compiler_params=params(12),
        name="project_query",
    )(pltpu.with_memory_space_constraint(tokens, pltpu.HBM), pltpu.with_memory_space_constraint(w, pltpu.HBM))


def rest_kernel(tokens, w, q, self_bias, w2, gate_out, self_out, w2_out, buf, sems, sem):
    held = pltpu.make_async_copy(w2, w2_out, sem)
    held.start()
    copies = []
    for i in range(4):
        for j, base in enumerate((0, D, 3 * D)):
            n = i * 3 + j
            copies.append(
                pltpu.make_async_copy(w.at[:, pl.ds(base + i * 256, 256)], buf.at[n], sems.at[n])
            )
    for c in copies:
        c.start()
    normed = norm(tokens[...].astype(jnp.float32)).astype(jnp.bfloat16)

    def proj(n):
        copies[n].wait()
        return silu(jnp.dot(normed, buf[n], preferred_element_type=jnp.float32)).astype(jnp.bfloat16)

    for i in range(4):
        wide = slice(i * 256, (i + 1) * 256)
        gate_out[:, wide] = proj(i * 3)
        v = proj(i * 3 + 1).astype(jnp.float32)
        k = proj(i * 3 + 2).astype(jnp.float32)
        qk = q[:, wide].astype(jnp.float32) * k
        for j in range(2):
            cols = slice(j * HEAD, (j + 1) * HEAD)
            s = jnp.sum(qk[:, cols], axis=1, keepdims=True) * SCALE + self_bias[i * 2 + j]
            self_out[:, i * 256 + j * HEAD : i * 256 + (j + 1) * HEAD] = silu(s) * v[:, cols]
    held.wait()


def rest(tokens, w, q, self_bias, w2):
    return pl.pallas_call(
        rest_kernel,
        out_shape=(
            jax.ShapeDtypeStruct((ROWS, D), jnp.bfloat16),
            jax.ShapeDtypeStruct((ROWS, D), jnp.float32),
            pltpu.VMEM((D, D), jnp.bfloat16),
        ),
        in_specs=[VM, HB, VM, SM, HB],
        out_specs=(VM, VM, VM),
        scratch_shapes=[
            pltpu.VMEM((12, D, 256), jnp.bfloat16),
            pltpu.SemaphoreType.DMA((12,)),
            pltpu.SemaphoreType.DMA,
        ],
        compiler_params=params(20),
        name="project_rest",
    )(
        tokens,
        pltpu.with_memory_space_constraint(w, pltpu.HBM),
        q,
        self_bias,
        pltpu.with_memory_space_constraint(w2, pltpu.HBM),
    )


def bundle_kernel(own, low, high, up, down):
    up[:QROWS] = own[...]
    up[QROWS : 2 * QROWS] = high[...]
    up[2 * QROWS :] = low[:CUT]
    down[:QROWS] = own[...]
    down[QROWS : 2 * QROWS] = low[...]
    down[2 * QROWS :] = high[CUT:]


def bundle(own, low, high):
    return pl.pallas_call(
        bundle_kernel,
        out_shape=(
            jax.ShapeDtypeStruct((2 * QROWS + CUT, HEAD), jnp.bfloat16),
            jax.ShapeDtypeStruct((3 * QROWS - CUT, HEAD), jnp.bfloat16),
        ),
        in_specs=[VM] * 3,
        out_specs=(VM, VM),
        compiler_params=params(12),
        name="bundle_queries",
    )(own, low, high)


def stack_kernel(own, low, high, up, down, out):
    out[0] = own[...]
    out[5] = low[...]
    out[3] = high[...]
    out[7] = up[:QROWS]
    out[2] = up[QROWS : 2 * QROWS]
    out[4, :CUT] = up[2 * QROWS :]
    out[1] = down[:QROWS]
    out[6] = down[QROWS : 2 * QROWS]
    out[4, CUT:] = down[2 * QROWS :]


def stack(*pieces):
    return pl.pallas_call(
        stack_kernel,
        out_shape=jax.ShapeDtypeStruct((NZ, QROWS, HEAD), jnp.bfloat16),
        in_specs=[VM] * 5,
        out_specs=VM,
        compiler_params=params(12),
        name="stack_queries",
    )(*pieces)


def table_kernel(where, q_own, q_other, plan, tab, ints, sem):
    o = where[0] * 2 + where[1]
    for i, q in enumerate((q_own, q_other)):
        for s in range(NZ):
            ints[i * NZ + s] = q[s, HALF:].astype(jnp.float32).astype(jnp.int32)[0:8]
    copy = pltpu.make_async_copy(ints.at[:, 0], tab, sem)
    copy.start()
    for i in range(3):
        for b in range(16):
            plan[i, b] = -1
    copy.wait()

    def step(row, carry):
        length = tab[row, 2 * NG * CAP] * 256 + tab[row, 2 * NG * CAP + 1]
        for c in range(CAP):
            slot = tab[row, o * CAP + c]

            @pl.when(slot >= 0)
            def _():
                p = tab[row, NG * CAP + o * CAP + c]
                plan[0, slot] = row
                plan[1, slot] = p
                plan[2, slot] = length - p * BLOCK

        return carry

    lax.fori_loop(0, NG, step, 0)


def table(where, q_own, q_other):
    return pl.pallas_call(
        table_kernel,
        out_shape=jax.ShapeDtypeStruct((3, 16), jnp.int32),
        in_specs=[SM, VM, VM],
        out_specs=SM,
        scratch_shapes=[
            pltpu.SMEM((NG, 128), jnp.int32),
            pltpu.VMEM((NG, 8, 128), jnp.int32),
            pltpu.SemaphoreType.DMA,
        ],
        compiler_params=params(12),
        name="read_tables",
    )(where, q_own, q_other)


def attend_blocks(base, plan, where, bias, q, blocks, ready, out, acc):
    h = where[2]
    acc[...] = jnp.zeros_like(acc)
    for b in range(BLK):
        ready(b)
        row = plan[0, b]

        @pl.when((row >= base) & (row < base + NZ))
        def _():
            keys = blocks[b, :, 0].reshape(BLOCK, HEAD)
            values = blocks[b, :, 1].reshape(BLOCK, HEAD)
            token = lax.broadcasted_iota(jnp.int32, (BLOCK, HEAD), 0)
            values = jnp.where(token < plan[2, b], values, jnp.zeros_like(values))
            scores = lax.dot_general(
                q[row - base, :HALF], keys, (((1,), (1,)), ((), ())), preferred_element_type=jnp.float32
            )
            t = scores * (0.5 * SCALE) + bias[h, plan[1, b]] * 0.5
            weights = (t + t * jnp.tanh(t)).astype(jnp.bfloat16)
            acc[row - base] += jnp.dot(weights, values, preferred_element_type=jnp.float32)

    out[...] = acc[...].astype(jnp.bfloat16)


def other_kernel(plan, where, bias, q, kv, out, blocks, acc, sems):
    copies = [pltpu.make_async_copy(kv.at[:, :, b], blocks.at[b], sems.at[b]) for b in range(BLK)]
    for c in copies:
        c.start()
    attend_blocks(NZ, plan, where, bias, q, blocks, lambda b: copies[b].wait(), out, acc)


def own_kernel(plan, where, bias, q, blocks, out, acc):
    attend_blocks(0, plan, where, bias, q, blocks, lambda b: None, out, acc)


def attend_other(plan, where, bias, q, kv):
    return pl.pallas_call(
        other_kernel,
        out_shape=(
            jax.ShapeDtypeStruct((NZ, HALF, HEAD), jnp.bfloat16),
            jax.ShapeDtypeStruct((BLK, NM, 2, SLAB, HEAD), jnp.bfloat16),
        ),
        in_specs=[SM, SM, SM, VM, HB],
        out_specs=(VM, VM),
        scratch_shapes=[pltpu.VMEM((NZ, HALF, HEAD), jnp.float32), pltpu.SemaphoreType.DMA((BLK,))],
        compiler_params=params(16),
        name="attend_other",
    )(plan, where, bias, q, pltpu.with_memory_space_constraint(kv, pltpu.HBM))


def attend_own(plan, where, bias, q, blocks):
    return pl.pallas_call(
        own_kernel,
        out_shape=jax.ShapeDtypeStruct((NZ, HALF, HEAD), jnp.bfloat16),
        in_specs=[SM, SM, SM, VM, VM],
        out_specs=VM,
        scratch_shapes=[pltpu.VMEM((NZ, HALF, HEAD), jnp.float32)],
        compiler_params=params(16),
        name="attend_own",
    )(plan, where, bias, q, blocks)


def add(*refs):
    total = refs[0].astype(jnp.float32)
    for r in refs[1:]:
        total += r.astype(jnp.float32)
    return total


def far_kernel(a, b, up, down, across):
    for out, slots in ((up, (1, 3)), (down, (7, 5))):
        for i, s in enumerate(slots):
            out[i] = add(a[s], b[s]).astype(jnp.bfloat16)
    across[...] = add(a[4], b[4]).astype(jnp.bfloat16)


def far(a, b):
    two = jax.ShapeDtypeStruct((2, HALF, HEAD), jnp.bfloat16)
    return pl.pallas_call(
        far_kernel,
        out_shape=(two, two, jax.ShapeDtypeStruct((HALF, HEAD), jnp.bfloat16)),
        in_specs=[VM] * 2,
        out_specs=(VM,) * 3,
        compiler_params=params(12),
        name="add_far",
    )(a, b)


def near_kernel(a, b, up, down, here, next_up, next_down):
    here[...] = add(a[0], b[0], up[0], down[0])
    next_up[...] = add(a[2], b[2], up[1]).astype(jnp.bfloat16)
    next_down[...] = add(a[6], b[6], down[1]).astype(jnp.bfloat16)


def near(*args):
    part = jax.ShapeDtypeStruct((HALF, HEAD), jnp.bfloat16)
    return pl.pallas_call(
        near_kernel,
        out_shape=(jax.ShapeDtypeStruct((HALF, HEAD), jnp.float32), part, part),
        in_specs=[VM] * 4,
        out_specs=(VM,) * 3,
        compiler_params=params(12),
        name="add_near",
    )(*args)


def total_kernel(here, across, up, down, out):
    out[...] = add(here[...], across[...], up[...], down[...]).astype(jnp.bfloat16).reshape(NM, 32, HEAD)


def total(*parts):
    return pl.pallas_call(
        total_kernel,
        out_shape=jax.ShapeDtypeStruct((NM, 32, HEAD), jnp.bfloat16),
        in_specs=[VM] * 4,
        out_specs=VM,
        compiler_params=params(12),
        name="add_groups",
    )(*parts)


def tail_kernel(hist, self_term, gate, tokens, w, where, count, out):
    cols = []
    for h in range(HEADS):
        cols.append(jnp.concatenate([hist[h * 2], hist[h * 2 + 1]], axis=0))
    attended = jnp.concatenate(cols, axis=1).astype(jnp.float32) + self_term[...]
    gated = (norm(attended) * gate[...].astype(jnp.float32)).astype(jnp.bfloat16)
    res = jnp.dot(gated, w[...], preferred_element_type=jnp.float32) + tokens[...].astype(jnp.float32)
    row = where[3] * ROWS + lax.broadcasted_iota(jnp.int32, (ROWS, D), 0)
    out[...] = jnp.where(row < count[0], res, 0.0).astype(jnp.bfloat16)


def tail(hist, self_term, gate, tokens, w, where, count):
    return pl.pallas_call(
        tail_kernel,
        out_shape=jax.ShapeDtypeStruct((ROWS, D), jnp.bfloat16),
        in_specs=[VM, VM, VM, VM, VM, SM, SM],
        out_specs=VM,
        compiler_params=params(16),
        name="output",
    )(hist, self_term, gate, tokens, w, where, count)


def move(value, step):
    return lax.ppermute(value, "z", [(i, (i + step) % NZ) for i in range(NZ)])


def swap(value):
    return lax.ppermute(value, "core", [(0, 1), (1, 0)])


def local(
    tokens,
    in_weight,
    out_weight,
    history_pool,
    position_bias,
    self_bias,
    history_length,
    candidate_count,
    block_slots,
    block_position,
):
    z, core, m = lax.axis_index("z"), lax.axis_index("core"), lax.axis_index(M)
    where = jnp.stack([z, core, m // 2, m]).astype(jnp.int32)
    length = history_length[:, None]
    mine = jnp.concatenate(
        [
            block_slots.reshape(1, NG * CAP),
            block_position.reshape(1, NG * CAP),
            length // 256,
            length % 256,
            jnp.zeros((1, 62), jnp.int32),
        ],
        axis=1,
    ).astype(jnp.bfloat16)
    mine = jnp.broadcast_to(mine, (16, 128))
    q, q_send = query(tokens, in_weight)
    q_mine = lax.all_to_all(q_send, M, split_axis=0, concat_axis=0, tiled=True)
    packed = pack(history_pool, q)
    q_mine, packed = lax.optimization_barrier((q_mine, packed))
    kv = lax.all_to_all(packed, M, split_axis=0, concat_axis=0, tiled=True)
    mine = jnp.concatenate([q_mine.reshape(HALF, HEAD), mine], axis=0)
    low, high = move(mine, 3), move(mine, -3)
    up, down = bundle(mine, low, high)
    q_own = stack(mine, low, high, move(up, 1), move(down, -1))
    q_other = swap(q_own)
    plan = table(where, q_own, q_other)
    gate, self_term, w2 = rest(tokens, in_weight, q, self_bias, out_weight)
    kv, gate, self_term, w2, plan = lax.optimization_barrier((kv, gate, self_term, w2, plan))
    other, blocks = attend_other(plan, where, position_bias, q_other, kv)
    other = swap(other)
    own = attend_own(plan, where, position_bias, q_own, blocks)
    up, down, across = far(own, other)
    across = move(across, 4)
    here, up, down = near(own, other, move(up, 1), move(down, -1))
    hist = total(here, across, move(up, 2), move(down, -2))
    hist = lax.all_to_all(hist, M, split_axis=0, concat_axis=0, tiled=True)
    return tail(hist, self_term, gate, tokens, w2, where, candidate_count)


def solution(mesh):
    fine = Mesh(mesh.devices.reshape(NZ, 2, 4, 4), ("z", "core", "x", "y"))
    placed = (
        P(("z", "core", "x", "y"), None),
        P(),
        P(),
        P(("z", "core"), ("x", "y"), None),
        P(),
        P(),
        P(("z", "core")),
        P(("z", "core")),
        P(("z", "core"), None, None),
        P(("z", "core"), None, None),
    )
    return jax.shard_map(
        local, mesh=fine, in_specs=placed, out_specs=P(("z", "core", "x", "y"), None), check_vma=False
    )
```

time: 128 us -> 125 us (0.977)
  the two profiles are of different devices: /device:TPU:2 before, /device:TPU:32 now
where the time goes in v3:
time: 125 us; the launch traced here: 124 us
  waiting for transfers between devices  52.7 us (42%)
  starting transfers between devices  41.8 us (33%)
  Pallas kernels  24.4 us (20%)
  local copies, waits for them, and re-layouts  3.73 us (3%)
  between operations  1.63 us (1%)
    ppermute x9, waiting for transfers between devices, move(): return lax.ppermute(value, 'z', [(i, (i + step) % NZ) for i in range(NZ)])  29.1 us
    ppermute x9, starting transfers between devices, move(): return lax.ppermute(value, 'z', [(i, (i + step) % NZ) for i in range(NZ)])  26.2 us
    all_to_all x1, waiting for transfers between devices, local(): kv = lax.all_to_all(packed, M, split_axis=0, concat_axis=0, tiled=True)  11 us
    all_to_all x1, waiting for transfers between devices, local(): hist = lax.all_to_all(hist, M, split_axis=0, concat_axis=0, tiled=True)  7.19 us
    all_to_all x1, starting transfers between devices, local(): q_mine = lax.all_to_all(q_send, M, split_axis=0, concat_axis=0, tiled=True)  7.05 us
    pallas_call x1, Pallas kernels, rest(): pl.pallas_call(rest_kernel, out_shape=(jax.ShapeDtypeStruct((ROWS, D), jn...  6.12 us
    pallas_call x1, Pallas kernels, attend_other(): pl.pallas_call(other_kernel, out_shape=(jax.ShapeDtypeStruct((NZ, HALF, H...  5.55 us
    all_to_all x1, waiting for transfers between devices, local(): q_mine = lax.all_to_all(q_send, M, split_axis=0, concat_axis=0, tiled=True)  5.48 us
  transfers between devices with their start and end apart: 14, of which 9 were waited for; matrix products, arithmetic and copies ran while one was open for 0% of the time, Pallas kernels for 11%

profile of v3, /device:TPU:32, one launch (start us, length us, event | category | flops | bytes accessed | tf_op | source)
XLA Modules:
  0.0 124.3 jit_solution(11866175475964045877)
XLA Ops:
  0.0 3.1 %project_query.1 = (bf16[64,1024]{1,0:T(8,128)(2,1)S(1)}, bf16[16,32,128]{2,1,0:T(8,128)(2,1)}) custom-call(bf16[64,1024]{1,0:T(8,128)(2,1)} %tokens.5, bf16[1024,4096]{1,0:T(8,128)(2,1)} %w.3), custom_call_target="tpu_custom_call" | custom-call | tf_op jit(solution)/shard_map/project_query/pallas_call | solution.py:87
  3.1 7.0 %all-to-all-start = ((bf16[16,32,128]{2,1,0:T(8,128)(2,1)}), bf16[16,32,128]{2,1,0:T(8,128)(2,1)S(1)}, u32[]{:S(2)}, u32[]{:S(2)}) async-start(bf16[16,32,128]{2,1,0:T(8,128)(2,1)} %get-tuple-element.27), calls=%async_computation | async-start | bytes 262144 | tf_op jit(solution)/shard_map/all_to_all | solution.py:430
  10.2 0.5 pack_history.1
  10.7 1.8 %copy-done = bf16[16,2,14,32,128]{4,3,2,1,0:T(8,128)(2,1)} copy-done((bf16[16,2,14,32,128]{4,3,2,1,0:T(8,128)(2,1)}, bf16[16,2,14,32,128]{4,3,2,1,0:T(8,128)(2,1)S(1)}, u32[]{:S(2)}) %copy-start) | copy-done | bytes 3670040
  12.5 5.5 %all-to-all-done = bf16[16,32,128]{2,1,0:T(8,128)(2,1)S(1)} async-done(((bf16[16,32,128]{2,1,0:T(8,128)(2,1)}), bf16[16,32,128]{2,1,0:T(8,128)(2,1)S(1)}, u32[]{:S(2)}, u32[]{:S(2)}) %all-to-all-start) | async-done | bytes 131104 | tf_op jit(solution)/shard_map/all_to_all | solution.py:430
  18.0 4.5 %all-to-all-start.1 = ((bf16[16,2,14,32,128]{4,3,2,1,0:T(8,128)(2,1)}), bf16[16,2,14,32,128]{4,3,2,1,0:T(8,128)(2,1)}, u32[]{:S(2)}, u32[]{:S(2)}) async-start(bf16[16,2,14,32,128]{4,3,2,1,0:T(8,128)(2,1)} %copy-done), calls=%async_computation.1 | async-start | bytes 7340032 | tf_op jit(solution)/shard_map/all_to_all | solution.py:433
  22.5 0.0 copy-start.4
  22.5 0.0 copy-start.6
  23.3 0.1 copy.13
  23.4 0.1 concatenate.20
  23.5 0.1 copy.14
  23.6 0.1 concatenate.21
  23.7 0.1 concatenate.24
  23.8 5.9 %collective-permute-start = (bf16[528,128]{1,0:T(8,128)(2,1)S(1)}, bf16[528,128]{1,0:T(8,128)(2,1)S(1)}, u32[]{:S(2)}, u32[]{:S(2)}) collective-permute-start(bf16[528,128]{1,0:T(8,128)(2,1)S(1)} %pad_maximum_fusion.own), channel_id=1, source_target_pairs={{0,96},{32,128},{64,160},{96,192},{128,224},{160,0},{192,32},{224,... | collective-permute-start | bytes 405512 | tf_op jit(solution)/shard_map/ppermute | solution.py:396
  29.7 0.1 collective-permute-start.1
  29.8 6.6 %collective-permute-done.low = bf16[528,128]{1,0:T(8,128)(2,1)S(1)} collective-permute-done((bf16[528,128]{1,0:T(8,128)(2,1)S(1)}, bf16[528,128]{1,0:T(8,128)(2,1)S(1)}, u32[]{:S(2)}, u32[]{:S(2)}) %collective-permute-start) | collective-permute-done | bytes 135200 | tf_op jit(solution)/shard_map/ppermute | solution.py:396
  36.4 4.2 %collective-permute-done.1.high = bf16[528,128]{1,0:T(8,128)(2,1)S(1)} collective-permute-done((bf16[528,128]{1,0:T(8,128)(2,1)S(1)}, bf16[528,128]{1,0:T(8,128)(2,1)S(1)}, u32[]{:S(2)}, u32[]{:S(2)}) %collective-permute-start.1) | collective-permute-done | bytes 135200 | tf_op jit(solution)/shard_map/ppermute | solution.py:396
  40.6 0.1 bundle_queries.1
  40.6 0.1 collective-permute-start.3
  40.7 2.9 %collective-permute-start.2 = (bf16[1312,128]{1,0:T(8,128)(2,1)S(1)}, bf16[1312,128]{1,0:T(8,128)(2,1)S(1)}, u32[]{:S(2)}, u32[]{:S(2)}) collective-permute-start(bf16[1312,128]{1,0:T(8,128)(2,1)S(1)} %get-tuple-element.34), channel_id=1, source_target_pairs={{0,32},{32,64},{64,96},{96,128},{128,160},{160,192},{192,224},{224... | collective-permute-start | bytes 1007624 | tf_op jit(solution)/shard_map/ppermute | solution.py:396
  43.6 6.3 %collective-permute-done.2.up = bf16[1312,128]{1,0:T(8,128)(2,1)S(1)} collective-permute-done((bf16[1312,128]{1,0:T(8,128)(2,1)S(1)}, bf16[1312,128]{1,0:T(8,128)(2,1)S(1)}, u32[]{:S(2)}, u32[]{:S(2)}) %collective-permute-start.2) | collective-permute-done | bytes 335904 | tf_op jit(solution)/shard_map/ppermute | solution.py:396
  49.9 0.0 collective-permute-done.3.down
  49.9 0.1 stack_queries.1.q_own.q
  50.0 0.1 collective-permute-start.4
  50.2 6.1 %project_rest.1 = (bf16[64,1024]{1,0:T(8,128)(2,1)S(1)}, f32[64,1024]{1,0:T(8,128)S(1)}, bf16[1024,1024]{1,0:T(8,128)(2,1)S(1)}) custom-call(bf16[64,1024]{1,0:T(8,128)(2,1)S(1)} %copy-done.4, bf16[1024,4096]{1,0:T(8,128)(2,1)} %w.3, bf16[64,1024]{1,0:T(8,128)(2,1)S(1)} %get-tuple-element.28.after.q, f32[8]{0:T(128)S(1)} %copy-done.6, bf16[1024,1024]{1,0:T(8,128)(2,1)} %w2.1), custom_call_target="tpu_custom_call" | custom-call | tf_op jit(solution)/shard_map/project_rest/pallas_call | solution.py:137
  56.3 1.4 %copy-done.1 = bf16[1024,1024]{1,0:T(8,128)(2,1)} copy-done((bf16[1024,1024]{1,0:T(8,128)(2,1)}, bf16[1024,1024]{1,0:T(8,128)(2,1)S(1)}, u32[]{:S(2)}) %copy-start.1) | copy-done | bytes 2097176
  57.7 0.1 pad_add_fusion.where
  57.8 0.0 collective-permute-done.4.q_other.q
  57.8 2.2 %read_tables.1.plan = s32[3,16]{1,0:T(4,128)S(1)} custom-call(s32[4]{0:T(128)S(1)} %pad_add_fusion.where, bf16[8,528,128]{2,1,0:T(8,128)(2,1)S(1)} %stack_queries.1.q_own.q, bf16[8,528,128]{2,1,0:T(8,128)(2,1)S(1)} %collective-permute-done.4.q_other.q), custom_call_target="tpu_custom_call" | custom-call | tf_op jit(solution)/shard_map/read_tables/pallas_call | solution.py:238
  60.0 11.0 %all-to-all-done.1.kv = bf16[16,2,14,32,128]{4,3,2,1,0:T(8,128)(2,1)} async-done(((bf16[16,2,14,32,128]{4,3,2,1,0:T(8,128)(2,1)}), bf16[16,2,14,32,128]{4,3,2,1,0:T(8,128)(2,1)}, u32[]{:S(2)}, u32[]{:S(2)}) %all-to-all-start.1) | async-done | bytes 3670048 | tf_op jit(solution)/shard_map/all_to_all | solution.py:433
  70.9 5.5 %attend_other.1 = (bf16[8,512,128]{2,1,0:T(8,128)(2,1)S(1)}, bf16[14,16,2,32,128]{4,3,2,1,0:T(8,128)(2,1)S(1)}) custom-call(s32[3,16]{1,0:T(4,128)S(1)} %read_tables.1.plan, s32[4]{0:T(128)S(1)} %pad_add_fusion.where, f32[8,14]{1,0:T(8,128)S(1)} %copy-done.5, bf16[8,528,128]{2,1,0:T(8,128)(2,1)S(1)} %collective-permute-done.4.q_other.q, ...), custom_call_target="tpu_custom_call" | custom-call | tf_op jit(solution)/shard_map/attend_other/pallas_call | solution.py:288
  76.5 0.1 collective-permute-start.5
  76.6 3.9 %attend_own.1.a = bf16[8,512,128]{2,1,0:T(8,128)(2,1)S(1)} custom-call(s32[3,16]{1,0:T(4,128)S(1)} %read_tables.1.plan, s32[4]{0:T(128)S(1)} %pad_add_fusion.where, f32[8,14]{1,0:T(8,128)S(1)} %copy-done.5, bf16[8,528,128]{2,1,0:T(8,128)(2,1)S(1)} %stack_queries.1.q_own.q, bf16[14,16,2,32,128]{4,3,2,1,0:T(8,128)(2,1)S(1)} %get-tuple-element.38.blocks), custom_call_target="tpu_custom_call" | custom-call | tf_op jit(solution)/shard_map/attend_own/pallas_call | solution.py:303
  80.5 0.0 collective-permute-done.5.b
  80.5 0.2 add_far.1
  80.7 2.6 %collective-permute-start.6 = (bf16[2,512,128]{2,1,0:T(8,128)(2,1)S(1)}, bf16[2,512,128]{2,1,0:T(8,128)(2,1)S(1)}, u32[]{:S(2)}, u32[]{:S(2)}) collective-permute-start(bf16[2,512,128]{2,1,0:T(8,128)(2,1)S(1)} %get-tuple-element.40), channel_id=1, source_target_pairs={{0,32},{32,64},{64,96},{96,128},{128,160},{160,192},{192,224},{224... | collective-permute-start | bytes 786440 | tf_op jit(solution)/shard_map/ppermute | solution.py:396
  83.3 0.0 collective-permute-start.7
  83.3 5.8 %collective-permute-start.8 = (bf16[512,128]{1,0:T(8,128)(2,1)S(1)}, bf16[512,128]{1,0:T(8,128)(2,1)S(1)}, u32[]{:S(2)}, u32[]{:S(2)}) collective-permute-start(bf16[512,128]{1,0:T(8,128)(2,1)S(1)} %get-tuple-element.43), channel_id=1, source_target_pairs={{0,128},{32,160},{64,192},{96,224},{128,0},{160,32},{192,64},{224,... | collective-permute-start | bytes 393224 | tf_op jit(solution)/shard_map/ppermute | solution.py:396
  89.1 2.0 %collective-permute-done.7.down = bf16[2,512,128]{2,1,0:T(8,128)(2,1)S(1)} collective-permute-done((bf16[2,512,128]{2,1,0:T(8,128)(2,1)S(1)}, bf16[2,512,128]{2,1,0:T(8,128)(2,1)S(1)}, u32[]{:S(2)}, u32[]{:S(2)}) %collective-permute-start.7) | collective-permute-done | bytes 262176 | tf_op jit(solution)/shard_map/ppermute | solution.py:396
  91.0 0.2 add_near.1
  91.2 8.9 %collective-permute-start.10 = (bf16[512,128]{1,0:T(8,128)(2,1)S(1)}, bf16[512,128]{1,0:T(8,128)(2,1)S(1)}, u32[]{:S(2)}, u32[]{:S(2)}) collective-permute-start(bf16[512,128]{1,0:T(8,128)(2,1)S(1)} %get-tuple-element.45), channel_id=1, source_target_pairs={{0,192},{32,224},{64,0},{96,32},{128,64},{160,96},{192,128},{224,1... | collective-permute-start | bytes 393224 | tf_op jit(solution)/shard_map/ppermute | solution.py:396
  100.1 0.0 collective-permute-start.9
  100.1 6.1 %collective-permute-done.10.down = bf16[512,128]{1,0:T(8,128)(2,1)S(1)} collective-permute-done((bf16[512,128]{1,0:T(8,128)(2,1)S(1)}, bf16[512,128]{1,0:T(8,128)(2,1)S(1)}, u32[]{:S(2)}, u32[]{:S(2)}) %collective-permute-start.10) | collective-permute-done | bytes 131104 | tf_op jit(solution)/shard_map/ppermute | solution.py:396
  106.2 3.9 %collective-permute-done.9.up = bf16[512,128]{1,0:T(8,128)(2,1)S(1)} collective-permute-done((bf16[512,128]{1,0:T(8,128)(2,1)S(1)}, bf16[512,128]{1,0:T(8,128)(2,1)S(1)}, u32[]{:S(2)}, u32[]{:S(2)}) %collective-permute-start.9) | collective-permute-done | bytes 131104 | tf_op jit(solution)/shard_map/ppermute | solution.py:396
  110.1 0.7 add_groups.1
  110.8 3.8 %all-to-all-start.2 = ((bf16[16,32,128]{2,1,0:T(8,128)(2,1)}), bf16[16,32,128]{2,1,0:T(8,128)(2,1)S(1)}, u32[]{:S(2)}, u32[]{:S(2)}) async-start(bf16[16,32,128]{2,1,0:T(8,128)(2,1)} %add_groups.1), calls=%async_computation.2 | async-start | bytes 262144 | tf_op jit(solution)/shard_map/all_to_all | solution.py:449
  115.3 7.2 %all-to-all-done.2.hist = bf16[16,32,128]{2,1,0:T(8,128)(2,1)S(1)} async-done(((bf16[16,32,128]{2,1,0:T(8,128)(2,1)}), bf16[16,32,128]{2,1,0:T(8,128)(2,1)S(1)}, u32[]{:S(2)}, u32[]{:S(2)}) %all-to-all-start.2) | async-done | bytes 131104 | tf_op jit(solution)/shard_map/all_to_all | solution.py:449
  122.5 1.9 %output.1 = bf16[64,1024]{1,0:T(8,128)(2,1)} custom-call(bf16[16,32,128]{2,1,0:T(8,128)(2,1)S(1)} %all-to-all-done.2.hist, f32[64,1024]{1,0:T(8,128)S(1)} %get-tuple-element.46.self_term, bf16[64,1024]{1,0:T(8,128)(2,1)S(1)} %get-tuple-element.47.gate, bf16[64,1024]{1,0:T(8,128)(2,1)S(1)} %copy-done.4, bf16[1024,1024]{1,0:T(8,128)(2,1)S(1)} %copy-done.2, ...), custom_call_target="tpu_custom_call" | custom-call | tf_op jit(solution)/shard_map/output/pallas_call | solution.py:385
  (21 shorter events, 0.1 us)
Async XLA Ops:
  0.0 10.1 %copy-start.3 = (bf16[14,32,2048]{2,1,0:T(8,128)(2,1)S(1)}, bf16[14,32,2048]{2,1,0:T(8,128)(2,1)}, u32[]{:S(2)}) copy-start(bf16[14,32,2048]{2,1,0:T(8,128)(2,1)} %pool.1) | copy-start | bytes 5505028
  3.1 14.9 %all-to-all-start = ((bf16[16,32,128]{2,1,0:T(8,128)(2,1)}), bf16[16,32,128]{2,1,0:T(8,128)(2,1)S(1)}, u32[]{:S(2)}, u32[]{:S(2)}) async-start(bf16[16,32,128]{2,1,0:T(8,128)(2,1)} %get-tuple-element.27), calls=%async_computation | async-start | bytes 262144 | tf_op jit(solution)/shard_map/all_to_all | solution.py:430
  10.7 1.8 %copy-start = (bf16[16,2,14,32,128]{4,3,2,1,0:T(8,128)(2,1)}, bf16[16,2,14,32,128]{4,3,2,1,0:T(8,128)(2,1)S(1)}, u32[]{:S(2)}) copy-start(bf16[16,2,14,32,128]{4,3,2,1,0:T(8,128)(2,1)S(1)} %pack_history.1) | copy-start | bytes 11010052
  12.5 10.8 %copy-start.7 = (s32[1,16,2]{1,2,0:T(2,128)S(1)}, s32[1,16,2]{1,2,0:T(2,128)}, u32[]{:S(2)}) copy-start(s32[1,16,2]{1,2,0:T(2,128)} %param.18) | copy-start | bytes 388
  12.5 11.0 %copy-start.8 = (s32[1,16,2]{1,2,0:T(2,128)S(1)}, s32[1,16,2]{1,2,0:T(2,128)}, u32[]{:S(2)}) copy-start(s32[1,16,2]{1,2,0:T(2,128)} %param.19) | copy-start | bytes 388
  18.0 52.9 %all-to-all-start.1 = ((bf16[16,2,14,32,128]{4,3,2,1,0:T(8,128)(2,1)}), bf16[16,2,14,32,128]{4,3,2,1,0:T(8,128)(2,1)}, u32[]{:S(2)}, u32[]{:S(2)}) async-start(bf16[16,2,14,32,128]{4,3,2,1,0:T(8,128)(2,1)} %copy-done), calls=%async_computation.1 | async-start | bytes 7340032 | tf_op jit(solution)/shard_map/all_to_all | solution.py:433
  22.5 27.6 %copy-start.4 = (bf16[64,1024]{1,0:T(8,128)(2,1)S(1)}, bf16[64,1024]{1,0:T(8,128)(2,1)}, u32[]{:S(2)}) copy-start(bf16[64,1024]{1,0:T(8,128)(2,1)} %tokens.5) | copy-start | bytes 393220
  22.5 27.6 %copy-start.6 = (f32[8]{0:T(128)S(1)}, f32[8]{0:T(128)}, u32[]{:S(2)}) copy-start(f32[8]{0:T(128)} %self_bias.1) | copy-start | bytes 100
  23.8 12.6 %collective-permute-start = (bf16[528,128]{1,0:T(8,128)(2,1)S(1)}, bf16[528,128]{1,0:T(8,128)(2,1)S(1)}, u32[]{:S(2)}, u32[]{:S(2)}) collective-permute-start(bf16[528,128]{1,0:T(8,128)(2,1)S(1)} %pad_maximum_fusion.own), channel_id=1, source_target_pairs={{0,96},{32,128},{64,160},{96,192},{128,224},{160,0},{192,32},{224,... | collective-permute-start | bytes 405512 | tf_op jit(solution)/shard_map/ppermute | solution.py:396
  29.7 10.8 %collective-permute-start.1 = (bf16[528,128]{1,0:T(8,128)(2,1)S(1)}, bf16[528,128]{1,0:T(8,128)(2,1)S(1)}, u32[]{:S(2)}, u32[]{:S(2)}) collective-permute-start(bf16[528,128]{1,0:T(8,128)(2,1)S(1)} %pad_maximum_fusion.own), channel_id=1, source_target_pairs={{0,160},{32,192},{64,224},{96,0},{128,32},{160,64},{192,96},{224,1... | collective-permute-start | bytes 405512 | tf_op jit(solution)/shard_map/ppermute | solution.py:396
  40.6 9.3 %collective-permute-start.3 = (bf16[1328,128]{1,0:T(8,128)(2,1)S(1)}, bf16[1328,128]{1,0:T(8,128)(2,1)S(1)}, u32[]{:S(2)}, u32[]{:S(2)}) collective-permute-start(bf16[1328,128]{1,0:T(8,128)(2,1)S(1)} %get-tuple-element.35), channel_id=1, source_target_pairs={{0,224},{32,0},{64,32},{96,64},{128,96},{160,128},{192,160},{224,1... | collective-permute-start | bytes 1019912 | tf_op jit(solution)/shard_map/ppermute | solution.py:396
  40.7 9.2 %collective-permute-start.2 = (bf16[1312,128]{1,0:T(8,128)(2,1)S(1)}, bf16[1312,128]{1,0:T(8,128)(2,1)S(1)}, u32[]{:S(2)}, u32[]{:S(2)}) collective-permute-start(bf16[1312,128]{1,0:T(8,128)(2,1)S(1)} %get-tuple-element.34), channel_id=1, source_target_pairs={{0,32},{32,64},{64,96},{96,128},{128,160},{160,192},{192,224},{224... | collective-permute-start | bytes 1007624 | tf_op jit(solution)/shard_map/ppermute | solution.py:396
  50.0 7.7 %collective-permute-start.4 = (bf16[8,528,128]{2,1,0:T(8,128)(2,1)S(1)}, bf16[8,528,128]{2,1,0:T(8,128)(2,1)S(1)}, u32[]{:S(2)}, u32[]{:S(2)}) collective-permute-start(bf16[8,528,128]{2,1,0:T(8,128)(2,1)S(1)} %stack_queries.1.q_own.q), channel_id=1, source_target_pairs={{0,16},{16,0},{1,17},{17,1},{2,18},{18,2},{3,19},{19,3},{4,20},{20... | collective-permute-start | bytes 3244040 | tf_op jit(solution)/shard_map/ppermute | solution.py:400
  56.3 1.4 %copy-start.1 = (bf16[1024,1024]{1,0:T(8,128)(2,1)}, bf16[1024,1024]{1,0:T(8,128)(2,1)S(1)}, u32[]{:S(2)}) copy-start(bf16[1024,1024]{1,0:T(8,128)(2,1)S(1)} %get-tuple-element.48.w) | copy-start | bytes 6291460
  57.7 13.2 %copy-start.5 = (f32[8,14]{1,0:T(8,128)S(1)}, f32[8,14]{1,0:T(8,128)}, u32[]{:S(2)}) copy-start(f32[8,14]{1,0:T(8,128)} %bias.3) | copy-start | bytes 1348
  76.5 4.0 %collective-permute-start.5 = (bf16[8,512,128]{2,1,0:T(8,128)(2,1)S(1)}, bf16[8,512,128]{2,1,0:T(8,128)(2,1)S(1)}, u32[]{:S(2)}, u32[]{:S(2)}) collective-permute-start(bf16[8,512,128]{2,1,0:T(8,128)(2,1)S(1)} %get-tuple-element.39), channel_id=1, source_target_pairs={{0,16},{16,0},{1,17},{17,1},{2,18},{18,2},{3,19},{19,3},{4,20},{20... | collective-permute-start | bytes 3145736 | tf_op jit(solution)/shard_map/ppermute | solution.py:400
  80.7 41.8 %copy-start.2 = (bf16[1024,1024]{1,0:T(8,128)(2,1)S(1)}, bf16[1024,1024]{1,0:T(8,128)(2,1)}, u32[]{:S(2)}) copy-start(bf16[1024,1024]{1,0:T(8,128)(2,1)} %copy-done.1) | copy-start | bytes 6291460
  80.7 8.4 %collective-permute-start.6 = (bf16[2,512,128]{2,1,0:T(8,128)(2,1)S(1)}, bf16[2,512,128]{2,1,0:T(8,128)(2,1)S(1)}, u32[]{:S(2)}, u32[]{:S(2)}) collective-permute-start(bf16[2,512,128]{2,1,0:T(8,128)(2,1)S(1)} %get-tuple-element.40), channel_id=1, source_target_pairs={{0,32},{32,64},{64,96},{96,128},{128,160},{160,192},{192,224},{224... | collective-permute-start | bytes 786440 | tf_op jit(solution)/shard_map/ppermute | solution.py:396
  83.3 7.8 %collective-permute-start.7 = (bf16[2,512,128]{2,1,0:T(8,128)(2,1)S(1)}, bf16[2,512,128]{2,1,0:T(8,128)(2,1)S(1)}, u32[]{:S(2)}, u32[]{:S(2)}) collective-permute-start(bf16[2,512,128]{2,1,0:T(8,128)(2,1)S(1)} %get-tuple-element.41), channel_id=1, source_target_pairs={{0,224},{32,0},{64,32},{96,64},{128,96},{160,128},{192,160},{224,1... | collective-permute-start | bytes 786440 | tf_op jit(solution)/shard_map/ppermute | solution.py:396
  83.3 16.8 %collective-permute-start.8 = (bf16[512,128]{1,0:T(8,128)(2,1)S(1)}, bf16[512,128]{1,0:T(8,128)(2,1)S(1)}, u32[]{:S(2)}, u32[]{:S(2)}) collective-permute-start(bf16[512,128]{1,0:T(8,128)(2,1)S(1)} %get-tuple-element.43), channel_id=1, source_target_pairs={{0,128},{32,160},{64,192},{96,224},{128,0},{160,32},{192,64},{224,... | collective-permute-start | bytes 393224 | tf_op jit(solution)/shard_map/ppermute | solution.py:396
  91.2 15.0 %collective-permute-start.10 = (bf16[512,128]{1,0:T(8,128)(2,1)S(1)}, bf16[512,128]{1,0:T(8,128)(2,1)S(1)}, u32[]{:S(2)}, u32[]{:S(2)}) collective-permute-start(bf16[512,128]{1,0:T(8,128)(2,1)S(1)} %get-tuple-element.45), channel_id=1, source_target_pairs={{0,192},{32,224},{64,0},{96,32},{128,64},{160,96},{192,128},{224,1... | collective-permute-start | bytes 393224 | tf_op jit(solution)/shard_map/ppermute | solution.py:396
  100.1 10.0 %collective-permute-start.9 = (bf16[512,128]{1,0:T(8,128)(2,1)S(1)}, bf16[512,128]{1,0:T(8,128)(2,1)S(1)}, u32[]{:S(2)}, u32[]{:S(2)}) collective-permute-start(bf16[512,128]{1,0:T(8,128)(2,1)S(1)} %get-tuple-element.44), channel_id=1, source_target_pairs={{0,64},{32,96},{64,128},{96,160},{128,192},{160,224},{192,0},{224,... | collective-permute-start | bytes 393224 | tf_op jit(solution)/shard_map/ppermute | solution.py:396
  110.8 11.6 %all-to-all-start.2 = ((bf16[16,32,128]{2,1,0:T(8,128)(2,1)}), bf16[16,32,128]{2,1,0:T(8,128)(2,1)S(1)}, u32[]{:S(2)}, u32[]{:S(2)}) async-start(bf16[16,32,128]{2,1,0:T(8,128)(2,1)} %add_groups.1), calls=%async_computation.2 | async-start | bytes 262144 | tf_op jit(solution)/shard_map/all_to_all | solution.py:449

commit v4 on v3

--- a/solution.py
+++ b/solution.py
@@ -20,7 +20,8 @@
 ROWS = 64
 HALF = 512
 QROWS = 528
-CUT = 256
+CUT = 272
+FIRST = 9
 EPS = 1e-05
 SCALE = HEAD**-0.5
 G = ("z", "core")
@@ -159,50 +160,66 @@
     )
 
 
-def bundle_kernel(own, low, high, up, down):
-    up[:QROWS] = own[...]
-    up[QROWS : 2 * QROWS] = high[...]
-    up[2 * QROWS :] = low[:CUT]
-    down[:QROWS] = own[...]
-    down[QROWS : 2 * QROWS] = low[...]
-    down[2 * QROWS :] = high[CUT:]
-
-
-def bundle(own, low, high):
+def by_side(where, body, first, second, width=1):
+    even = lax.rem(lax.div(where[0], width), 2) == 0
+
+    @pl.when(even)
+    def _():
+        body(*first, *second)
+
+    @pl.when(jnp.logical_not(even))
+    def _():
+        body(*second, *first)
+
+
+def bundle_kernel(where, own, far_a, far_b, out_a, out_b):
+    def body(high, up, low, down):
+        up[:QROWS] = own[...]
+        up[QROWS : 2 * QROWS] = high[...]
+        up[2 * QROWS :] = low[:CUT]
+        down[:QROWS] = own[...]
+        down[QROWS : 2 * QROWS] = low[...]
+        down[2 * QROWS :] = high[QROWS - CUT :]
+
+    by_side(where, body, (far_a, out_a), (far_b, out_b))
+
+
+def bundle(*args):
+    shape = jax.ShapeDtypeStruct((2 * QROWS + CUT, HEAD), jnp.bfloat16)
     return pl.pallas_call(
         bundle_kernel,
-        out_shape=(
-            jax.ShapeDtypeStruct((2 * QROWS + CUT, HEAD), jnp.bfloat16),
-            jax.ShapeDtypeStruct((3 * QROWS - CUT, HEAD), jnp.bfloat16),
-        ),
-        in_specs=[VM] * 3,
+        out_shape=(shape, shape),
+        in_specs=[SM] + [VM] * 3,
         out_specs=(VM, VM),
         compiler_params=params(12),
         name="bundle_queries",
-    )(own, low, high)
-
-
-def stack_kernel(own, low, high, up, down, out):
-    out[0] = own[...]
-    out[5] = low[...]
-    out[3] = high[...]
-    out[7] = up[:QROWS]
-    out[2] = up[QROWS : 2 * QROWS]
-    out[4, :CUT] = up[2 * QROWS :]
-    out[1] = down[:QROWS]
-    out[6] = down[QROWS : 2 * QROWS]
-    out[4, CUT:] = down[2 * QROWS :]
-
-
-def stack(*pieces):
+    )(*args)
+
+
+def stack_kernel(where, own, far_a, far_b, near_a, near_b, out):
+    def body(high, plus, low, minus):
+        out[0] = own[...]
+        out[5] = low[...]
+        out[3] = high[...]
+        out[7] = minus[:QROWS]
+        out[2] = minus[QROWS : 2 * QROWS]
+        out[4, :CUT] = minus[2 * QROWS :]
+        out[1] = plus[:QROWS]
+        out[6] = plus[QROWS : 2 * QROWS]
+        out[4, QROWS - CUT :] = plus[2 * QROWS :]
+
+    by_side(where, body, (far_a, near_a), (far_b, near_b))
+
+
+def stack(*args):
     return pl.pallas_call(
         stack_kernel,
         out_shape=jax.ShapeDtypeStruct((NZ, QROWS, HEAD), jnp.bfloat16),
-        in_specs=[VM] * 5,
+        in_specs=[SM] + [VM] * 5,
         out_specs=VM,
         compiler_params=params(12),
         name="stack_queries",
-    )(*pieces)
+    )(*args)
 
 
 def table_kernel(where, q_own, q_other, plan, tab, ints, sem):
@@ -212,7 +229,7 @@
             ints[i * NZ + s] = q[s, HALF:].astype(jnp.float32).astype(jnp.int32)[0:8]
     copy = pltpu.make_async_copy(ints.at[:, 0], tab, sem)
     copy.start()
-    for i in range(3):
+    for i in range(4):
         for b in range(16):
             plan[i, b] = -1
     copy.wait()
@@ -232,12 +249,21 @@
         return carry
 
     lax.fori_loop(0, NG, step, 0)
+    budget = FIRST
+    for b in range(BLK):
+        budget -= (plan[0, b] >= NZ).astype(jnp.int32)
+    for b in range(BLK):
+        row = plan[0, b]
+        mine = (row >= 0) & (row < NZ)
+        later = mine & (budget <= 0)
+        budget -= mine.astype(jnp.int32)
+        plan[3, b] = jnp.where(row < 0, -1, jnp.where(later, 1, 0))
 
 
 def table(where, q_own, q_other):
     return pl.pallas_call(
         table_kernel,
-        out_shape=jax.ShapeDtypeStruct((3, 16), jnp.int32),
+        out_shape=jax.ShapeDtypeStruct((4, 16), jnp.int32),
         in_specs=[SM, VM, VM],
         out_specs=SM,
         scratch_shapes=[
@@ -250,65 +276,72 @@
     )(where, q_own, q_other)
 
 
-def attend_blocks(base, plan, where, bias, q, blocks, ready, out, acc):
+def attend_blocks(phase, plan, where, bias, pick, blocks, ready, acc):
     h = where[2]
-    acc[...] = jnp.zeros_like(acc)
     for b in range(BLK):
         ready(b)
-        row = plan[0, b]
-
-        @pl.when((row >= base) & (row < base + NZ))
+
+        @pl.when(plan[3, b] == phase)
         def _():
+            row = plan[0, b]
             keys = blocks[b, :, 0].reshape(BLOCK, HEAD)
             values = blocks[b, :, 1].reshape(BLOCK, HEAD)
             token = lax.broadcasted_iota(jnp.int32, (BLOCK, HEAD), 0)
             values = jnp.where(token < plan[2, b], values, jnp.zeros_like(values))
             scores = lax.dot_general(
-                q[row - base, :HALF], keys, (((1,), (1,)), ((), ())), preferred_element_type=jnp.float32
+                pick(row), keys, (((1,), (1,)), ((), ())), preferred_element_type=jnp.float32
             )
             t = scores * (0.5 * SCALE) + bias[h, plan[1, b]] * 0.5
             weights = (t + t * jnp.tanh(t)).astype(jnp.bfloat16)
-            acc[row - base] += jnp.dot(weights, values, preferred_element_type=jnp.float32)
-
-    out[...] = acc[...].astype(jnp.bfloat16)
-
-
-def other_kernel(plan, where, bias, q, kv, out, blocks, acc, sems):
+            acc[row] += jnp.dot(weights, values, preferred_element_type=jnp.float32)
+
+
+def first_kernel(plan, where, bias, q_own, q_other, kv, own, other, blocks, acc, sems):
     copies = [pltpu.make_async_copy(kv.at[:, :, b], blocks.at[b], sems.at[b]) for b in range(BLK)]
     for c in copies:
         c.start()
-    attend_blocks(NZ, plan, where, bias, q, blocks, lambda b: copies[b].wait(), out, acc)
-
-
-def own_kernel(plan, where, bias, q, blocks, out, acc):
-    attend_blocks(0, plan, where, bias, q, blocks, lambda b: None, out, acc)
-
-
-def attend_other(plan, where, bias, q, kv):
-    return pl.pallas_call(
-        other_kernel,
+    acc[...] = jnp.zeros_like(acc)
+
+    def pick(row):
+        return jnp.where(row < NZ, q_own[lax.rem(row, NZ), :HALF], q_other[lax.rem(row, NZ), :HALF])
+
+    attend_blocks(0, plan, where, bias, pick, blocks, lambda b: copies[b].wait(), acc)
+    own[...] = acc[:NZ]
+    other[...] = acc[NZ:].astype(jnp.bfloat16)
+
+
+def second_kernel(plan, where, bias, q, blocks, own, out, acc):
+    acc[...] = own[...]
+    attend_blocks(1, plan, where, bias, lambda row: q[row, :HALF], blocks, lambda b: None, acc)
+    out[...] = acc[...].astype(jnp.bfloat16)
+
+
+def attend_first(plan, where, bias, q_own, q_other, kv):
+    return pl.pallas_call(
+        first_kernel,
         out_shape=(
+            jax.ShapeDtypeStruct((NZ, HALF, HEAD), jnp.float32),
             jax.ShapeDtypeStruct((NZ, HALF, HEAD), jnp.bfloat16),
             jax.ShapeDtypeStruct((BLK, NM, 2, SLAB, HEAD), jnp.bfloat16),
         ),
-        in_specs=[SM, SM, SM, VM, HB],
-        out_specs=(VM, VM),
-        scratch_shapes=[pltpu.VMEM((NZ, HALF, HEAD), jnp.float32), pltpu.SemaphoreType.DMA((BLK,))],
-        compiler_params=params(16),
-        name="attend_other",
-    )(plan, where, bias, q, pltpu.with_memory_space_constraint(kv, pltpu.HBM))
-
-
-def attend_own(plan, where, bias, q, blocks):
-    return pl.pallas_call(
-        own_kernel,
+        in_specs=[SM, SM, SM, VM, VM, HB],
+        out_specs=(VM, VM, VM),
+        scratch_shapes=[pltpu.VMEM((NG, HALF, HEAD), jnp.float32), pltpu.SemaphoreType.DMA((BLK,))],
+        compiler_params=params(20),
+        name="attend_first",
+    )(plan, where, bias, q_own, q_other, pltpu.with_memory_space_constraint(kv, pltpu.HBM))
+
+
+def attend_second(plan, where, bias, q, blocks, own):
+    return pl.pallas_call(
+        second_kernel,
         out_shape=jax.ShapeDtypeStruct((NZ, HALF, HEAD), jnp.bfloat16),
-        in_specs=[SM, SM, SM, VM, VM],
+        in_specs=[SM, SM, SM, VM, VM, VM],
         out_specs=VM,
         scratch_shapes=[pltpu.VMEM((NZ, HALF, HEAD), jnp.float32)],
         compiler_params=params(16),
-        name="attend_own",
-    )(plan, where, bias, q, blocks)
+        name="attend_second",
+    )(plan, where, bias, q, blocks, own)
 
 
 def add(*refs):
@@ -318,52 +351,90 @@
     return total
 
 
-def far_kernel(a, b, up, down, across):
-    for out, slots in ((up, (1, 3)), (down, (7, 5))):
-        for i, s in enumerate(slots):
-            out[i] = add(a[s], b[s]).astype(jnp.bfloat16)
-    across[...] = add(a[4], b[4]).astype(jnp.bfloat16)
-
-
-def far(a, b):
-    two = jax.ShapeDtypeStruct((2, HALF, HEAD), jnp.bfloat16)
+def far_kernel(where, a, b, out_a, out_b, half_a, half_b):
+    def body(up, down):
+        up[...] = add(a[3], b[3]).astype(jnp.bfloat16)
+        down[...] = add(a[5], b[5]).astype(jnp.bfloat16)
+
+    def opposite(up, down):
+        up[...] = add(a[4, :256], b[4, :256]).astype(jnp.bfloat16)
+        down[...] = add(a[4, 256:], b[4, 256:]).astype(jnp.bfloat16)
+
+    by_side(where, body, (out_a,), (out_b,))
+    by_side(where, opposite, (half_a,), (half_b,), 2)
+
+
+def far(*args):
+    part = jax.ShapeDtypeStruct((HALF, HEAD), jnp.bfloat16)
+    half = jax.ShapeDtypeStruct((256, HEAD), jnp.bfloat16)
     return pl.pallas_call(
         far_kernel,
-        out_shape=(two, two, jax.ShapeDtypeStruct((HALF, HEAD), jnp.bfloat16)),
-        in_specs=[VM] * 2,
-        out_specs=(VM,) * 3,
+        out_shape=(part, part, half, half),
+        in_specs=[SM] + [VM] * 2,
+        out_specs=(VM,) * 4,
         compiler_params=params(12),
         name="add_far",
-    )(a, b)
-
-
-def near_kernel(a, b, up, down, here, next_up, next_down):
-    here[...] = add(a[0], b[0], up[0], down[0])
-    next_up[...] = add(a[2], b[2], up[1]).astype(jnp.bfloat16)
-    next_down[...] = add(a[6], b[6], down[1]).astype(jnp.bfloat16)
+    )(*args)
+
+
+def side_kernel(where, a, b, after, out_a, out_b):
+    def body(up, down):
+        up[...] = add(a[1], b[1]).astype(jnp.bfloat16)
+        down[...] = add(a[7], b[7]).astype(jnp.bfloat16)
+
+    by_side(where, body, (out_a,), (out_b,))
+
+
+def side(*args):
+    part = jax.ShapeDtypeStruct((HALF, HEAD), jnp.bfloat16)
+    return pl.pallas_call(
+        side_kernel,
+        out_shape=(part, part),
+        in_specs=[SM] + [VM] * 3,
+        out_specs=(VM,) * 2,
+        compiler_params=params(12),
+        name="add_side",
+    )(*args)
+
+
+def near_kernel(where, a, b, near_a, near_b, half_a, half_b, out_a, out_b, ups, downs):
+    def body(plus, minus):
+        ups[...] = add(a[2], b[2], minus[...])
+        downs[...] = add(a[6], b[6], plus[...])
+
+    def opposite(plus, up, minus, down):
+        up[:256] = add(ups[:256], minus[...]).astype(jnp.bfloat16)
+        up[256:] = ups[256:].astype(jnp.bfloat16)
+        down[:256] = downs[:256].astype(jnp.bfloat16)
+        down[256:] = add(downs[256:], plus[...]).astype(jnp.bfloat16)
+
+    by_side(where, body, (near_a,), (near_b,))
+    by_side(where, opposite, (half_a, out_a), (half_b, out_b), 2)
 
 
 def near(*args):
     part = jax.ShapeDtypeStruct((HALF, HEAD), jnp.bfloat16)
     return pl.pallas_call(
         near_kernel,
-        out_shape=(jax.ShapeDtypeStruct((HALF, HEAD), jnp.float32), part, part),
-        in_specs=[VM] * 4,
-        out_specs=(VM,) * 3,
+        out_shape=(part, part),
+        in_specs=[SM] + [VM] * 6,
+        out_specs=(VM,) * 2,
+        scratch_shapes=[pltpu.VMEM((HALF, HEAD), jnp.float32)] * 2,
         compiler_params=params(12),
         name="add_near",
     )(*args)
 
 
-def total_kernel(here, across, up, down, out):
-    out[...] = add(here[...], across[...], up[...], down[...]).astype(jnp.bfloat16).reshape(NM, 32, HEAD)
+def total_kernel(own, other, *refs):
+    total = add(own[0], other[0], *(r[...] for r in refs[:-1]))
+    refs[-1][...] = total.astype(jnp.bfloat16).reshape(NM, 32, HEAD)
 
 
 def total(*parts):
     return pl.pallas_call(
         total_kernel,
         out_shape=jax.ShapeDtypeStruct((NM, 32, HEAD), jnp.bfloat16),
-        in_specs=[VM] * 4,
+        in_specs=[VM] * 6,
         out_specs=VM,
         compiler_params=params(12),
         name="add_groups",
@@ -392,8 +463,9 @@
     )(hist, self_term, gate, tokens, w, where, count)
 
 
-def move(value, step):
-    return lax.ppermute(value, "z", [(i, (i + step) % NZ) for i in range(NZ)])
+def move(value, step, width=1):
+    pairs = [(i, (i + (-step if i // width % 2 else step)) % NZ) for i in range(NZ)]
+    return lax.ppermute(value, "z", pairs)
 
 
 def swap(value):
@@ -432,20 +504,22 @@
     q_mine, packed = lax.optimization_barrier((q_mine, packed))
     kv = lax.all_to_all(packed, M, split_axis=0, concat_axis=0, tiled=True)
     mine = jnp.concatenate([q_mine.reshape(HALF, HEAD), mine], axis=0)
-    low, high = move(mine, 3), move(mine, -3)
-    up, down = bundle(mine, low, high)
-    q_own = stack(mine, low, high, move(up, 1), move(down, -1))
+    far_a, far_b = move(mine, 3), move(mine, -3)
+    out_a, out_b = bundle(where, mine, far_a, far_b)
+    q_own = stack(where, mine, far_a, far_b, move(out_a, 1), move(out_b, -1))
     q_other = swap(q_own)
     plan = table(where, q_own, q_other)
     gate, self_term, w2 = rest(tokens, in_weight, q, self_bias, out_weight)
     kv, gate, self_term, w2, plan = lax.optimization_barrier((kv, gate, self_term, w2, plan))
-    other, blocks = attend_other(plan, where, position_bias, q_other, kv)
+    own, other, blocks = attend_first(plan, where, position_bias, q_own, q_other, kv)
     other = swap(other)
-    own = attend_own(plan, where, position_bias, q_own, blocks)
-    up, down, across = far(own, other)
-    across = move(across, 4)
-    here, up, down = near(own, other, move(up, 1), move(down, -1))
-    hist = total(here, across, move(up, 2), move(down, -2))
+    own = attend_second(plan, where, position_bias, q_own, blocks, own)
+    out_a, out_b, half_a, half_b = far(where, own, other)
+    side_a, side_b = side(where, own, other, out_a)
+    side_a, side_b = move(side_a, 1), move(side_b, -1)
+    half_a, half_b = move(half_a, 2, 2), move(half_b, -2, 2)
+    out_a, out_b = near(where, own, other, move(out_a, 1), move(out_b, -1), half_a, half_b)
+    hist = total(own, other, side_a, side_b, move(out_a, 2, 2), move(out_b, -2, 2))
     hist = lax.all_to_all(hist, M, split_axis=0, concat_axis=0, tiled=True)
     return tail(hist, self_term, gate, tokens, w2, where, candidate_count)
 

time: 125 us -> 122 us (0.976)
  the two profiles are of different devices: /device:TPU:32 before, /device:TPU:2 now
where the time goes in v4:
time: 122 us; the launch traced here: 121 us
  starting transfers between devices  50.2 us (41%)
  waiting for transfers between devices  37.5 us (31%)
  Pallas kernels  27.4 us (22%)
  local copies, waits for them, and re-layouts  3.74 us (3%)
  between operations  1.62 us (1%)
    ppermute x12, starting transfers between devices, move(): return lax.ppermute(value, 'z', pairs)  28.9 us
    ppermute x12, waiting for transfers between devices, move(): return lax.ppermute(value, 'z', pairs)  24 us
    all_to_all x1, starting transfers between devices, local(): hist = lax.all_to_all(hist, M, split_axis=0, concat_axis=0, tiled=True)  7.84 us
    all_to_all x1, starting transfers between devices, local(): q_mine = lax.all_to_all(q_send, M, split_axis=0, concat_axis=0, tiled=True)  7.49 us
    pallas_call x1, Pallas kernels, attend_first(): pl.pallas_call(first_kernel, out_shape=(jax.ShapeDtypeStruct((NZ, HALF, H...  6.71 us
    pallas_call x1, Pallas kernels, rest(): pl.pallas_call(rest_kernel, out_shape=(jax.ShapeDtypeStruct((ROWS, D), jn...  6.12 us
    all_to_all x1, starting transfers between devices, local(): kv = lax.all_to_all(packed, M, split_axis=0, concat_axis=0, tiled=True)  5.8 us
    all_to_all x1, waiting for transfers between devices, local(): hist = lax.all_to_all(hist, M, split_axis=0, concat_axis=0, tiled=True)  5.74 us
  transfers between devices with their start and end apart: 17, of which 11 were waited for; matrix products, arithmetic and copies ran while one was open for 0% of the time, Pallas kernels for 12%

profile of v4, /device:TPU:2, one launch (start us, length us, event | category | flops | bytes accessed | tf_op | source)
XLA Modules:
  0.0 120.6 jit_solution(7655636350112603491)
XLA Ops:
  0.0 3.1 %project_query.1 = (bf16[64,1024]{1,0:T(8,128)(2,1)S(1)}, bf16[16,32,128]{2,1,0:T(8,128)(2,1)}) custom-call(bf16[64,1024]{1,0:T(8,128)(2,1)} %tokens.5, bf16[1024,4096]{1,0:T(8,128)(2,1)} %w.3), custom_call_target="tpu_custom_call" | custom-call | tf_op jit(solution)/shard_map/project_query/pallas_call | solution.py:88
  3.1 7.5 %all-to-all-start = ((bf16[16,32,128]{2,1,0:T(8,128)(2,1)}), bf16[16,32,128]{2,1,0:T(8,128)(2,1)S(1)}, u32[]{:S(2)}, u32[]{:S(2)}) async-start(bf16[16,32,128]{2,1,0:T(8,128)(2,1)} %get-tuple-element.30), calls=%async_computation | async-start | bytes 262144 | tf_op jit(solution)/shard_map/all_to_all | solution.py:502
  10.6 0.5 pack_history.1
  11.1 1.8 %copy-done = bf16[16,2,14,32,128]{4,3,2,1,0:T(8,128)(2,1)} copy-done((bf16[16,2,14,32,128]{4,3,2,1,0:T(8,128)(2,1)}, bf16[16,2,14,32,128]{4,3,2,1,0:T(8,128)(2,1)S(1)}, u32[]{:S(2)}) %copy-start) | copy-done | bytes 3670040
  12.9 4.0 %all-to-all-done = bf16[16,32,128]{2,1,0:T(8,128)(2,1)S(1)} async-done(((bf16[16,32,128]{2,1,0:T(8,128)(2,1)}), bf16[16,32,128]{2,1,0:T(8,128)(2,1)S(1)}, u32[]{:S(2)}, u32[]{:S(2)}) %all-to-all-start) | async-done | bytes 131104 | tf_op jit(solution)/shard_map/all_to_all | solution.py:502
  17.0 5.8 %all-to-all-start.1 = ((bf16[16,2,14,32,128]{4,3,2,1,0:T(8,128)(2,1)}), bf16[16,2,14,32,128]{4,3,2,1,0:T(8,128)(2,1)}, u32[]{:S(2)}, u32[]{:S(2)}) async-start(bf16[16,2,14,32,128]{4,3,2,1,0:T(8,128)(2,1)} %copy-done), calls=%async_computation.1 | async-start | bytes 7340032 | tf_op jit(solution)/shard_map/all_to_all | solution.py:505
  23.5 0.1 copy.13
  23.6 0.1 concatenate.20
  23.7 0.1 copy.14
  23.8 0.1 concatenate.21
  24.0 0.1 concatenate.24
  24.1 4.7 %collective-permute-start = (bf16[528,128]{1,0:T(8,128)(2,1)S(1)}, bf16[528,128]{1,0:T(8,128)(2,1)S(1)}, u32[]{:S(2)}, u32[]{:S(2)}) collective-permute-start(bf16[528,128]{1,0:T(8,128)(2,1)S(1)} %pad_maximum_fusion.own), channel_id=1, source_target_pairs={{0,96},{32,192},{64,160},{96,0},{128,224},{160,64},{192,32},{224,1... | collective-permute-start | bytes 405512 | tf_op jit(solution)/shard_map/ppermute | solution.py:468
  28.8 2.2 %collective-permute-start.1 = (bf16[528,128]{1,0:T(8,128)(2,1)S(1)}, bf16[528,128]{1,0:T(8,128)(2,1)S(1)}, u32[]{:S(2)}, u32[]{:S(2)}) collective-permute-start(bf16[528,128]{1,0:T(8,128)(2,1)S(1)} %pad_maximum_fusion.own), channel_id=1, source_target_pairs={{0,160},{32,128},{64,224},{96,192},{128,32},{160,0},{192,96},{224,... | collective-permute-start | bytes 405512 | tf_op jit(solution)/shard_map/ppermute | solution.py:468
  31.0 0.1 pad_add_fusion.where
  31.1 2.2 %collective-permute-done.far_a = bf16[528,128]{1,0:T(8,128)(2,1)S(1)} collective-permute-done((bf16[528,128]{1,0:T(8,128)(2,1)S(1)}, bf16[528,128]{1,0:T(8,128)(2,1)S(1)}, u32[]{:S(2)}, u32[]{:S(2)}) %collective-permute-start) | collective-permute-done | bytes 135200 | tf_op jit(solution)/shard_map/ppermute | solution.py:468
  33.3 6.8 %collective-permute-done.1.far_b = bf16[528,128]{1,0:T(8,128)(2,1)S(1)} collective-permute-done((bf16[528,128]{1,0:T(8,128)(2,1)S(1)}, bf16[528,128]{1,0:T(8,128)(2,1)S(1)}, u32[]{:S(2)}, u32[]{:S(2)}) %collective-permute-start.1) | collective-permute-done | bytes 135200 | tf_op jit(solution)/shard_map/ppermute | solution.py:468
  40.1 0.6 bundle_queries.1
  40.7 1.6 %collective-permute-start.2 = (bf16[1328,128]{1,0:T(8,128)(2,1)S(1)}, bf16[1328,128]{1,0:T(8,128)(2,1)S(1)}, u32[]{:S(2)}, u32[]{:S(2)}) collective-permute-start(bf16[1328,128]{1,0:T(8,128)(2,1)S(1)} %get-tuple-element.37), channel_id=1, source_target_pairs={{0,32},{32,0},{64,96},{96,64},{128,160},{160,128},{192,224},{224,1... | collective-permute-start | bytes 1019912 | tf_op jit(solution)/shard_map/ppermute | solution.py:468
  42.3 2.2 %collective-permute-start.3 = (bf16[1328,128]{1,0:T(8,128)(2,1)S(1)}, bf16[1328,128]{1,0:T(8,128)(2,1)S(1)}, u32[]{:S(2)}, u32[]{:S(2)}) collective-permute-start(bf16[1328,128]{1,0:T(8,128)(2,1)S(1)} %get-tuple-element.38), channel_id=1, source_target_pairs={{0,224},{32,64},{64,32},{96,128},{128,96},{160,192},{192,160},{224... | collective-permute-start | bytes 1019912 | tf_op jit(solution)/shard_map/ppermute | solution.py:468
  44.4 6.0 %collective-permute-done.2.near_a = bf16[1328,128]{1,0:T(8,128)(2,1)S(1)} collective-permute-done((bf16[1328,128]{1,0:T(8,128)(2,1)S(1)}, bf16[1328,128]{1,0:T(8,128)(2,1)S(1)}, u32[]{:S(2)}, u32[]{:S(2)}) %collective-permute-start.2) | collective-permute-done | bytes 340000 | tf_op jit(solution)/shard_map/ppermute | solution.py:468
  50.4 2.7 %collective-permute-done.3.near_b = bf16[1328,128]{1,0:T(8,128)(2,1)S(1)} collective-permute-done((bf16[1328,128]{1,0:T(8,128)(2,1)S(1)}, bf16[1328,128]{1,0:T(8,128)(2,1)S(1)}, u32[]{:S(2)}, u32[]{:S(2)}) %collective-permute-start.3) | collective-permute-done | bytes 340000 | tf_op jit(solution)/shard_map/ppermute | solution.py:468
  53.1 0.6 stack_queries.1.q_own.q
  53.7 0.1 collective-permute-start.4
  53.9 6.1 %project_rest.1 = (bf16[64,1024]{1,0:T(8,128)(2,1)S(1)}, f32[64,1024]{1,0:T(8,128)S(1)}, bf16[1024,1024]{1,0:T(8,128)(2,1)S(1)}) custom-call(bf16[64,1024]{1,0:T(8,128)(2,1)S(1)} %copy-done.4, bf16[1024,4096]{1,0:T(8,128)(2,1)} %w.3, bf16[64,1024]{1,0:T(8,128)(2,1)S(1)} %get-tuple-element.31.after.q, f32[8]{0:T(128)S(1)} %copy-done.6, bf16[1024,1024]{1,0:T(8,128)(2,1)} %w2.1), custom_call_target="tpu_custom_call" | custom-call | tf_op jit(solution)/shard_map/project_rest/pallas_call | solution.py:138
  60.0 1.4 %copy-done.1 = bf16[1024,1024]{1,0:T(8,128)(2,1)} copy-done((bf16[1024,1024]{1,0:T(8,128)(2,1)}, bf16[1024,1024]{1,0:T(8,128)(2,1)S(1)}, u32[]{:S(2)}) %copy-start.1) | copy-done | bytes 2097176
  61.4 2.3 %read_tables.1.plan = s32[4,16]{1,0:T(4,128)S(1)} custom-call(s32[4]{0:T(128)S(1)} %pad_add_fusion.where, bf16[8,528,128]{2,1,0:T(8,128)(2,1)S(1)} %stack_queries.1.q_own.q, bf16[8,528,128]{2,1,0:T(8,128)(2,1)S(1)} %collective-permute-done.4.q_other), custom_call_target="tpu_custom_call" | custom-call | tf_op jit(solution)/shard_map/read_tables/pallas_call | solution.py:264
  63.7 3.7 %all-to-all-done.1.kv = bf16[16,2,14,32,128]{4,3,2,1,0:T(8,128)(2,1)} async-done(((bf16[16,2,14,32,128]{4,3,2,1,0:T(8,128)(2,1)}), bf16[16,2,14,32,128]{4,3,2,1,0:T(8,128)(2,1)}, u32[]{:S(2)}, u32[]{:S(2)}) %all-to-all-start.1) | async-done | bytes 3670048 | tf_op jit(solution)/shard_map/all_to_all | solution.py:505
  67.3 6.7 %attend_first.1 = (f32[8,512,128]{2,1,0:T(8,128)S(1)}, bf16[8,512,128]{2,1,0:T(8,128)(2,1)S(1)}, bf16[14,16,2,32,128]{4,3,2,1,0:T(8,128)(2,1)S(1)}) custom-call(s32[4,16]{1,0:T(4,128)S(1)} %read_tables.1.plan, s32[4]{0:T(128)S(1)} %pad_add_fusion.where, f32[8,14]{1,0:T(8,128)S(1)} %copy-done.5, bf16[8,528,128]{2,1,0:T(8,128)(2,1)S(1)} %stack_queries.1.q_own.q, ...), custom_call_target="tpu_custom_call" | custom-call | tf_op jit(solution)/shard_map/attend_first/pallas_call | solution.py:320
  74.1 0.1 collective-permute-start.5
  74.2 2.9 %attend_second.1.a.own = bf16[8,512,128]{2,1,0:T(8,128)(2,1)S(1)} custom-call(s32[4,16]{1,0:T(4,128)S(1)} %read_tables.1.plan, s32[4]{0:T(128)S(1)} %pad_add_fusion.where, f32[8,14]{1,0:T(8,128)S(1)} %copy-done.5, bf16[8,528,128]{2,1,0:T(8,128)(2,1)S(1)} %stack_queries.1.q_own.q, bf16[14,16,2,32,128]{4,3,2,1,0:T(8,128)(2,1)S(1)} %get-tuple-element.41.blocks, ...), custom_call_target="tpu_custom_call" | custom-call | tf_op jit(solution)/shard_map/attend_second/pallas_call | solution.py:336
  77.1 0.7 add_far.1
  77.8 1.9 %collective-permute-start.8 = (bf16[512,128]{1,0:T(8,128)(2,1)S(1)}, bf16[512,128]{1,0:T(8,128)(2,1)S(1)}, u32[]{:S(2)}, u32[]{:S(2)}) collective-permute-start(bf16[512,128]{1,0:T(8,128)(2,1)S(1)} %get-tuple-element.44.after), channel_id=1, source_target_pairs={{0,32},{32,0},{64,96},{96,64},{128,160},{160,128},{192,224},{224,1... | collective-permute-start | bytes 393224 | tf_op jit(solution)/shard_map/ppermute | solution.py:468
  79.7 4.9 %collective-permute-start.9 = (bf16[512,128]{1,0:T(8,128)(2,1)S(1)}, bf16[512,128]{1,0:T(8,128)(2,1)S(1)}, u32[]{:S(2)}, u32[]{:S(2)}) collective-permute-start(bf16[512,128]{1,0:T(8,128)(2,1)S(1)} %get-tuple-element.47), channel_id=1, source_target_pairs={{0,224},{32,64},{64,32},{96,128},{128,96},{160,192},{192,160},{224... | collective-permute-start | bytes 393224 | tf_op jit(solution)/shard_map/ppermute | solution.py:468
  84.7 1.9 %collective-permute-start.11 = (bf16[256,128]{1,0:T(8,128)(2,1)S(1)}, bf16[256,128]{1,0:T(8,128)(2,1)S(1)}, u32[]{:S(2)}, u32[]{:S(2)}) collective-permute-start(bf16[256,128]{1,0:T(8,128)(2,1)S(1)} %get-tuple-element.49), channel_id=1, source_target_pairs={{0,192},{32,224},{64,128},{96,160},{128,64},{160,96},{192,0},{224,... | collective-permute-start | bytes 196616 | tf_op jit(solution)/shard_map/ppermute | solution.py:468
  86.6 0.6 add_side.1
  87.2 2.6 %collective-permute-start.6 = (bf16[512,128]{1,0:T(8,128)(2,1)S(1)}, bf16[512,128]{1,0:T(8,128)(2,1)S(1)}, u32[]{:S(2)}, u32[]{:S(2)}) collective-permute-start(bf16[512,128]{1,0:T(8,128)(2,1)S(1)} %get-tuple-element.45), channel_id=1, source_target_pairs={{0,32},{32,0},{64,96},{96,64},{128,160},{160,128},{192,224},{224,1... | collective-permute-start | bytes 393224 | tf_op jit(solution)/shard_map/ppermute | solution.py:468
  89.8 0.5 collective-permute-done.10.half_a
  90.3 3.9 %collective-permute-start.7 = (bf16[512,128]{1,0:T(8,128)(2,1)S(1)}, bf16[512,128]{1,0:T(8,128)(2,1)S(1)}, u32[]{:S(2)}, u32[]{:S(2)}) collective-permute-start(bf16[512,128]{1,0:T(8,128)(2,1)S(1)} %get-tuple-element.46), channel_id=1, source_target_pairs={{0,224},{32,64},{64,32},{96,128},{128,96},{160,192},{192,160},{224... | collective-permute-start | bytes 393224 | tf_op jit(solution)/shard_map/ppermute | solution.py:468
  94.2 0.7 add_near.1
  94.9 0.1 collective-permute-start.12
  95.0 2.8 %collective-permute-start.13 = (bf16[512,128]{1,0:T(8,128)(2,1)S(1)}, bf16[512,128]{1,0:T(8,128)(2,1)S(1)}, u32[]{:S(2)}, u32[]{:S(2)}) collective-permute-start(bf16[512,128]{1,0:T(8,128)(2,1)S(1)} %get-tuple-element.51), channel_id=1, source_target_pairs={{0,192},{32,224},{64,128},{96,160},{128,64},{160,96},{192,0},{224,... | collective-permute-start | bytes 393224 | tf_op jit(solution)/shard_map/ppermute | solution.py:468
  97.8 1.8 %collective-permute-done.7.refs_1_ = bf16[512,128]{1,0:T(8,128)(2,1)S(1)} collective-permute-done((bf16[512,128]{1,0:T(8,128)(2,1)S(1)}, bf16[512,128]{1,0:T(8,128)(2,1)S(1)}, u32[]{:S(2)}, u32[]{:S(2)}) %collective-permute-start.7) | collective-permute-done | bytes 131104 | tf_op jit(solution)/shard_map/ppermute | solution.py:468
  99.6 3.1 %collective-permute-done.12.refs_2_ = bf16[512,128]{1,0:T(8,128)(2,1)S(1)} collective-permute-done((bf16[512,128]{1,0:T(8,128)(2,1)S(1)}, bf16[512,128]{1,0:T(8,128)(2,1)S(1)}, u32[]{:S(2)}, u32[]{:S(2)}) %collective-permute-start.12) | collective-permute-done | bytes 131104 | tf_op jit(solution)/shard_map/ppermute | solution.py:468
  102.7 1.0 collective-permute-done.13.refs_3_
  103.7 0.8 add_groups.1
  104.5 7.8 %all-to-all-start.2 = ((bf16[16,32,128]{2,1,0:T(8,128)(2,1)}), bf16[16,32,128]{2,1,0:T(8,128)(2,1)S(1)}, u32[]{:S(2)}, u32[]{:S(2)}) async-start(bf16[16,32,128]{2,1,0:T(8,128)(2,1)} %add_groups.1), calls=%async_computation.2 | async-start | bytes 262144 | tf_op jit(solution)/shard_map/all_to_all | solution.py:523
  113.0 5.7 %all-to-all-done.2.hist = bf16[16,32,128]{2,1,0:T(8,128)(2,1)S(1)} async-done(((bf16[16,32,128]{2,1,0:T(8,128)(2,1)}), bf16[16,32,128]{2,1,0:T(8,128)(2,1)S(1)}, u32[]{:S(2)}, u32[]{:S(2)}) %all-to-all-start.2) | async-done | bytes 131104 | tf_op jit(solution)/shard_map/all_to_all | solution.py:523
  118.7 1.9 %output.1 = bf16[64,1024]{1,0:T(8,128)(2,1)} custom-call(bf16[16,32,128]{2,1,0:T(8,128)(2,1)S(1)} %all-to-all-done.2.hist, f32[64,1024]{1,0:T(8,128)S(1)} %get-tuple-element.52.self_term, bf16[64,1024]{1,0:T(8,128)(2,1)S(1)} %get-tuple-element.53.gate, bf16[64,1024]{1,0:T(8,128)(2,1)S(1)} %copy-done.4, bf16[1024,1024]{1,0:T(8,128)(2,1)S(1)} %copy-done.2, ...), custom_call_target="tpu_custom_call" | custom-call | tf_op jit(solution)/shard_map/output/pallas_call | solution.py:456
  (28 shorter events, 0.1 us)
Async XLA Ops:
  0.0 10.6 %copy-start.3 = (bf16[14,32,2048]{2,1,0:T(8,128)(2,1)S(1)}, bf16[14,32,2048]{2,1,0:T(8,128)(2,1)}, u32[]{:S(2)}) copy-start(bf16[14,32,2048]{2,1,0:T(8,128)(2,1)} %pool.1) | copy-start | bytes 5505028
  3.1 13.9 %all-to-all-start = ((bf16[16,32,128]{2,1,0:T(8,128)(2,1)}), bf16[16,32,128]{2,1,0:T(8,128)(2,1)S(1)}, u32[]{:S(2)}, u32[]{:S(2)}) async-start(bf16[16,32,128]{2,1,0:T(8,128)(2,1)} %get-tuple-element.30), calls=%async_computation | async-start | bytes 262144 | tf_op jit(solution)/shard_map/all_to_all | solution.py:502
  11.1 1.8 %copy-start = (bf16[16,2,14,32,128]{4,3,2,1,0:T(8,128)(2,1)}, bf16[16,2,14,32,128]{4,3,2,1,0:T(8,128)(2,1)S(1)}, u32[]{:S(2)}) copy-start(bf16[16,2,14,32,128]{4,3,2,1,0:T(8,128)(2,1)S(1)} %pack_history.1) | copy-start | bytes 11010052
  12.9 10.6 %copy-start.7 = (s32[1,16,2]{1,2,0:T(2,128)S(1)}, s32[1,16,2]{1,2,0:T(2,128)}, u32[]{:S(2)}) copy-start(s32[1,16,2]{1,2,0:T(2,128)} %param.18) | copy-start | bytes 388
  12.9 10.8 %copy-start.8 = (s32[1,16,2]{1,2,0:T(2,128)S(1)}, s32[1,16,2]{1,2,0:T(2,128)}, u32[]{:S(2)}) copy-start(s32[1,16,2]{1,2,0:T(2,128)} %param.19) | copy-start | bytes 388
  17.0 50.4 %all-to-all-start.1 = ((bf16[16,2,14,32,128]{4,3,2,1,0:T(8,128)(2,1)}), bf16[16,2,14,32,128]{4,3,2,1,0:T(8,128)(2,1)}, u32[]{:S(2)}, u32[]{:S(2)}) async-start(bf16[16,2,14,32,128]{4,3,2,1,0:T(8,128)(2,1)} %copy-done), calls=%async_computation.1 | async-start | bytes 7340032 | tf_op jit(solution)/shard_map/all_to_all | solution.py:505
  22.8 31.1 %copy-start.4 = (bf16[64,1024]{1,0:T(8,128)(2,1)S(1)}, bf16[64,1024]{1,0:T(8,128)(2,1)}, u32[]{:S(2)}) copy-start(bf16[64,1024]{1,0:T(8,128)(2,1)} %tokens.5) | copy-start | bytes 393220
  22.8 31.1 %copy-start.6 = (f32[8]{0:T(128)S(1)}, f32[8]{0:T(128)}, u32[]{:S(2)}) copy-start(f32[8]{0:T(128)} %self_bias.1) | copy-start | bytes 100
  24.1 9.2 %collective-permute-start = (bf16[528,128]{1,0:T(8,128)(2,1)S(1)}, bf16[528,128]{1,0:T(8,128)(2,1)S(1)}, u32[]{:S(2)}, u32[]{:S(2)}) collective-permute-start(bf16[528,128]{1,0:T(8,128)(2,1)S(1)} %pad_maximum_fusion.own), channel_id=1, source_target_pairs={{0,96},{32,192},{64,160},{96,0},{128,224},{160,64},{192,32},{224,1... | collective-permute-start | bytes 405512 | tf_op jit(solution)/shard_map/ppermute | solution.py:468
  28.8 11.3 %collective-permute-start.1 = (bf16[528,128]{1,0:T(8,128)(2,1)S(1)}, bf16[528,128]{1,0:T(8,128)(2,1)S(1)}, u32[]{:S(2)}, u32[]{:S(2)}) collective-permute-start(bf16[528,128]{1,0:T(8,128)(2,1)S(1)} %pad_maximum_fusion.own), channel_id=1, source_target_pairs={{0,160},{32,128},{64,224},{96,192},{128,32},{160,0},{192,96},{224,... | collective-permute-start | bytes 405512 | tf_op jit(solution)/shard_map/ppermute | solution.py:468
  40.7 9.7 %collective-permute-start.2 = (bf16[1328,128]{1,0:T(8,128)(2,1)S(1)}, bf16[1328,128]{1,0:T(8,128)(2,1)S(1)}, u32[]{:S(2)}, u32[]{:S(2)}) collective-permute-start(bf16[1328,128]{1,0:T(8,128)(2,1)S(1)} %get-tuple-element.37), channel_id=1, source_target_pairs={{0,32},{32,0},{64,96},{96,64},{128,160},{160,128},{192,224},{224,1... | collective-permute-start | bytes 1019912 | tf_op jit(solution)/shard_map/ppermute | solution.py:468
  42.3 10.8 %collective-permute-start.3 = (bf16[1328,128]{1,0:T(8,128)(2,1)S(1)}, bf16[1328,128]{1,0:T(8,128)(2,1)S(1)}, u32[]{:S(2)}, u32[]{:S(2)}) collective-permute-start(bf16[1328,128]{1,0:T(8,128)(2,1)S(1)} %get-tuple-element.38), channel_id=1, source_target_pairs={{0,224},{32,64},{64,32},{96,128},{128,96},{160,192},{192,160},{224... | collective-permute-start | bytes 1019912 | tf_op jit(solution)/shard_map/ppermute | solution.py:468
  53.7 7.7 %collective-permute-start.4 = (bf16[8,528,128]{2,1,0:T(8,128)(2,1)S(1)}, bf16[8,528,128]{2,1,0:T(8,128)(2,1)S(1)}, u32[]{:S(2)}, u32[]{:S(2)}) collective-permute-start(bf16[8,528,128]{2,1,0:T(8,128)(2,1)S(1)} %stack_queries.1.q_own.q), channel_id=1, source_target_pairs={{0,16},{16,0},{1,17},{17,1},{2,18},{18,2},{3,19},{19,3},{4,20},{20... | collective-permute-start | bytes 3244040 | tf_op jit(solution)/shard_map/ppermute | solution.py:472
  60.0 1.4 %copy-start.1 = (bf16[1024,1024]{1,0:T(8,128)(2,1)}, bf16[1024,1024]{1,0:T(8,128)(2,1)S(1)}, u32[]{:S(2)}) copy-start(bf16[1024,1024]{1,0:T(8,128)(2,1)S(1)} %get-tuple-element.54.w) | copy-start | bytes 6291460
  61.4 5.9 %copy-start.5 = (f32[8,14]{1,0:T(8,128)S(1)}, f32[8,14]{1,0:T(8,128)}, u32[]{:S(2)}) copy-start(f32[8,14]{1,0:T(8,128)} %bias.3) | copy-start | bytes 1348
  74.1 3.0 %collective-permute-start.5 = (bf16[8,512,128]{2,1,0:T(8,128)(2,1)S(1)}, bf16[8,512,128]{2,1,0:T(8,128)(2,1)S(1)}, u32[]{:S(2)}, u32[]{:S(2)}) collective-permute-start(bf16[8,512,128]{2,1,0:T(8,128)(2,1)S(1)} %get-tuple-element.43), channel_id=1, source_target_pairs={{0,16},{16,0},{1,17},{17,1},{2,18},{18,2},{3,19},{19,3},{4,20},{20... | collective-permute-start | bytes 3145736 | tf_op jit(solution)/shard_map/ppermute | solution.py:472
  77.8 16.4 %collective-permute-start.8 = (bf16[512,128]{1,0:T(8,128)(2,1)S(1)}, bf16[512,128]{1,0:T(8,128)(2,1)S(1)}, u32[]{:S(2)}, u32[]{:S(2)}) collective-permute-start(bf16[512,128]{1,0:T(8,128)(2,1)S(1)} %get-tuple-element.44.after), channel_id=1, source_target_pairs={{0,32},{32,0},{64,96},{96,64},{128,160},{160,128},{192,224},{224,1... | collective-permute-start | bytes 393224 | tf_op jit(solution)/shard_map/ppermute | solution.py:468
  79.7 14.4 %collective-permute-start.9 = (bf16[512,128]{1,0:T(8,128)(2,1)S(1)}, bf16[512,128]{1,0:T(8,128)(2,1)S(1)}, u32[]{:S(2)}, u32[]{:S(2)}) collective-permute-start(bf16[512,128]{1,0:T(8,128)(2,1)S(1)} %get-tuple-element.47), channel_id=1, source_target_pairs={{0,224},{32,64},{64,32},{96,128},{128,96},{160,192},{192,160},{224... | collective-permute-start | bytes 393224 | tf_op jit(solution)/shard_map/ppermute | solution.py:468
  84.7 5.6 %collective-permute-start.10 = (bf16[256,128]{1,0:T(8,128)(2,1)S(1)}, bf16[256,128]{1,0:T(8,128)(2,1)S(1)}, u32[]{:S(2)}, u32[]{:S(2)}) collective-permute-start(bf16[256,128]{1,0:T(8,128)(2,1)S(1)} %get-tuple-element.48), channel_id=1, source_target_pairs={{0,64},{32,96},{64,0},{96,32},{128,192},{160,224},{192,128},{224,1... | collective-permute-start | bytes 196616 | tf_op jit(solution)/shard_map/ppermute | solution.py:468
  84.7 9.5 %collective-permute-start.11 = (bf16[256,128]{1,0:T(8,128)(2,1)S(1)}, bf16[256,128]{1,0:T(8,128)(2,1)S(1)}, u32[]{:S(2)}, u32[]{:S(2)}) collective-permute-start(bf16[256,128]{1,0:T(8,128)(2,1)S(1)} %get-tuple-element.49), channel_id=1, source_target_pairs={{0,192},{32,224},{64,128},{96,160},{128,64},{160,96},{192,0},{224,... | collective-permute-start | bytes 196616 | tf_op jit(solution)/shard_map/ppermute | solution.py:468
  87.2 10.6 %collective-permute-start.6 = (bf16[512,128]{1,0:T(8,128)(2,1)S(1)}, bf16[512,128]{1,0:T(8,128)(2,1)S(1)}, u32[]{:S(2)}, u32[]{:S(2)}) collective-permute-start(bf16[512,128]{1,0:T(8,128)(2,1)S(1)} %get-tuple-element.45), channel_id=1, source_target_pairs={{0,32},{32,0},{64,96},{96,64},{128,160},{160,128},{192,224},{224,1... | collective-permute-start | bytes 393224 | tf_op jit(solution)/shard_map/ppermute | solution.py:468
  90.3 9.4 %collective-permute-start.7 = (bf16[512,128]{1,0:T(8,128)(2,1)S(1)}, bf16[512,128]{1,0:T(8,128)(2,1)S(1)}, u32[]{:S(2)}, u32[]{:S(2)}) collective-permute-start(bf16[512,128]{1,0:T(8,128)(2,1)S(1)} %get-tuple-element.46), channel_id=1, source_target_pairs={{0,224},{32,64},{64,32},{96,128},{128,96},{160,192},{192,160},{224... | collective-permute-start | bytes 393224 | tf_op jit(solution)/shard_map/ppermute | solution.py:468
  94.9 23.8 %copy-start.2 = (bf16[1024,1024]{1,0:T(8,128)(2,1)S(1)}, bf16[1024,1024]{1,0:T(8,128)(2,1)}, u32[]{:S(2)}) copy-start(bf16[1024,1024]{1,0:T(8,128)(2,1)} %copy-done.1) | copy-start | bytes 6291460
  94.9 7.9 %collective-permute-start.12 = (bf16[512,128]{1,0:T(8,128)(2,1)S(1)}, bf16[512,128]{1,0:T(8,128)(2,1)S(1)}, u32[]{:S(2)}, u32[]{:S(2)}) collective-permute-start(bf16[512,128]{1,0:T(8,128)(2,1)S(1)} %get-tuple-element.50), channel_id=1, source_target_pairs={{0,64},{32,96},{64,0},{96,32},{128,192},{160,224},{192,128},{224,1... | collective-permute-start | bytes 393224 | tf_op jit(solution)/shard_map/ppermute | solution.py:468
  95.0 8.7 %collective-permute-start.13 = (bf16[512,128]{1,0:T(8,128)(2,1)S(1)}, bf16[512,128]{1,0:T(8,128)(2,1)S(1)}, u32[]{:S(2)}, u32[]{:S(2)}) collective-permute-start(bf16[512,128]{1,0:T(8,128)(2,1)S(1)} %get-tuple-element.51), channel_id=1, source_target_pairs={{0,192},{32,224},{64,128},{96,160},{128,64},{160,96},{192,0},{224,... | collective-permute-start | bytes 393224 | tf_op jit(solution)/shard_map/ppermute | solution.py:468
  104.5 14.2 %all-to-all-start.2 = ((bf16[16,32,128]{2,1,0:T(8,128)(2,1)}), bf16[16,32,128]{2,1,0:T(8,128)(2,1)S(1)}, u32[]{:S(2)}, u32[]{:S(2)}) async-start(bf16[16,32,128]{2,1,0:T(8,128)(2,1)} %add_groups.1), calls=%async_computation.2 | async-start | bytes 262144 | tf_op jit(solution)/shard_map/all_to_all | solution.py:523

commit v5 on v4

--- a/solution.py
+++ b/solution.py
@@ -25,7 +25,8 @@
 EPS = 1e-05
 SCALE = HEAD**-0.5
 G = ("z", "core")
-M = ("x", "y")
+M = ("half", "pair", "y")
+W = ("pair", "y")
 VM = pl.BlockSpec(memory_space=pltpu.VMEM)
 SM = pl.BlockSpec(memory_space=pltpu.SMEM)
 HB = pl.BlockSpec(memory_space=pltpu.HBM)
@@ -51,7 +52,7 @@
         for kv in range(2):
             cols = pool[:, :, kv * D + h * HEAD : kv * D + (h + 1) * HEAD]
             for ch in range(2):
-                out[h * 2 + ch, kv] = cols
+                out[ch * HEADS + h, kv] = cols
 
 
 def pack(pool, after):
@@ -80,8 +81,7 @@
         q = silu(jnp.dot(normed, buf[i], preferred_element_type=jnp.float32)).astype(jnp.bfloat16)
         q_out[:, i * 256 : (i + 1) * 256] = q
         for j in range(2):
-            for ch in range(2):
-                send_out[i * 4 + j * 2 + ch] = q[ch * 32 : ch * 32 + 32, j * HEAD : (j + 1) * HEAD]
+            send_out[i * 2 + j] = q[:, j * HEAD : (j + 1) * HEAD]
 
 
 def query(tokens, w):
@@ -89,7 +89,7 @@
         query_kernel,
         out_shape=(
             jax.ShapeDtypeStruct((ROWS, D), jnp.bfloat16),
-            jax.ShapeDtypeStruct((NM, 32, HEAD), jnp.bfloat16),
+            jax.ShapeDtypeStruct((HEADS, ROWS, HEAD), jnp.bfloat16),
         ),
         in_specs=[HB, HB],
         out_specs=(VM, VM),
@@ -427,13 +427,13 @@
 
 def total_kernel(own, other, *refs):
     total = add(own[0], other[0], *(r[...] for r in refs[:-1]))
-    refs[-1][...] = total.astype(jnp.bfloat16).reshape(NM, 32, HEAD)
+    refs[-1][...] = total.astype(jnp.bfloat16).reshape(HEADS, ROWS, HEAD)
 
 
 def total(*parts):
     return pl.pallas_call(
         total_kernel,
-        out_shape=jax.ShapeDtypeStruct((NM, 32, HEAD), jnp.bfloat16),
+        out_shape=jax.ShapeDtypeStruct((HEADS, ROWS, HEAD), jnp.bfloat16),
         in_specs=[VM] * 6,
         out_specs=VM,
         compiler_params=params(12),
@@ -442,10 +442,7 @@
 
 
 def tail_kernel(hist, self_term, gate, tokens, w, where, count, out):
-    cols = []
-    for h in range(HEADS):
-        cols.append(jnp.concatenate([hist[h * 2], hist[h * 2 + 1]], axis=0))
-    attended = jnp.concatenate(cols, axis=1).astype(jnp.float32) + self_term[...]
+    attended = jnp.concatenate([hist[h] for h in range(HEADS)], axis=1).astype(jnp.float32) + self_term[...]
     gated = (norm(attended) * gate[...].astype(jnp.float32)).astype(jnp.bfloat16)
     res = jnp.dot(gated, w[...], preferred_element_type=jnp.float32) + tokens[...].astype(jnp.float32)
     row = where[3] * ROWS + lax.broadcasted_iota(jnp.int32, (ROWS, D), 0)
@@ -485,7 +482,7 @@
     block_position,
 ):
     z, core, m = lax.axis_index("z"), lax.axis_index("core"), lax.axis_index(M)
-    where = jnp.stack([z, core, m // 2, m]).astype(jnp.int32)
+    where = jnp.stack([z, core, m % HEADS, m]).astype(jnp.int32)
     length = history_length[:, None]
     mine = jnp.concatenate(
         [
@@ -499,7 +496,7 @@
     ).astype(jnp.bfloat16)
     mine = jnp.broadcast_to(mine, (16, 128))
     q, q_send = query(tokens, in_weight)
-    q_mine = lax.all_to_all(q_send, M, split_axis=0, concat_axis=0, tiled=True)
+    q_mine = lax.all_to_all(q_send, W, split_axis=0, concat_axis=0, tiled=True)
     packed = pack(history_pool, q)
     q_mine, packed = lax.optimization_barrier((q_mine, packed))
     kv = lax.all_to_all(packed, M, split_axis=0, concat_axis=0, tiled=True)
@@ -520,24 +517,25 @@
     half_a, half_b = move(half_a, 2, 2), move(half_b, -2, 2)
     out_a, out_b = near(where, own, other, move(out_a, 1), move(out_b, -1), half_a, half_b)
     hist = total(own, other, side_a, side_b, move(out_a, 2, 2), move(out_b, -2, 2))
-    hist = lax.all_to_all(hist, M, split_axis=0, concat_axis=0, tiled=True)
+    hist = lax.all_to_all(hist, W, split_axis=0, concat_axis=0, tiled=True)
     return tail(hist, self_term, gate, tokens, w2, where, candidate_count)
 
 
 def solution(mesh):
-    fine = Mesh(mesh.devices.reshape(NZ, 2, 4, 4), ("z", "core", "x", "y"))
+    names = ("z", "core", "half", "pair", "y")
+    fine = Mesh(mesh.devices.reshape(NZ, 2, 2, 2, 4), names)
     placed = (
-        P(("z", "core", "x", "y"), None),
+        P(names, None),
         P(),
         P(),
-        P(("z", "core"), ("x", "y"), None),
+        P(G, M, None),
         P(),
         P(),
-        P(("z", "core")),
-        P(("z", "core")),
-        P(("z", "core"), None, None),
-        P(("z", "core"), None, None),
+        P(G),
+        P(G),
+        P(G, None, None),
+        P(G, None, None),
     )
     return jax.shard_map(
-        local, mesh=fine, in_specs=placed, out_specs=P(("z", "core", "x", "y"), None), check_vma=False
+        local, mesh=fine, in_specs=placed, out_specs=P(names, None), check_vma=False
     )

time: 122 us -> 118 us (0.967)
  starting transfers between devices: 50.2 us -> 46.2 us
    ppermute x12, waiting for transfers between devices: 24 us -> 26.8 us  [move(): return lax.ppermute(value, 'z', pairs)]
    all_to_all x2, waiting for transfers between devices: 9.78 us -> 7.49 us  [the longest x1 4.6 us: local(): hist = lax.all_to_all(hist, W, split_axis=0, concat_axis=0, tiled=True)]
    all_to_all x2, starting transfers between devices: 15.3 us -> 13.2 us  [the longest x1 7.23 us: local(): hist = lax.all_to_all(hist, W, split_axis=0, concat_axis=0, tiled=True)]
    ppermute x12, starting transfers between devices: 28.9 us -> 26.9 us  [move(): return lax.ppermute(value, 'z', pairs)]
  transfers between devices with their start and end apart: 17 -> 17, of which waited for: 11 -> 11; matrix products, arithmetic and copies ran while one was open for 0% -> 1% of each run, Pallas kernels for 12% -> 13%
where the time goes in v5:
time: 118 us; the launch traced here: 117 us
  starting transfers between devices  46.2 us (39%)
  waiting for transfers between devices  37.8 us (32%)
  Pallas kernels  27.8 us (24%)
  local copies, waits for them, and re-layouts  3.74 us (3%)
  between operations  1.61 us (1%)
    ppermute x12, starting transfers between devices, move(): return lax.ppermute(value, 'z', pairs)  26.9 us
    ppermute x12, waiting for transfers between devices, move(): return lax.ppermute(value, 'z', pairs)  26.8 us
    all_to_all x1, starting transfers between devices, local(): hist = lax.all_to_all(hist, W, split_axis=0, concat_axis=0, tiled=True)  7.23 us
    pallas_call x1, Pallas kernels, attend_first(): pl.pallas_call(first_kernel, out_shape=(jax.ShapeDtypeStruct((NZ, HALF, H...  6.63 us
    pallas_call x1, Pallas kernels, rest(): pl.pallas_call(rest_kernel, out_shape=(jax.ShapeDtypeStruct((ROWS, D), jn...  6.12 us
    all_to_all x1, starting transfers between devices, local(): q_mine = lax.all_to_all(q_send, W, split_axis=0, concat_axis=0, tiled=True)  5.94 us
    all_to_all x1, starting transfers between devices, local(): kv = lax.all_to_all(packed, M, split_axis=0, concat_axis=0, tiled=True)  5.91 us
    all_to_all x1, waiting for transfers between devices, local(): hist = lax.all_to_all(hist, W, split_axis=0, concat_axis=0, tiled=True)  4.6 us
  transfers between devices with their start and end apart: 17, of which 11 were waited for; matrix products, arithmetic and copies ran while one was open for 1% of the time, Pallas kernels for 13%

profile of v5, /device:TPU:2, one launch (start us, length us, event | category | flops | bytes accessed | tf_op | source)
XLA Modules:
  0.0 117.3 jit_solution(6141389697541577795)
XLA Ops:
  0.0 3.1 %project_query.1 = (bf16[64,1024]{1,0:T(8,128)(2,1)S(1)}, bf16[8,64,128]{2,1,0:T(8,128)(2,1)}) custom-call(bf16[64,1024]{1,0:T(8,128)(2,1)} %tokens.5, bf16[1024,4096]{1,0:T(8,128)(2,1)} %w.3), custom_call_target="tpu_custom_call" | custom-call | tf_op jit(solution)/shard_map/project_query/pallas_call | solution.py:88
  3.1 5.9 %all-to-all-start = ((bf16[8,64,128]{2,1,0:T(8,128)(2,1)}), bf16[8,64,128]{2,1,0:T(8,128)(2,1)S(1)}, u32[]{:S(2)}, u32[]{:S(2)}) async-start(bf16[8,64,128]{2,1,0:T(8,128)(2,1)} %get-tuple-element.30), calls=%async_computation | async-start | bytes 262144 | tf_op jit(solution)/shard_map/all_to_all | solution.py:499
  9.0 0.5 pack_history.1
  9.6 1.8 %copy-done = bf16[16,2,14,32,128]{4,3,2,1,0:T(8,128)(2,1)} copy-done((bf16[16,2,14,32,128]{4,3,2,1,0:T(8,128)(2,1)}, bf16[16,2,14,32,128]{4,3,2,1,0:T(8,128)(2,1)S(1)}, u32[]{:S(2)}) %copy-start) | copy-done | bytes 3670040
  11.4 2.9 %all-to-all-done = bf16[8,64,128]{2,1,0:T(8,128)(2,1)S(1)} async-done(((bf16[8,64,128]{2,1,0:T(8,128)(2,1)}), bf16[8,64,128]{2,1,0:T(8,128)(2,1)S(1)}, u32[]{:S(2)}, u32[]{:S(2)}) %all-to-all-start) | async-done | bytes 131104 | tf_op jit(solution)/shard_map/all_to_all | solution.py:499
  14.3 5.9 %all-to-all-start.1 = ((bf16[16,2,14,32,128]{4,3,2,1,0:T(8,128)(2,1)}), bf16[16,2,14,32,128]{4,3,2,1,0:T(8,128)(2,1)}, u32[]{:S(2)}, u32[]{:S(2)}) async-start(bf16[16,2,14,32,128]{4,3,2,1,0:T(8,128)(2,1)} %copy-done), calls=%async_computation.1 | async-start | bytes 7340032 | tf_op jit(solution)/shard_map/all_to_all | solution.py:502
  20.9 0.1 copy.13
  21.0 0.1 concatenate.20
  21.2 0.1 copy.14
  21.3 0.1 concatenate.21
  21.4 0.1 concatenate.24
  21.5 4.7 %collective-permute-start = (bf16[528,128]{1,0:T(8,128)(2,1)S(1)}, bf16[528,128]{1,0:T(8,128)(2,1)S(1)}, u32[]{:S(2)}, u32[]{:S(2)}) collective-permute-start(bf16[528,128]{1,0:T(8,128)(2,1)S(1)} %pad_maximum_fusion.own), channel_id=1, source_target_pairs={{0,96},{32,192},{64,160},{96,0},{128,224},{160,64},{192,32},{224,1... | collective-permute-start | bytes 405512 | tf_op jit(solution)/shard_map/ppermute | solution.py:465
  26.2 2.2 %collective-permute-start.1 = (bf16[528,128]{1,0:T(8,128)(2,1)S(1)}, bf16[528,128]{1,0:T(8,128)(2,1)S(1)}, u32[]{:S(2)}, u32[]{:S(2)}) collective-permute-start(bf16[528,128]{1,0:T(8,128)(2,1)S(1)} %pad_maximum_fusion.own), channel_id=1, source_target_pairs={{0,160},{32,128},{64,224},{96,192},{128,32},{160,0},{192,96},{224,... | collective-permute-start | bytes 405512 | tf_op jit(solution)/shard_map/ppermute | solution.py:465
  28.4 0.1 pad_add_fusion.where
  28.5 2.2 %collective-permute-done.far_a = bf16[528,128]{1,0:T(8,128)(2,1)S(1)} collective-permute-done((bf16[528,128]{1,0:T(8,128)(2,1)S(1)}, bf16[528,128]{1,0:T(8,128)(2,1)S(1)}, u32[]{:S(2)}, u32[]{:S(2)}) %collective-permute-start) | collective-permute-done | bytes 135200 | tf_op jit(solution)/shard_map/ppermute | solution.py:465
  30.7 6.3 %collective-permute-done.1.far_b = bf16[528,128]{1,0:T(8,128)(2,1)S(1)} collective-permute-done((bf16[528,128]{1,0:T(8,128)(2,1)S(1)}, bf16[528,128]{1,0:T(8,128)(2,1)S(1)}, u32[]{:S(2)}, u32[]{:S(2)}) %collective-permute-start.1) | collective-permute-done | bytes 135200 | tf_op jit(solution)/shard_map/ppermute | solution.py:465
  37.0 0.6 bundle_queries.1
  37.7 1.6 %collective-permute-start.2 = (bf16[1328,128]{1,0:T(8,128)(2,1)S(1)}, bf16[1328,128]{1,0:T(8,128)(2,1)S(1)}, u32[]{:S(2)}, u32[]{:S(2)}) collective-permute-start(bf16[1328,128]{1,0:T(8,128)(2,1)S(1)} %get-tuple-element.37), channel_id=1, source_target_pairs={{0,32},{32,0},{64,96},{96,64},{128,160},{160,128},{192,224},{224,1... | collective-permute-start | bytes 1019912 | tf_op jit(solution)/shard_map/ppermute | solution.py:465
  39.3 2.4 %collective-permute-start.3 = (bf16[1328,128]{1,0:T(8,128)(2,1)S(1)}, bf16[1328,128]{1,0:T(8,128)(2,1)S(1)}, u32[]{:S(2)}, u32[]{:S(2)}) collective-permute-start(bf16[1328,128]{1,0:T(8,128)(2,1)S(1)} %get-tuple-element.38), channel_id=1, source_target_pairs={{0,224},{32,64},{64,32},{96,128},{128,96},{160,192},{192,160},{224... | collective-permute-start | bytes 1019912 | tf_op jit(solution)/shard_map/ppermute | solution.py:465
  41.7 5.7 %collective-permute-done.2.near_a = bf16[1328,128]{1,0:T(8,128)(2,1)S(1)} collective-permute-done((bf16[1328,128]{1,0:T(8,128)(2,1)S(1)}, bf16[1328,128]{1,0:T(8,128)(2,1)S(1)}, u32[]{:S(2)}, u32[]{:S(2)}) %collective-permute-start.2) | collective-permute-done | bytes 340000 | tf_op jit(solution)/shard_map/ppermute | solution.py:465
  47.4 2.7 %collective-permute-done.3.near_b = bf16[1328,128]{1,0:T(8,128)(2,1)S(1)} collective-permute-done((bf16[1328,128]{1,0:T(8,128)(2,1)S(1)}, bf16[1328,128]{1,0:T(8,128)(2,1)S(1)}, u32[]{:S(2)}, u32[]{:S(2)}) %collective-permute-start.3) | collective-permute-done | bytes 340000 | tf_op jit(solution)/shard_map/ppermute | solution.py:465
  50.1 0.6 stack_queries.1.q_own.q
  50.7 0.1 collective-permute-start.4
  50.8 6.1 %project_rest.1 = (bf16[64,1024]{1,0:T(8,128)(2,1)S(1)}, f32[64,1024]{1,0:T(8,128)S(1)}, bf16[1024,1024]{1,0:T(8,128)(2,1)S(1)}) custom-call(bf16[64,1024]{1,0:T(8,128)(2,1)S(1)} %copy-done.4, bf16[1024,4096]{1,0:T(8,128)(2,1)} %w.3, bf16[64,1024]{1,0:T(8,128)(2,1)S(1)} %get-tuple-element.31.after.q, f32[8]{0:T(128)S(1)} %copy-done.6, bf16[1024,1024]{1,0:T(8,128)(2,1)} %w2.1), custom_call_target="tpu_custom_call" | custom-call | tf_op jit(solution)/shard_map/project_rest/pallas_call | solution.py:138
  57.0 1.4 %copy-done.1 = bf16[1024,1024]{1,0:T(8,128)(2,1)} copy-done((bf16[1024,1024]{1,0:T(8,128)(2,1)}, bf16[1024,1024]{1,0:T(8,128)(2,1)S(1)}, u32[]{:S(2)}) %copy-start.1) | copy-done | bytes 2097176
  58.4 2.3 %read_tables.1.plan = s32[4,16]{1,0:T(4,128)S(1)} custom-call(s32[4]{0:T(128)S(1)} %pad_add_fusion.where, bf16[8,528,128]{2,1,0:T(8,128)(2,1)S(1)} %stack_queries.1.q_own.q, bf16[8,528,128]{2,1,0:T(8,128)(2,1)S(1)} %collective-permute-done.4.q_other), custom_call_target="tpu_custom_call" | custom-call | tf_op jit(solution)/shard_map/read_tables/pallas_call | solution.py:264
  60.6 3.5 %all-to-all-done.1.kv = bf16[16,2,14,32,128]{4,3,2,1,0:T(8,128)(2,1)} async-done(((bf16[16,2,14,32,128]{4,3,2,1,0:T(8,128)(2,1)}), bf16[16,2,14,32,128]{4,3,2,1,0:T(8,128)(2,1)}, u32[]{:S(2)}, u32[]{:S(2)}) %all-to-all-start.1) | async-done | bytes 3670048 | tf_op jit(solution)/shard_map/all_to_all | solution.py:502
  64.1 6.6 %attend_first.1 = (f32[8,512,128]{2,1,0:T(8,128)S(1)}, bf16[8,512,128]{2,1,0:T(8,128)(2,1)S(1)}, bf16[14,16,2,32,128]{4,3,2,1,0:T(8,128)(2,1)S(1)}) custom-call(s32[4,16]{1,0:T(4,128)S(1)} %read_tables.1.plan, s32[4]{0:T(128)S(1)} %pad_add_fusion.where, f32[8,14]{1,0:T(8,128)S(1)} %copy-done.5, bf16[8,528,128]{2,1,0:T(8,128)(2,1)S(1)} %stack_queries.1.q_own.q, ...), custom_call_target="tpu_custom_call" | custom-call | tf_op jit(solution)/shard_map/attend_first/pallas_call | solution.py:320
  70.7 0.1 collective-permute-start.5
  70.8 3.4 %attend_second.1.a.own = bf16[8,512,128]{2,1,0:T(8,128)(2,1)S(1)} custom-call(s32[4,16]{1,0:T(4,128)S(1)} %read_tables.1.plan, s32[4]{0:T(128)S(1)} %pad_add_fusion.where, f32[8,14]{1,0:T(8,128)S(1)} %copy-done.5, bf16[8,528,128]{2,1,0:T(8,128)(2,1)S(1)} %stack_queries.1.q_own.q, bf16[14,16,2,32,128]{4,3,2,1,0:T(8,128)(2,1)S(1)} %get-tuple-element.41.blocks, ...), custom_call_target="tpu_custom_call" | custom-call | tf_op jit(solution)/shard_map/attend_second/pallas_call | solution.py:336
  74.3 0.7 add_far.1
  74.9 1.2 %collective-permute-start.8 = (bf16[512,128]{1,0:T(8,128)(2,1)S(1)}, bf16[512,128]{1,0:T(8,128)(2,1)S(1)}, u32[]{:S(2)}, u32[]{:S(2)}) collective-permute-start(bf16[512,128]{1,0:T(8,128)(2,1)S(1)} %get-tuple-element.44.after), channel_id=1, source_target_pairs={{0,32},{32,0},{64,96},{96,64},{128,160},{160,128},{192,224},{224,1... | collective-permute-start | bytes 393224 | tf_op jit(solution)/shard_map/ppermute | solution.py:465
  76.1 5.0 %collective-permute-start.9 = (bf16[512,128]{1,0:T(8,128)(2,1)S(1)}, bf16[512,128]{1,0:T(8,128)(2,1)S(1)}, u32[]{:S(2)}, u32[]{:S(2)}) collective-permute-start(bf16[512,128]{1,0:T(8,128)(2,1)S(1)} %get-tuple-element.47), channel_id=1, source_target_pairs={{0,224},{32,64},{64,32},{96,128},{128,96},{160,192},{192,160},{224... | collective-permute-start | bytes 393224 | tf_op jit(solution)/shard_map/ppermute | solution.py:465
  81.1 2.2 %collective-permute-start.11 = (bf16[256,128]{1,0:T(8,128)(2,1)S(1)}, bf16[256,128]{1,0:T(8,128)(2,1)S(1)}, u32[]{:S(2)}, u32[]{:S(2)}) collective-permute-start(bf16[256,128]{1,0:T(8,128)(2,1)S(1)} %get-tuple-element.49), channel_id=1, source_target_pairs={{0,192},{32,224},{64,128},{96,160},{128,64},{160,96},{192,0},{224,... | collective-permute-start | bytes 196616 | tf_op jit(solution)/shard_map/ppermute | solution.py:465
  83.3 0.6 add_side.1
  83.9 2.1 %collective-permute-start.6 = (bf16[512,128]{1,0:T(8,128)(2,1)S(1)}, bf16[512,128]{1,0:T(8,128)(2,1)S(1)}, u32[]{:S(2)}, u32[]{:S(2)}) collective-permute-start(bf16[512,128]{1,0:T(8,128)(2,1)S(1)} %get-tuple-element.45), channel_id=1, source_target_pairs={{0,32},{32,0},{64,96},{96,64},{128,160},{160,128},{192,224},{224,1... | collective-permute-start | bytes 393224 | tf_op jit(solution)/shard_map/ppermute | solution.py:465
  86.1 1.4 %collective-permute-done.10.half_a = bf16[256,128]{1,0:T(8,128)(2,1)S(1)} collective-permute-done((bf16[256,128]{1,0:T(8,128)(2,1)S(1)}, bf16[256,128]{1,0:T(8,128)(2,1)S(1)}, u32[]{:S(2)}, u32[]{:S(2)}) %collective-permute-start.10) | collective-permute-done | bytes 65568 | tf_op jit(solution)/shard_map/ppermute | solution.py:465
  87.5 3.4 %collective-permute-start.7 = (bf16[512,128]{1,0:T(8,128)(2,1)S(1)}, bf16[512,128]{1,0:T(8,128)(2,1)S(1)}, u32[]{:S(2)}, u32[]{:S(2)}) collective-permute-start(bf16[512,128]{1,0:T(8,128)(2,1)S(1)} %get-tuple-element.46), channel_id=1, source_target_pairs={{0,224},{32,64},{64,32},{96,128},{128,96},{160,192},{192,160},{224... | collective-permute-start | bytes 393224 | tf_op jit(solution)/shard_map/ppermute | solution.py:465
  90.9 0.7 add_near.1
  91.6 0.6 collective-permute-start.12
  92.2 1.5 %collective-permute-start.13 = (bf16[512,128]{1,0:T(8,128)(2,1)S(1)}, bf16[512,128]{1,0:T(8,128)(2,1)S(1)}, u32[]{:S(2)}, u32[]{:S(2)}) collective-permute-start(bf16[512,128]{1,0:T(8,128)(2,1)S(1)} %get-tuple-element.51), channel_id=1, source_target_pairs={{0,192},{32,224},{64,128},{96,160},{128,64},{160,96},{192,0},{224,... | collective-permute-start | bytes 393224 | tf_op jit(solution)/shard_map/ppermute | solution.py:465
  93.7 0.6 collective-permute-done.7.refs_1_
  94.3 5.4 %collective-permute-done.12.refs_2_ = bf16[512,128]{1,0:T(8,128)(2,1)S(1)} collective-permute-done((bf16[512,128]{1,0:T(8,128)(2,1)S(1)}, bf16[512,128]{1,0:T(8,128)(2,1)S(1)}, u32[]{:S(2)}, u32[]{:S(2)}) %collective-permute-start.12) | collective-permute-done | bytes 131104 | tf_op jit(solution)/shard_map/ppermute | solution.py:465
  99.7 2.5 %collective-permute-done.13.refs_3_ = bf16[512,128]{1,0:T(8,128)(2,1)S(1)} collective-permute-done((bf16[512,128]{1,0:T(8,128)(2,1)S(1)}, bf16[512,128]{1,0:T(8,128)(2,1)S(1)}, u32[]{:S(2)}, u32[]{:S(2)}) %collective-permute-start.13) | collective-permute-done | bytes 131104 | tf_op jit(solution)/shard_map/ppermute | solution.py:465
  102.2 0.8 add_groups.1
  102.9 7.2 %all-to-all-start.2 = ((bf16[8,64,128]{2,1,0:T(8,128)(2,1)}), bf16[8,64,128]{2,1,0:T(8,128)(2,1)S(1)}, u32[]{:S(2)}, u32[]{:S(2)}) async-start(bf16[8,64,128]{2,1,0:T(8,128)(2,1)} %add_groups.1), calls=%async_computation.2 | async-start | bytes 262144 | tf_op jit(solution)/shard_map/all_to_all | solution.py:520
  110.8 4.6 %all-to-all-done.2.hist = bf16[8,64,128]{2,1,0:T(8,128)(2,1)S(1)} async-done(((bf16[8,64,128]{2,1,0:T(8,128)(2,1)}), bf16[8,64,128]{2,1,0:T(8,128)(2,1)S(1)}, u32[]{:S(2)}, u32[]{:S(2)}) %all-to-all-start.2) | async-done | bytes 131104 | tf_op jit(solution)/shard_map/all_to_all | solution.py:520
  115.4 1.8 %output.1 = bf16[64,1024]{1,0:T(8,128)(2,1)} custom-call(bf16[8,64,128]{2,1,0:T(8,128)(2,1)S(1)} %all-to-all-done.2.hist, f32[64,1024]{1,0:T(8,128)S(1)} %get-tuple-element.52.self_term, bf16[64,1024]{1,0:T(8,128)(2,1)S(1)} %get-tuple-element.53.gate, bf16[64,1024]{1,0:T(8,128)(2,1)S(1)} %copy-done.4, bf16[1024,1024]{1,0:T(8,128)(2,1)S(1)} %copy-done.2, ...), custom_call_target="tpu_custom_call" | custom-call | tf_op jit(solution)/shard_map/output/pallas_call | solution.py:453
  (28 shorter events, 0.1 us)
Async XLA Ops:
  0.0 9.0 %copy-start.3 = (bf16[14,32,2048]{2,1,0:T(8,128)(2,1)S(1)}, bf16[14,32,2048]{2,1,0:T(8,128)(2,1)}, u32[]{:S(2)}) copy-start(bf16[14,32,2048]{2,1,0:T(8,128)(2,1)} %pool.1) | copy-start | bytes 5505028
  3.1 11.2 %all-to-all-start = ((bf16[8,64,128]{2,1,0:T(8,128)(2,1)}), bf16[8,64,128]{2,1,0:T(8,128)(2,1)S(1)}, u32[]{:S(2)}, u32[]{:S(2)}) async-start(bf16[8,64,128]{2,1,0:T(8,128)(2,1)} %get-tuple-element.30), calls=%async_computation | async-start | bytes 262144 | tf_op jit(solution)/shard_map/all_to_all | solution.py:499
  9.6 1.8 %copy-start = (bf16[16,2,14,32,128]{4,3,2,1,0:T(8,128)(2,1)}, bf16[16,2,14,32,128]{4,3,2,1,0:T(8,128)(2,1)S(1)}, u32[]{:S(2)}) copy-start(bf16[16,2,14,32,128]{4,3,2,1,0:T(8,128)(2,1)S(1)} %pack_history.1) | copy-start | bytes 11010052
  11.4 9.6 %copy-start.7 = (s32[1,16,2]{1,2,0:T(2,128)S(1)}, s32[1,16,2]{1,2,0:T(2,128)}, u32[]{:S(2)}) copy-start(s32[1,16,2]{1,2,0:T(2,128)} %param.18) | copy-start | bytes 388
  11.4 9.8 %copy-start.8 = (s32[1,16,2]{1,2,0:T(2,128)S(1)}, s32[1,16,2]{1,2,0:T(2,128)}, u32[]{:S(2)}) copy-start(s32[1,16,2]{1,2,0:T(2,128)} %param.19) | copy-start | bytes 388
  14.3 49.8 %all-to-all-start.1 = ((bf16[16,2,14,32,128]{4,3,2,1,0:T(8,128)(2,1)}), bf16[16,2,14,32,128]{4,3,2,1,0:T(8,128)(2,1)}, u32[]{:S(2)}, u32[]{:S(2)}) async-start(bf16[16,2,14,32,128]{4,3,2,1,0:T(8,128)(2,1)} %copy-done), calls=%async_computation.1 | async-start | bytes 7340032 | tf_op jit(solution)/shard_map/all_to_all | solution.py:502
  20.2 30.6 %copy-start.4 = (bf16[64,1024]{1,0:T(8,128)(2,1)S(1)}, bf16[64,1024]{1,0:T(8,128)(2,1)}, u32[]{:S(2)}) copy-start(bf16[64,1024]{1,0:T(8,128)(2,1)} %tokens.5) | copy-start | bytes 393220
  20.2 30.6 %copy-start.6 = (f32[8]{0:T(128)S(1)}, f32[8]{0:T(128)}, u32[]{:S(2)}) copy-start(f32[8]{0:T(128)} %self_bias.1) | copy-start | bytes 100
  21.5 9.2 %collective-permute-start = (bf16[528,128]{1,0:T(8,128)(2,1)S(1)}, bf16[528,128]{1,0:T(8,128)(2,1)S(1)}, u32[]{:S(2)}, u32[]{:S(2)}) collective-permute-start(bf16[528,128]{1,0:T(8,128)(2,1)S(1)} %pad_maximum_fusion.own), channel_id=1, source_target_pairs={{0,96},{32,192},{64,160},{96,0},{128,224},{160,64},{192,32},{224,1... | collective-permute-start | bytes 405512 | tf_op jit(solution)/shard_map/ppermute | solution.py:465
  26.2 10.8 %collective-permute-start.1 = (bf16[528,128]{1,0:T(8,128)(2,1)S(1)}, bf16[528,128]{1,0:T(8,128)(2,1)S(1)}, u32[]{:S(2)}, u32[]{:S(2)}) collective-permute-start(bf16[528,128]{1,0:T(8,128)(2,1)S(1)} %pad_maximum_fusion.own), channel_id=1, source_target_pairs={{0,160},{32,128},{64,224},{96,192},{128,32},{160,0},{192,96},{224,... | collective-permute-start | bytes 405512 | tf_op jit(solution)/shard_map/ppermute | solution.py:465
  37.7 9.7 %collective-permute-start.2 = (bf16[1328,128]{1,0:T(8,128)(2,1)S(1)}, bf16[1328,128]{1,0:T(8,128)(2,1)S(1)}, u32[]{:S(2)}, u32[]{:S(2)}) collective-permute-start(bf16[1328,128]{1,0:T(8,128)(2,1)S(1)} %get-tuple-element.37), channel_id=1, source_target_pairs={{0,32},{32,0},{64,96},{96,64},{128,160},{160,128},{192,224},{224,1... | collective-permute-start | bytes 1019912 | tf_op jit(solution)/shard_map/ppermute | solution.py:465
  39.3 10.8 %collective-permute-start.3 = (bf16[1328,128]{1,0:T(8,128)(2,1)S(1)}, bf16[1328,128]{1,0:T(8,128)(2,1)S(1)}, u32[]{:S(2)}, u32[]{:S(2)}) collective-permute-start(bf16[1328,128]{1,0:T(8,128)(2,1)S(1)} %get-tuple-element.38), channel_id=1, source_target_pairs={{0,224},{32,64},{64,32},{96,128},{128,96},{160,192},{192,160},{224... | collective-permute-start | bytes 1019912 | tf_op jit(solution)/shard_map/ppermute | solution.py:465
  50.7 7.7 %collective-permute-start.4 = (bf16[8,528,128]{2,1,0:T(8,128)(2,1)S(1)}, bf16[8,528,128]{2,1,0:T(8,128)(2,1)S(1)}, u32[]{:S(2)}, u32[]{:S(2)}) collective-permute-start(bf16[8,528,128]{2,1,0:T(8,128)(2,1)S(1)} %stack_queries.1.q_own.q), channel_id=1, source_target_pairs={{0,16},{16,0},{1,17},{17,1},{2,18},{18,2},{3,19},{19,3},{4,20},{20... | collective-permute-start | bytes 3244040 | tf_op jit(solution)/shard_map/ppermute | solution.py:469
  56.9 1.4 %copy-start.1 = (bf16[1024,1024]{1,0:T(8,128)(2,1)}, bf16[1024,1024]{1,0:T(8,128)(2,1)S(1)}, u32[]{:S(2)}) copy-start(bf16[1024,1024]{1,0:T(8,128)(2,1)S(1)} %get-tuple-element.54.w) | copy-start | bytes 6291460
  58.4 5.7 %copy-start.5 = (f32[8,14]{1,0:T(8,128)S(1)}, f32[8,14]{1,0:T(8,128)}, u32[]{:S(2)}) copy-start(f32[8,14]{1,0:T(8,128)} %bias.3) | copy-start | bytes 1348
  70.7 3.5 %collective-permute-start.5 = (bf16[8,512,128]{2,1,0:T(8,128)(2,1)S(1)}, bf16[8,512,128]{2,1,0:T(8,128)(2,1)S(1)}, u32[]{:S(2)}, u32[]{:S(2)}) collective-permute-start(bf16[8,512,128]{2,1,0:T(8,128)(2,1)S(1)} %get-tuple-element.43), channel_id=1, source_target_pairs={{0,16},{16,0},{1,17},{17,1},{2,18},{18,2},{3,19},{19,3},{4,20},{20... | collective-permute-start | bytes 3145736 | tf_op jit(solution)/shard_map/ppermute | solution.py:469
  74.9 15.9 %collective-permute-start.8 = (bf16[512,128]{1,0:T(8,128)(2,1)S(1)}, bf16[512,128]{1,0:T(8,128)(2,1)S(1)}, u32[]{:S(2)}, u32[]{:S(2)}) collective-permute-start(bf16[512,128]{1,0:T(8,128)(2,1)S(1)} %get-tuple-element.44.after), channel_id=1, source_target_pairs={{0,32},{32,0},{64,96},{96,64},{128,160},{160,128},{192,224},{224,1... | collective-permute-start | bytes 393224 | tf_op jit(solution)/shard_map/ppermute | solution.py:465
  76.1 14.7 %collective-permute-start.9 = (bf16[512,128]{1,0:T(8,128)(2,1)S(1)}, bf16[512,128]{1,0:T(8,128)(2,1)S(1)}, u32[]{:S(2)}, u32[]{:S(2)}) collective-permute-start(bf16[512,128]{1,0:T(8,128)(2,1)S(1)} %get-tuple-element.47), channel_id=1, source_target_pairs={{0,224},{32,64},{64,32},{96,128},{128,96},{160,192},{192,160},{224... | collective-permute-start | bytes 393224 | tf_op jit(solution)/shard_map/ppermute | solution.py:465
  81.1 6.4 %collective-permute-start.10 = (bf16[256,128]{1,0:T(8,128)(2,1)S(1)}, bf16[256,128]{1,0:T(8,128)(2,1)S(1)}, u32[]{:S(2)}, u32[]{:S(2)}) collective-permute-start(bf16[256,128]{1,0:T(8,128)(2,1)S(1)} %get-tuple-element.48), channel_id=1, source_target_pairs={{0,64},{32,96},{64,0},{96,32},{128,192},{160,224},{192,128},{224,1... | collective-permute-start | bytes 196616 | tf_op jit(solution)/shard_map/ppermute | solution.py:465
  81.1 9.8 %collective-permute-start.11 = (bf16[256,128]{1,0:T(8,128)(2,1)S(1)}, bf16[256,128]{1,0:T(8,128)(2,1)S(1)}, u32[]{:S(2)}, u32[]{:S(2)}) collective-permute-start(bf16[256,128]{1,0:T(8,128)(2,1)S(1)} %get-tuple-element.49), channel_id=1, source_target_pairs={{0,192},{32,224},{64,128},{96,160},{128,64},{160,96},{192,0},{224,... | collective-permute-start | bytes 196616 | tf_op jit(solution)/shard_map/ppermute | solution.py:465
  83.9 9.8 %collective-permute-start.6 = (bf16[512,128]{1,0:T(8,128)(2,1)S(1)}, bf16[512,128]{1,0:T(8,128)(2,1)S(1)}, u32[]{:S(2)}, u32[]{:S(2)}) collective-permute-start(bf16[512,128]{1,0:T(8,128)(2,1)S(1)} %get-tuple-element.45), channel_id=1, source_target_pairs={{0,32},{32,0},{64,96},{96,64},{128,160},{160,128},{192,224},{224,1... | collective-permute-start | bytes 393224 | tf_op jit(solution)/shard_map/ppermute | solution.py:465
  87.5 6.8 %collective-permute-start.7 = (bf16[512,128]{1,0:T(8,128)(2,1)S(1)}, bf16[512,128]{1,0:T(8,128)(2,1)S(1)}, u32[]{:S(2)}, u32[]{:S(2)}) collective-permute-start(bf16[512,128]{1,0:T(8,128)(2,1)S(1)} %get-tuple-element.46), channel_id=1, source_target_pairs={{0,224},{32,64},{64,32},{96,128},{128,96},{160,192},{192,160},{224... | collective-permute-start | bytes 393224 | tf_op jit(solution)/shard_map/ppermute | solution.py:465
  91.6 23.8 %copy-start.2 = (bf16[1024,1024]{1,0:T(8,128)(2,1)S(1)}, bf16[1024,1024]{1,0:T(8,128)(2,1)}, u32[]{:S(2)}) copy-start(bf16[1024,1024]{1,0:T(8,128)(2,1)} %copy-done.1) | copy-start | bytes 6291460
  91.6 8.0 %collective-permute-start.12 = (bf16[512,128]{1,0:T(8,128)(2,1)S(1)}, bf16[512,128]{1,0:T(8,128)(2,1)S(1)}, u32[]{:S(2)}, u32[]{:S(2)}) collective-permute-start(bf16[512,128]{1,0:T(8,128)(2,1)S(1)} %get-tuple-element.50), channel_id=1, source_target_pairs={{0,64},{32,96},{64,0},{96,32},{128,192},{160,224},{192,128},{224,1... | collective-permute-start | bytes 393224 | tf_op jit(solution)/shard_map/ppermute | solution.py:465
  92.2 9.9 %collective-permute-start.13 = (bf16[512,128]{1,0:T(8,128)(2,1)S(1)}, bf16[512,128]{1,0:T(8,128)(2,1)S(1)}, u32[]{:S(2)}, u32[]{:S(2)}) collective-permute-start(bf16[512,128]{1,0:T(8,128)(2,1)S(1)} %get-tuple-element.51), channel_id=1, source_target_pairs={{0,192},{32,224},{64,128},{96,160},{128,64},{160,96},{192,0},{224,... | collective-permute-start | bytes 393224 | tf_op jit(solution)/shard_map/ppermute | solution.py:465
  102.9 12.5 %all-to-all-start.2 = ((bf16[8,64,128]{2,1,0:T(8,128)(2,1)}), bf16[8,64,128]{2,1,0:T(8,128)(2,1)S(1)}, u32[]{:S(2)}, u32[]{:S(2)}) async-start(bf16[8,64,128]{2,1,0:T(8,128)(2,1)} %add_groups.1), calls=%async_computation.2 | async-start | bytes 262144 | tf_op jit(solution)/shard_map/all_to_all | solution.py:520

commit v6 on v5

--- a/solution.py
+++ b/solution.py
@@ -66,7 +66,7 @@
     )(pool, after)
 
 
-def query_kernel(tokens, w, q_out, send_out, rows, buf, sems):
+def query_kernel(tokens, w, q_out, send_out, rows, buf, send, sems):
     first = pltpu.make_async_copy(tokens, rows, sems.at[4])
     first.start()
     copies = [
@@ -76,12 +76,18 @@
         c.start()
     first.wait()
     normed = norm(rows[...].astype(jnp.float32)).astype(jnp.bfloat16)
+    moves = []
     for i in range(4):
         copies[i].wait()
         q = silu(jnp.dot(normed, buf[i], preferred_element_type=jnp.float32)).astype(jnp.bfloat16)
+        for j in range(2):
+            send[i * 2 + j] = q[:, j * HEAD : (j + 1) * HEAD]
+        two = pl.ds(i * 2, 2)
+        moves.append(pltpu.make_async_copy(send.at[two], send_out.at[two], sems.at[5 + i]))
+        moves[i].start()
         q_out[:, i * 256 : (i + 1) * 256] = q
-        for j in range(2):
-            send_out[i * 2 + j] = q[:, j * HEAD : (j + 1) * HEAD]
+    for c in moves:
+        c.wait()
 
 
 def query(tokens, w):
@@ -92,11 +98,12 @@
             jax.ShapeDtypeStruct((HEADS, ROWS, HEAD), jnp.bfloat16),
         ),
         in_specs=[HB, HB],
-        out_specs=(VM, VM),
+        out_specs=(VM, HB),
         scratch_shapes=[
             pltpu.VMEM((ROWS, D), jnp.bfloat16),
             pltpu.VMEM((4, D, 256), jnp.bfloat16),
-            pltpu.SemaphoreType.DMA((5,)),
+            pltpu.VMEM((HEADS, ROWS, HEAD), jnp.bfloat16),
+            pltpu.SemaphoreType.DMA((9,)),
         ],
         compiler_params=params(12),
         name="project_query",
@@ -298,9 +305,11 @@
 
 def first_kernel(plan, where, bias, q_own, q_other, kv, own, other, blocks, acc, sems):
     copies = [pltpu.make_async_copy(kv.at[:, :, b], blocks.at[b], sems.at[b]) for b in range(BLK)]
-    for c in copies:
+    for c in copies[:2]:
         c.start()
     acc[...] = jnp.zeros_like(acc)
+    for c in copies[2:]:
+        c.start()
 
     def pick(row):
         return jnp.where(row < NZ, q_own[lax.rem(row, NZ), :HALF], q_other[lax.rem(row, NZ), :HALF])
@@ -351,27 +360,22 @@
     return total
 
 
-def far_kernel(where, a, b, out_a, out_b, half_a, half_b):
+def far_kernel(where, a, b, out_a, out_b, across):
     def body(up, down):
         up[...] = add(a[3], b[3]).astype(jnp.bfloat16)
         down[...] = add(a[5], b[5]).astype(jnp.bfloat16)
 
-    def opposite(up, down):
-        up[...] = add(a[4, :256], b[4, :256]).astype(jnp.bfloat16)
-        down[...] = add(a[4, 256:], b[4, 256:]).astype(jnp.bfloat16)
-
     by_side(where, body, (out_a,), (out_b,))
-    by_side(where, opposite, (half_a,), (half_b,), 2)
+    across[...] = add(a[4], b[4]).astype(jnp.bfloat16)
 
 
 def far(*args):
     part = jax.ShapeDtypeStruct((HALF, HEAD), jnp.bfloat16)
-    half = jax.ShapeDtypeStruct((256, HEAD), jnp.bfloat16)
     return pl.pallas_call(
         far_kernel,
-        out_shape=(part, part, half, half),
+        out_shape=(part,) * 3,
         in_specs=[SM] + [VM] * 2,
-        out_specs=(VM,) * 4,
+        out_specs=(VM,) * 3,
         compiler_params=params(12),
         name="add_far",
     )(*args)
@@ -397,19 +401,20 @@
     )(*args)
 
 
-def near_kernel(where, a, b, near_a, near_b, half_a, half_b, out_a, out_b, ups, downs):
-    def body(plus, minus):
-        ups[...] = add(a[2], b[2], minus[...])
-        downs[...] = add(a[6], b[6], plus[...])
-
-    def opposite(plus, up, minus, down):
-        up[:256] = add(ups[:256], minus[...]).astype(jnp.bfloat16)
-        up[256:] = ups[256:].astype(jnp.bfloat16)
-        down[:256] = downs[:256].astype(jnp.bfloat16)
-        down[256:] = add(downs[256:], plus[...]).astype(jnp.bfloat16)
-
-    by_side(where, body, (near_a,), (near_b,))
-    by_side(where, opposite, (half_a, out_a), (half_b, out_b), 2)
+def near_kernel(where, a, b, near_a, near_b, across, out_a, out_b):
+    rising = lax.rem(lax.div(where[0], 2), 2) == 0
+    goes_up = rising == (where[1] == 1)
+
+    def width(up, down):
+        def body(ahead, behind):
+            moved = across[...].astype(jnp.float32)
+            none = jnp.zeros_like(moved)
+            up[...] = add(a[2], b[2], behind[...], jnp.where(goes_up, moved, none)).astype(jnp.bfloat16)
+            down[...] = add(a[6], b[6], ahead[...], jnp.where(goes_up, none, moved)).astype(jnp.bfloat16)
+
+        by_side(where, body, (near_a,), (near_b,))
+
+    by_side(where, width, (out_a,), (out_b,), 2)
 
 
 def near(*args):
@@ -417,9 +422,8 @@
     return pl.pallas_call(
         near_kernel,
         out_shape=(part, part),
-        in_specs=[SM] + [VM] * 6,
+        in_specs=[SM] + [VM] * 5,
         out_specs=(VM,) * 2,
-        scratch_shapes=[pltpu.VMEM((HALF, HEAD), jnp.float32)] * 2,
         compiler_params=params(12),
         name="add_near",
     )(*args)
@@ -463,6 +467,14 @@
 def move(value, step, width=1):
     pairs = [(i, (i + (-step if i // width % 2 else step)) % NZ) for i in range(NZ)]
     return lax.ppermute(value, "z", pairs)
+
+
+def cross(value):
+    pairs = []
+    for i in range(NG):
+        step = 2 if (i // 4 + i) % 2 == 0 else -2
+        pairs.append((i, (i // 2 + step) % NZ * 2 + i % 2))
+    return lax.ppermute(value, G, pairs)
 
 
 def swap(value):
@@ -511,11 +523,10 @@
     own, other, blocks = attend_first(plan, where, position_bias, q_own, q_other, kv)
     other = swap(other)
     own = attend_second(plan, where, position_bias, q_own, blocks, own)
-    out_a, out_b, half_a, half_b = far(where, own, other)
+    out_a, out_b, across = far(where, own, other)
     side_a, side_b = side(where, own, other, out_a)
     side_a, side_b = move(side_a, 1), move(side_b, -1)
-    half_a, half_b = move(half_a, 2, 2), move(half_b, -2, 2)
-    out_a, out_b = near(where, own, other, move(out_a, 1), move(out_b, -1), half_a, half_b)
+    out_a, out_b = near(where, own, other, move(out_a, 1), move(out_b, -1), cross(across))
     hist = total(own, other, side_a, side_b, move(out_a, 2, 2), move(out_b, -2, 2))
     hist = lax.all_to_all(hist, W, split_axis=0, concat_axis=0, tiled=True)
     return tail(hist, self_term, gate, tokens, w2, where, candidate_count)

time: 118 us -> 116 us (0.983)
  waiting for transfers between devices: 37.8 us -> 35.8 us
    ppermute x0 -> x1, starting transfers between devices: none -> 3.85 us  [cross(): return lax.ppermute(value, G, pairs)]
    ppermute x12 -> x10, starting transfers between devices: 26.9 us -> 23.7 us  [move(): return lax.ppermute(value, 'z', pairs)]
    ppermute x12 -> x10, waiting for transfers between devices: 26.8 us -> 24.8 us  [move(): return lax.ppermute(value, 'z', pairs)]
  transfers between devices with their start and end apart: 17 -> 16, of which waited for: 11 -> 10; matrix products, arithmetic and copies ran while one was open for 1% -> 1% of each run, Pallas kernels for 13% -> 12%
where the time goes in v6:
time: 116 us; the launch traced here: 115 us
  starting transfers between devices  46.9 us (40%)
  waiting for transfers between devices  35.8 us (31%)
  Pallas kernels  27.4 us (24%)
  local copies, waits for them, and re-layouts  3.75 us (3%)
  between operations  1.62 us (1%)
    ppermute x10, waiting for transfers between devices, move(): return lax.ppermute(value, 'z', pairs)  24.8 us
    ppermute x10, starting transfers between devices, move(): return lax.ppermute(value, 'z', pairs)  23.7 us
    all_to_all x1, starting transfers between devices, local(): hist = lax.all_to_all(hist, W, split_axis=0, concat_axis=0, tiled=True)  7.25 us
    pallas_call x1, Pallas kernels, attend_first(): pl.pallas_call(first_kernel, out_shape=(jax.ShapeDtypeStruct((NZ, HALF, H...  6.64 us
    pallas_call x1, Pallas kernels, rest(): pl.pallas_call(rest_kernel, out_shape=(jax.ShapeDtypeStruct((ROWS, D), jn...  6.12 us
    all_to_all x1, starting transfers between devices, local(): q_mine = lax.all_to_all(q_send, W, split_axis=0, concat_axis=0, tiled=True)  5.94 us
    all_to_all x1, starting transfers between devices, local(): kv = lax.all_to_all(packed, M, split_axis=0, concat_axis=0, tiled=True)  5.91 us
    all_to_all x1, waiting for transfers between devices, local(): hist = lax.all_to_all(hist, W, split_axis=0, concat_axis=0, tiled=True)  4.6 us
  transfers between devices with their start and end apart: 16, of which 10 were waited for; matrix products, arithmetic and copies ran while one was open for 1% of the time, Pallas kernels for 12%

profile of v6, /device:TPU:2, one launch (start us, length us, event | category | flops | bytes accessed | tf_op | source)
XLA Modules:
  0.0 115.5 jit_solution(17998307717279655414)
XLA Ops:
  0.0 3.1 %project_query.1 = (bf16[64,1024]{1,0:T(8,128)(2,1)S(1)}, bf16[8,64,128]{2,1,0:T(8,128)(2,1)}) custom-call(bf16[64,1024]{1,0:T(8,128)(2,1)} %tokens.5, bf16[1024,4096]{1,0:T(8,128)(2,1)} %w.3), custom_call_target="tpu_custom_call" | custom-call | tf_op jit(solution)/shard_map/project_query/pallas_call | solution.py:94
  3.1 5.9 %all-to-all-start = ((bf16[8,64,128]{2,1,0:T(8,128)(2,1)}), bf16[8,64,128]{2,1,0:T(8,128)(2,1)S(1)}, u32[]{:S(2)}, u32[]{:S(2)}) async-start(bf16[8,64,128]{2,1,0:T(8,128)(2,1)} %get-tuple-element.29), calls=%async_computation | async-start | bytes 262144 | tf_op jit(solution)/shard_map/all_to_all | solution.py:511
  9.0 0.5 pack_history.1
  9.6 1.8 %copy-done = bf16[16,2,14,32,128]{4,3,2,1,0:T(8,128)(2,1)} copy-done((bf16[16,2,14,32,128]{4,3,2,1,0:T(8,128)(2,1)}, bf16[16,2,14,32,128]{4,3,2,1,0:T(8,128)(2,1)S(1)}, u32[]{:S(2)}) %copy-start) | copy-done | bytes 3670040
  11.4 2.9 %all-to-all-done = bf16[8,64,128]{2,1,0:T(8,128)(2,1)S(1)} async-done(((bf16[8,64,128]{2,1,0:T(8,128)(2,1)}), bf16[8,64,128]{2,1,0:T(8,128)(2,1)S(1)}, u32[]{:S(2)}, u32[]{:S(2)}) %all-to-all-start) | async-done | bytes 131104 | tf_op jit(solution)/shard_map/all_to_all | solution.py:511
  14.3 5.9 %all-to-all-start.1 = ((bf16[16,2,14,32,128]{4,3,2,1,0:T(8,128)(2,1)}), bf16[16,2,14,32,128]{4,3,2,1,0:T(8,128)(2,1)}, u32[]{:S(2)}, u32[]{:S(2)}) async-start(bf16[16,2,14,32,128]{4,3,2,1,0:T(8,128)(2,1)} %copy-done), calls=%async_computation.1 | async-start | bytes 7340032 | tf_op jit(solution)/shard_map/all_to_all | solution.py:514
  20.2 0.0 copy-start.6
  20.9 0.1 copy.13
  21.0 0.1 concatenate.20
  21.2 0.1 copy.14
  21.3 0.1 concatenate.21
  21.4 0.1 concatenate.24
  21.5 4.7 %collective-permute-start = (bf16[528,128]{1,0:T(8,128)(2,1)S(1)}, bf16[528,128]{1,0:T(8,128)(2,1)S(1)}, u32[]{:S(2)}, u32[]{:S(2)}) collective-permute-start(bf16[528,128]{1,0:T(8,128)(2,1)S(1)} %pad_maximum_fusion.own), channel_id=1, source_target_pairs={{0,96},{32,192},{64,160},{96,0},{128,224},{160,64},{192,32},{224,1... | collective-permute-start | bytes 405512 | tf_op jit(solution)/shard_map/ppermute | solution.py:469
  26.2 2.2 %collective-permute-start.1 = (bf16[528,128]{1,0:T(8,128)(2,1)S(1)}, bf16[528,128]{1,0:T(8,128)(2,1)S(1)}, u32[]{:S(2)}, u32[]{:S(2)}) collective-permute-start(bf16[528,128]{1,0:T(8,128)(2,1)S(1)} %pad_maximum_fusion.own), channel_id=1, source_target_pairs={{0,160},{32,128},{64,224},{96,192},{128,32},{160,0},{192,96},{224,... | collective-permute-start | bytes 405512 | tf_op jit(solution)/shard_map/ppermute | solution.py:469
  28.4 0.1 pad_add_fusion.where
  28.5 2.2 %collective-permute-done.far_a = bf16[528,128]{1,0:T(8,128)(2,1)S(1)} collective-permute-done((bf16[528,128]{1,0:T(8,128)(2,1)S(1)}, bf16[528,128]{1,0:T(8,128)(2,1)S(1)}, u32[]{:S(2)}, u32[]{:S(2)}) %collective-permute-start) | collective-permute-done | bytes 135200 | tf_op jit(solution)/shard_map/ppermute | solution.py:469
  30.7 6.3 %collective-permute-done.1.far_b = bf16[528,128]{1,0:T(8,128)(2,1)S(1)} collective-permute-done((bf16[528,128]{1,0:T(8,128)(2,1)S(1)}, bf16[528,128]{1,0:T(8,128)(2,1)S(1)}, u32[]{:S(2)}, u32[]{:S(2)}) %collective-permute-start.1) | collective-permute-done | bytes 135200 | tf_op jit(solution)/shard_map/ppermute | solution.py:469
  37.0 0.6 bundle_queries.1
  37.7 1.6 %collective-permute-start.2 = (bf16[1328,128]{1,0:T(8,128)(2,1)S(1)}, bf16[1328,128]{1,0:T(8,128)(2,1)S(1)}, u32[]{:S(2)}, u32[]{:S(2)}) collective-permute-start(bf16[1328,128]{1,0:T(8,128)(2,1)S(1)} %get-tuple-element.36), channel_id=1, source_target_pairs={{0,32},{32,0},{64,96},{96,64},{128,160},{160,128},{192,224},{224,1... | collective-permute-start | bytes 1019912 | tf_op jit(solution)/shard_map/ppermute | solution.py:469
  39.3 2.4 %collective-permute-start.3 = (bf16[1328,128]{1,0:T(8,128)(2,1)S(1)}, bf16[1328,128]{1,0:T(8,128)(2,1)S(1)}, u32[]{:S(2)}, u32[]{:S(2)}) collective-permute-start(bf16[1328,128]{1,0:T(8,128)(2,1)S(1)} %get-tuple-element.37), channel_id=1, source_target_pairs={{0,224},{32,64},{64,32},{96,128},{128,96},{160,192},{192,160},{224... | collective-permute-start | bytes 1019912 | tf_op jit(solution)/shard_map/ppermute | solution.py:469
  41.6 5.7 %collective-permute-done.2.near_a = bf16[1328,128]{1,0:T(8,128)(2,1)S(1)} collective-permute-done((bf16[1328,128]{1,0:T(8,128)(2,1)S(1)}, bf16[1328,128]{1,0:T(8,128)(2,1)S(1)}, u32[]{:S(2)}, u32[]{:S(2)}) %collective-permute-start.2) | collective-permute-done | bytes 340000 | tf_op jit(solution)/shard_map/ppermute | solution.py:469
  47.4 2.7 %collective-permute-done.3.near_b = bf16[1328,128]{1,0:T(8,128)(2,1)S(1)} collective-permute-done((bf16[1328,128]{1,0:T(8,128)(2,1)S(1)}, bf16[1328,128]{1,0:T(8,128)(2,1)S(1)}, u32[]{:S(2)}, u32[]{:S(2)}) %collective-permute-start.3) | collective-permute-done | bytes 340000 | tf_op jit(solution)/shard_map/ppermute | solution.py:469
  50.1 0.6 stack_queries.1.q_own.q
  50.7 0.1 collective-permute-start.4
  50.8 6.1 %project_rest.1 = (bf16[64,1024]{1,0:T(8,128)(2,1)S(1)}, f32[64,1024]{1,0:T(8,128)S(1)}, bf16[1024,1024]{1,0:T(8,128)(2,1)S(1)}) custom-call(bf16[64,1024]{1,0:T(8,128)(2,1)S(1)} %copy-done.4, bf16[1024,4096]{1,0:T(8,128)(2,1)} %w.3, bf16[64,1024]{1,0:T(8,128)(2,1)S(1)} %get-tuple-element.30.after.q, f32[8]{0:T(128)S(1)} %copy-done.6, bf16[1024,1024]{1,0:T(8,128)(2,1)} %w2.1), custom_call_target="tpu_custom_call" | custom-call | tf_op jit(solution)/shard_map/project_rest/pallas_call | solution.py:145
  56.9 1.4 %copy-done.1 = bf16[1024,1024]{1,0:T(8,128)(2,1)} copy-done((bf16[1024,1024]{1,0:T(8,128)(2,1)}, bf16[1024,1024]{1,0:T(8,128)(2,1)S(1)}, u32[]{:S(2)}) %copy-start.1) | copy-done | bytes 2097176
  58.4 2.3 %read_tables.1.plan = s32[4,16]{1,0:T(4,128)S(1)} custom-call(s32[4]{0:T(128)S(1)} %pad_add_fusion.where, bf16[8,528,128]{2,1,0:T(8,128)(2,1)S(1)} %stack_queries.1.q_own.q, bf16[8,528,128]{2,1,0:T(8,128)(2,1)S(1)} %collective-permute-done.4.q_other), custom_call_target="tpu_custom_call" | custom-call | tf_op jit(solution)/shard_map/read_tables/pallas_call | solution.py:271
  60.6 3.5 %all-to-all-done.1.kv = bf16[16,2,14,32,128]{4,3,2,1,0:T(8,128)(2,1)} async-done(((bf16[16,2,14,32,128]{4,3,2,1,0:T(8,128)(2,1)}), bf16[16,2,14,32,128]{4,3,2,1,0:T(8,128)(2,1)}, u32[]{:S(2)}, u32[]{:S(2)}) %all-to-all-start.1) | async-done | bytes 3670048 | tf_op jit(solution)/shard_map/all_to_all | solution.py:514
  64.1 6.6 %attend_first.1 = (f32[8,512,128]{2,1,0:T(8,128)S(1)}, bf16[8,512,128]{2,1,0:T(8,128)(2,1)S(1)}, bf16[14,16,2,32,128]{4,3,2,1,0:T(8,128)(2,1)S(1)}) custom-call(s32[4,16]{1,0:T(4,128)S(1)} %read_tables.1.plan, s32[4]{0:T(128)S(1)} %pad_add_fusion.where, f32[8,14]{1,0:T(8,128)S(1)} %copy-done.5, bf16[8,528,128]{2,1,0:T(8,128)(2,1)S(1)} %stack_queries.1.q_own.q, ...), custom_call_target="tpu_custom_call" | custom-call | tf_op jit(solution)/shard_map/attend_first/pallas_call | solution.py:329
  70.7 0.1 collective-permute-start.5
  70.8 2.9 %attend_second.1.a.own = bf16[8,512,128]{2,1,0:T(8,128)(2,1)S(1)} custom-call(s32[4,16]{1,0:T(4,128)S(1)} %read_tables.1.plan, s32[4]{0:T(128)S(1)} %pad_add_fusion.where, f32[8,14]{1,0:T(8,128)S(1)} %copy-done.5, bf16[8,528,128]{2,1,0:T(8,128)(2,1)S(1)} %stack_queries.1.q_own.q, bf16[14,16,2,32,128]{4,3,2,1,0:T(8,128)(2,1)S(1)} %get-tuple-element.40.blocks, ...), custom_call_target="tpu_custom_call" | custom-call | tf_op jit(solution)/shard_map/attend_second/pallas_call | solution.py:345
  73.8 0.6 add_far.1
  74.5 3.9 %collective-permute-start.10 = (bf16[512,128]{1,0:T(8,128)(2,1)S(1)}, bf16[512,128]{1,0:T(8,128)(2,1)S(1)}, u32[]{:S(2)}, u32[]{:S(2)}) collective-permute-start(bf16[512,128]{1,0:T(8,128)(2,1)S(1)} %get-tuple-element.47), channel_id=1, source_target_pairs={{0,64},{16,208},{32,96},{48,240},{64,0},{80,144},{96,32},{112,176}... | collective-permute-start | bytes 393224 | tf_op jit(solution)/shard_map/ppermute | solution.py:477
  78.3 1.2 %collective-permute-start.8 = (bf16[512,128]{1,0:T(8,128)(2,1)S(1)}, bf16[512,128]{1,0:T(8,128)(2,1)S(1)}, u32[]{:S(2)}, u32[]{:S(2)}) collective-permute-start(bf16[512,128]{1,0:T(8,128)(2,1)S(1)} %get-tuple-element.43.after), channel_id=1, source_target_pairs={{0,32},{32,0},{64,96},{96,64},{128,160},{160,128},{192,224},{224,1... | collective-permute-start | bytes 393224 | tf_op jit(solution)/shard_map/ppermute | solution.py:469
  79.5 3.0 %collective-permute-start.9 = (bf16[512,128]{1,0:T(8,128)(2,1)S(1)}, bf16[512,128]{1,0:T(8,128)(2,1)S(1)}, u32[]{:S(2)}, u32[]{:S(2)}) collective-permute-start(bf16[512,128]{1,0:T(8,128)(2,1)S(1)} %get-tuple-element.46), channel_id=1, source_target_pairs={{0,224},{32,64},{64,32},{96,128},{128,96},{160,192},{192,160},{224... | collective-permute-start | bytes 393224 | tf_op jit(solution)/shard_map/ppermute | solution.py:469
  82.5 0.6 add_side.1
  83.1 0.1 collective-permute-start.6
  83.2 2.8 %collective-permute-start.7 = (bf16[512,128]{1,0:T(8,128)(2,1)S(1)}, bf16[512,128]{1,0:T(8,128)(2,1)S(1)}, u32[]{:S(2)}, u32[]{:S(2)}) collective-permute-start(bf16[512,128]{1,0:T(8,128)(2,1)S(1)} %get-tuple-element.45), channel_id=1, source_target_pairs={{0,224},{32,64},{64,32},{96,128},{128,96},{160,192},{192,160},{224... | collective-permute-start | bytes 393224 | tf_op jit(solution)/shard_map/ppermute | solution.py:469
  86.1 1.2 %collective-permute-done.9.near_b = bf16[512,128]{1,0:T(8,128)(2,1)S(1)} collective-permute-done((bf16[512,128]{1,0:T(8,128)(2,1)S(1)}, bf16[512,128]{1,0:T(8,128)(2,1)S(1)}, u32[]{:S(2)}, u32[]{:S(2)}) %collective-permute-start.9) | collective-permute-done | bytes 131104 | tf_op jit(solution)/shard_map/ppermute | solution.py:469
  87.3 0.7 add_near.1
  88.0 0.1 collective-permute-start.11
  88.1 5.6 %collective-permute-start.12 = (bf16[512,128]{1,0:T(8,128)(2,1)S(1)}, bf16[512,128]{1,0:T(8,128)(2,1)S(1)}, u32[]{:S(2)}, u32[]{:S(2)}) collective-permute-start(bf16[512,128]{1,0:T(8,128)(2,1)S(1)} %get-tuple-element.49), channel_id=1, source_target_pairs={{0,192},{32,224},{64,128},{96,160},{128,64},{160,96},{192,0},{224,... | collective-permute-start | bytes 393224 | tf_op jit(solution)/shard_map/ppermute | solution.py:469
  93.7 3.8 %collective-permute-done.11.refs_2_ = bf16[512,128]{1,0:T(8,128)(2,1)S(1)} collective-permute-done((bf16[512,128]{1,0:T(8,128)(2,1)S(1)}, bf16[512,128]{1,0:T(8,128)(2,1)S(1)}, u32[]{:S(2)}, u32[]{:S(2)}) %collective-permute-start.11) | collective-permute-done | bytes 131104 | tf_op jit(solution)/shard_map/ppermute | solution.py:469
  97.6 2.8 %collective-permute-done.12.refs_3_ = bf16[512,128]{1,0:T(8,128)(2,1)S(1)} collective-permute-done((bf16[512,128]{1,0:T(8,128)(2,1)S(1)}, bf16[512,128]{1,0:T(8,128)(2,1)S(1)}, u32[]{:S(2)}, u32[]{:S(2)}) %collective-permute-start.12) | collective-permute-done | bytes 131104 | tf_op jit(solution)/shard_map/ppermute | solution.py:469
  100.4 0.8 add_groups.1
  101.1 7.3 %all-to-all-start.2 = ((bf16[8,64,128]{2,1,0:T(8,128)(2,1)}), bf16[8,64,128]{2,1,0:T(8,128)(2,1)S(1)}, u32[]{:S(2)}, u32[]{:S(2)}) async-start(bf16[8,64,128]{2,1,0:T(8,128)(2,1)} %add_groups.1), calls=%async_computation.2 | async-start | bytes 262144 | tf_op jit(solution)/shard_map/all_to_all | solution.py:531
  109.0 4.6 %all-to-all-done.2.hist = bf16[8,64,128]{2,1,0:T(8,128)(2,1)S(1)} async-done(((bf16[8,64,128]{2,1,0:T(8,128)(2,1)}), bf16[8,64,128]{2,1,0:T(8,128)(2,1)S(1)}, u32[]{:S(2)}, u32[]{:S(2)}) %all-to-all-start.2) | async-done | bytes 131104 | tf_op jit(solution)/shard_map/all_to_all | solution.py:531
  113.6 1.8 %output.1 = bf16[64,1024]{1,0:T(8,128)(2,1)} custom-call(bf16[8,64,128]{2,1,0:T(8,128)(2,1)S(1)} %all-to-all-done.2.hist, f32[64,1024]{1,0:T(8,128)S(1)} %get-tuple-element.50.self_term, bf16[64,1024]{1,0:T(8,128)(2,1)S(1)} %get-tuple-element.51.gate, bf16[64,1024]{1,0:T(8,128)(2,1)S(1)} %copy-done.4, bf16[1024,1024]{1,0:T(8,128)(2,1)S(1)} %copy-done.2, ...), custom_call_target="tpu_custom_call" | custom-call | tf_op jit(solution)/shard_map/output/pallas_call | solution.py:457
  (26 shorter events, 0.1 us)
Async XLA Ops:
  0.0 9.0 %copy-start.3 = (bf16[14,32,2048]{2,1,0:T(8,128)(2,1)S(1)}, bf16[14,32,2048]{2,1,0:T(8,128)(2,1)}, u32[]{:S(2)}) copy-start(bf16[14,32,2048]{2,1,0:T(8,128)(2,1)} %pool.1) | copy-start | bytes 5505028
  3.1 11.2 %all-to-all-start = ((bf16[8,64,128]{2,1,0:T(8,128)(2,1)}), bf16[8,64,128]{2,1,0:T(8,128)(2,1)S(1)}, u32[]{:S(2)}, u32[]{:S(2)}) async-start(bf16[8,64,128]{2,1,0:T(8,128)(2,1)} %get-tuple-element.29), calls=%async_computation | async-start | bytes 262144 | tf_op jit(solution)/shard_map/all_to_all | solution.py:511
  9.5 1.8 %copy-start = (bf16[16,2,14,32,128]{4,3,2,1,0:T(8,128)(2,1)}, bf16[16,2,14,32,128]{4,3,2,1,0:T(8,128)(2,1)S(1)}, u32[]{:S(2)}) copy-start(bf16[16,2,14,32,128]{4,3,2,1,0:T(8,128)(2,1)S(1)} %pack_history.1) | copy-start | bytes 11010052
  11.4 9.5 %copy-start.7 = (s32[1,16,2]{1,2,0:T(2,128)S(1)}, s32[1,16,2]{1,2,0:T(2,128)}, u32[]{:S(2)}) copy-start(s32[1,16,2]{1,2,0:T(2,128)} %param.18) | copy-start | bytes 388
  11.4 9.8 %copy-start.8 = (s32[1,16,2]{1,2,0:T(2,128)S(1)}, s32[1,16,2]{1,2,0:T(2,128)}, u32[]{:S(2)}) copy-start(s32[1,16,2]{1,2,0:T(2,128)} %param.19) | copy-start | bytes 388
  14.3 49.8 %all-to-all-start.1 = ((bf16[16,2,14,32,128]{4,3,2,1,0:T(8,128)(2,1)}), bf16[16,2,14,32,128]{4,3,2,1,0:T(8,128)(2,1)}, u32[]{:S(2)}, u32[]{:S(2)}) async-start(bf16[16,2,14,32,128]{4,3,2,1,0:T(8,128)(2,1)} %copy-done), calls=%async_computation.1 | async-start | bytes 7340032 | tf_op jit(solution)/shard_map/all_to_all | solution.py:514
  20.2 30.6 %copy-start.4 = (bf16[64,1024]{1,0:T(8,128)(2,1)S(1)}, bf16[64,1024]{1,0:T(8,128)(2,1)}, u32[]{:S(2)}) copy-start(bf16[64,1024]{1,0:T(8,128)(2,1)} %tokens.5) | copy-start | bytes 393220
  20.2 30.6 %copy-start.6 = (f32[8]{0:T(128)S(1)}, f32[8]{0:T(128)}, u32[]{:S(2)}) copy-start(f32[8]{0:T(128)} %self_bias.1) | copy-start | bytes 100
  21.5 9.2 %collective-permute-start = (bf16[528,128]{1,0:T(8,128)(2,1)S(1)}, bf16[528,128]{1,0:T(8,128)(2,1)S(1)}, u32[]{:S(2)}, u32[]{:S(2)}) collective-permute-start(bf16[528,128]{1,0:T(8,128)(2,1)S(1)} %pad_maximum_fusion.own), channel_id=1, source_target_pairs={{0,96},{32,192},{64,160},{96,0},{128,224},{160,64},{192,32},{224,1... | collective-permute-start | bytes 405512 | tf_op jit(solution)/shard_map/ppermute | solution.py:469
  26.2 10.8 %collective-permute-start.1 = (bf16[528,128]{1,0:T(8,128)(2,1)S(1)}, bf16[528,128]{1,0:T(8,128)(2,1)S(1)}, u32[]{:S(2)}, u32[]{:S(2)}) collective-permute-start(bf16[528,128]{1,0:T(8,128)(2,1)S(1)} %pad_maximum_fusion.own), channel_id=1, source_target_pairs={{0,160},{32,128},{64,224},{96,192},{128,32},{160,0},{192,96},{224,... | collective-permute-start | bytes 405512 | tf_op jit(solution)/shard_map/ppermute | solution.py:469
  37.7 9.7 %collective-permute-start.2 = (bf16[1328,128]{1,0:T(8,128)(2,1)S(1)}, bf16[1328,128]{1,0:T(8,128)(2,1)S(1)}, u32[]{:S(2)}, u32[]{:S(2)}) collective-permute-start(bf16[1328,128]{1,0:T(8,128)(2,1)S(1)} %get-tuple-element.36), channel_id=1, source_target_pairs={{0,32},{32,0},{64,96},{96,64},{128,160},{160,128},{192,224},{224,1... | collective-permute-start | bytes 1019912 | tf_op jit(solution)/shard_map/ppermute | solution.py:469
  39.3 10.8 %collective-permute-start.3 = (bf16[1328,128]{1,0:T(8,128)(2,1)S(1)}, bf16[1328,128]{1,0:T(8,128)(2,1)S(1)}, u32[]{:S(2)}, u32[]{:S(2)}) collective-permute-start(bf16[1328,128]{1,0:T(8,128)(2,1)S(1)} %get-tuple-element.37), channel_id=1, source_target_pairs={{0,224},{32,64},{64,32},{96,128},{128,96},{160,192},{192,160},{224... | collective-permute-start | bytes 1019912 | tf_op jit(solution)/shard_map/ppermute | solution.py:469
  50.7 7.7 %collective-permute-start.4 = (bf16[8,528,128]{2,1,0:T(8,128)(2,1)S(1)}, bf16[8,528,128]{2,1,0:T(8,128)(2,1)S(1)}, u32[]{:S(2)}, u32[]{:S(2)}) collective-permute-start(bf16[8,528,128]{2,1,0:T(8,128)(2,1)S(1)} %stack_queries.1.q_own.q), channel_id=1, source_target_pairs={{0,16},{16,0},{1,17},{17,1},{2,18},{18,2},{3,19},{19,3},{4,20},{20... | collective-permute-start | bytes 3244040 | tf_op jit(solution)/shard_map/ppermute | solution.py:481
  56.9 1.4 %copy-start.1 = (bf16[1024,1024]{1,0:T(8,128)(2,1)}, bf16[1024,1024]{1,0:T(8,128)(2,1)S(1)}, u32[]{:S(2)}) copy-start(bf16[1024,1024]{1,0:T(8,128)(2,1)S(1)} %get-tuple-element.52.w) | copy-start | bytes 6291460
  58.4 5.7 %copy-start.5 = (f32[8,14]{1,0:T(8,128)S(1)}, f32[8,14]{1,0:T(8,128)}, u32[]{:S(2)}) copy-start(f32[8,14]{1,0:T(8,128)} %bias.3) | copy-start | bytes 1348
  70.7 3.0 %collective-permute-start.5 = (bf16[8,512,128]{2,1,0:T(8,128)(2,1)S(1)}, bf16[8,512,128]{2,1,0:T(8,128)(2,1)S(1)}, u32[]{:S(2)}, u32[]{:S(2)}) collective-permute-start(bf16[8,512,128]{2,1,0:T(8,128)(2,1)S(1)} %get-tuple-element.42), channel_id=1, source_target_pairs={{0,16},{16,0},{1,17},{17,1},{2,18},{18,2},{3,19},{19,3},{4,20},{20... | collective-permute-start | bytes 3145736 | tf_op jit(solution)/shard_map/ppermute | solution.py:481
  74.5 11.6 %collective-permute-start.10 = (bf16[512,128]{1,0:T(8,128)(2,1)S(1)}, bf16[512,128]{1,0:T(8,128)(2,1)S(1)}, u32[]{:S(2)}, u32[]{:S(2)}) collective-permute-start(bf16[512,128]{1,0:T(8,128)(2,1)S(1)} %get-tuple-element.47), channel_id=1, source_target_pairs={{0,64},{16,208},{32,96},{48,240},{64,0},{80,144},{96,32},{112,176}... | collective-permute-start | bytes 393224 | tf_op jit(solution)/shard_map/ppermute | solution.py:477
  78.3 7.8 %collective-permute-start.8 = (bf16[512,128]{1,0:T(8,128)(2,1)S(1)}, bf16[512,128]{1,0:T(8,128)(2,1)S(1)}, u32[]{:S(2)}, u32[]{:S(2)}) collective-permute-start(bf16[512,128]{1,0:T(8,128)(2,1)S(1)} %get-tuple-element.43.after), channel_id=1, source_target_pairs={{0,32},{32,0},{64,96},{96,64},{128,160},{160,128},{192,224},{224,1... | collective-permute-start | bytes 393224 | tf_op jit(solution)/shard_map/ppermute | solution.py:469
  79.5 7.8 %collective-permute-start.9 = (bf16[512,128]{1,0:T(8,128)(2,1)S(1)}, bf16[512,128]{1,0:T(8,128)(2,1)S(1)}, u32[]{:S(2)}, u32[]{:S(2)}) collective-permute-start(bf16[512,128]{1,0:T(8,128)(2,1)S(1)} %get-tuple-element.46), channel_id=1, source_target_pairs={{0,224},{32,64},{64,32},{96,128},{128,96},{160,192},{192,160},{224... | collective-permute-start | bytes 393224 | tf_op jit(solution)/shard_map/ppermute | solution.py:469
  83.1 10.6 %collective-permute-start.6 = (bf16[512,128]{1,0:T(8,128)(2,1)S(1)}, bf16[512,128]{1,0:T(8,128)(2,1)S(1)}, u32[]{:S(2)}, u32[]{:S(2)}) collective-permute-start(bf16[512,128]{1,0:T(8,128)(2,1)S(1)} %get-tuple-element.44), channel_id=1, source_target_pairs={{0,32},{32,0},{64,96},{96,64},{128,160},{160,128},{192,224},{224,1... | collective-permute-start | bytes 393224 | tf_op jit(solution)/shard_map/ppermute | solution.py:469
  83.2 10.5 %collective-permute-start.7 = (bf16[512,128]{1,0:T(8,128)(2,1)S(1)}, bf16[512,128]{1,0:T(8,128)(2,1)S(1)}, u32[]{:S(2)}, u32[]{:S(2)}) collective-permute-start(bf16[512,128]{1,0:T(8,128)(2,1)S(1)} %get-tuple-element.45), channel_id=1, source_target_pairs={{0,224},{32,64},{64,32},{96,128},{128,96},{160,192},{192,160},{224... | collective-permute-start | bytes 393224 | tf_op jit(solution)/shard_map/ppermute | solution.py:469
  88.0 25.6 %copy-start.2 = (bf16[1024,1024]{1,0:T(8,128)(2,1)S(1)}, bf16[1024,1024]{1,0:T(8,128)(2,1)}, u32[]{:S(2)}) copy-start(bf16[1024,1024]{1,0:T(8,128)(2,1)} %copy-done.1) | copy-start | bytes 6291460
  88.0 9.5 %collective-permute-start.11 = (bf16[512,128]{1,0:T(8,128)(2,1)S(1)}, bf16[512,128]{1,0:T(8,128)(2,1)S(1)}, u32[]{:S(2)}, u32[]{:S(2)}) collective-permute-start(bf16[512,128]{1,0:T(8,128)(2,1)S(1)} %get-tuple-element.48), channel_id=1, source_target_pairs={{0,64},{32,96},{64,0},{96,32},{128,192},{160,224},{192,128},{224,1... | collective-permute-start | bytes 393224 | tf_op jit(solution)/shard_map/ppermute | solution.py:469
  88.1 12.2 %collective-permute-start.12 = (bf16[512,128]{1,0:T(8,128)(2,1)S(1)}, bf16[512,128]{1,0:T(8,128)(2,1)S(1)}, u32[]{:S(2)}, u32[]{:S(2)}) collective-permute-start(bf16[512,128]{1,0:T(8,128)(2,1)S(1)} %get-tuple-element.49), channel_id=1, source_target_pairs={{0,192},{32,224},{64,128},{96,160},{128,64},{160,96},{192,0},{224,... | collective-permute-start | bytes 393224 | tf_op jit(solution)/shard_map/ppermute | solution.py:469
  101.1 12.5 %all-to-all-start.2 = ((bf16[8,64,128]{2,1,0:T(8,128)(2,1)}), bf16[8,64,128]{2,1,0:T(8,128)(2,1)S(1)}, u32[]{:S(2)}, u32[]{:S(2)}) async-start(bf16[8,64,128]{2,1,0:T(8,128)(2,1)} %add_groups.1), calls=%async_computation.2 | async-start | bytes 262144 | tf_op jit(solution)/shard_map/all_to_all | solution.py:531

commit v7 on v6

--- a/solution.py
+++ b/solution.py
@@ -256,7 +256,7 @@
         return carry
 
     lax.fori_loop(0, NG, step, 0)
-    budget = FIRST
+    budget = FIRST + 3 * where[1]
     for b in range(BLK):
         budget -= (plan[0, b] >= NZ).astype(jnp.int32)
     for b in range(BLK):
@@ -293,8 +293,6 @@
             row = plan[0, b]
             keys = blocks[b, :, 0].reshape(BLOCK, HEAD)
             values = blocks[b, :, 1].reshape(BLOCK, HEAD)
-            token = lax.broadcasted_iota(jnp.int32, (BLOCK, HEAD), 0)
-            values = jnp.where(token < plan[2, b], values, jnp.zeros_like(values))
             scores = lax.dot_general(
                 pick(row), keys, (((1,), (1,)), ((), ())), preferred_element_type=jnp.float32
             )
@@ -314,7 +312,17 @@
     def pick(row):
         return jnp.where(row < NZ, q_own[lax.rem(row, NZ), :HALF], q_other[lax.rem(row, NZ), :HALF])
 
-    attend_blocks(0, plan, where, bias, pick, blocks, lambda b: copies[b].wait(), acc)
+    def ready(b):
+        copies[b].wait()
+
+        @pl.when((plan[0, b] >= 0) & (plan[2, b] < BLOCK))
+        def _():
+            values = blocks[b, :, 1].reshape(BLOCK, HEAD)
+            token = lax.broadcasted_iota(jnp.int32, (BLOCK, HEAD), 0)
+            values = jnp.where(token < plan[2, b], values, jnp.zeros_like(values))
+            blocks[b, :, 1] = values.reshape(NM, SLAB, HEAD)
+
+    attend_blocks(0, plan, where, bias, pick, blocks, ready, acc)
     own[...] = acc[:NZ]
     other[...] = acc[NZ:].astype(jnp.bfloat16)
 
@@ -407,10 +415,15 @@
 
     def width(up, down):
         def body(ahead, behind):
-            moved = across[...].astype(jnp.float32)
-            none = jnp.zeros_like(moved)
-            up[...] = add(a[2], b[2], behind[...], jnp.where(goes_up, moved, none)).astype(jnp.bfloat16)
-            down[...] = add(a[6], b[6], ahead[...], jnp.where(goes_up, none, moved)).astype(jnp.bfloat16)
+            @pl.when(goes_up)
+            def _():
+                up[...] = add(a[2], b[2], behind[...], across[...]).astype(jnp.bfloat16)
+                down[...] = add(a[6], b[6], ahead[...]).astype(jnp.bfloat16)
+
+            @pl.when(jnp.logical_not(goes_up))
+            def _():
+                up[...] = add(a[2], b[2], behind[...]).astype(jnp.bfloat16)
+                down[...] = add(a[6], b[6], ahead[...], across[...]).astype(jnp.bfloat16)
 
         by_side(where, body, (near_a,), (near_b,))
 

time: 116 us -> 115 us (level)
  transfers between devices with their start and end apart: 16 -> 16, of which waited for: 10 -> 11; matrix products, arithmetic and copies ran while one was open for 1% -> 1% of each run, Pallas kernels for 12% -> 12%
where the time goes in v7:
time: 115 us; the launch traced here: 114 us
  starting transfers between devices  46.6 us (41%)
  waiting for transfers between devices  35.2 us (31%)
  Pallas kernels  27 us (23%)
  local copies, waits for them, and re-layouts  3.75 us (3%)
  between operations  1.6 us (1%)
    ppermute x10, waiting for transfers between devices, move(): return lax.ppermute(value, 'z', pairs)  24 us
    ppermute x10, starting transfers between devices, move(): return lax.ppermute(value, 'z', pairs)  23.1 us
    all_to_all x1, starting transfers between devices, local(): hist = lax.all_to_all(hist, W, split_axis=0, concat_axis=0, tiled=True)  7.25 us
    pallas_call x1, Pallas kernels, attend_first(): pl.pallas_call(first_kernel, out_shape=(jax.ShapeDtypeStruct((NZ, HALF, H...  6.76 us
    pallas_call x1, Pallas kernels, rest(): pl.pallas_call(rest_kernel, out_shape=(jax.ShapeDtypeStruct((ROWS, D), jn...  6.12 us
    all_to_all x1, starting transfers between devices, local(): q_mine = lax.all_to_all(q_send, W, split_axis=0, concat_axis=0, tiled=True)  5.94 us
    all_to_all x1, starting transfers between devices, local(): kv = lax.all_to_all(packed, M, split_axis=0, concat_axis=0, tiled=True)  5.91 us
    all_to_all x1, waiting for transfers between devices, local(): hist = lax.all_to_all(hist, W, split_axis=0, concat_axis=0, tiled=True)  4.6 us
  transfers between devices with their start and end apart: 16, of which 11 were waited for; matrix products, arithmetic and copies ran while one was open for 1% of the time, Pallas kernels for 12%

profile of v7, /device:TPU:2, one launch (start us, length us, event | category | flops | bytes accessed | tf_op | source)
XLA Modules:
  0.0 114.2 jit_solution(12801448755505319925)
XLA Ops:
  0.0 3.1 %project_query.1 = (bf16[64,1024]{1,0:T(8,128)(2,1)S(1)}, bf16[8,64,128]{2,1,0:T(8,128)(2,1)}) custom-call(bf16[64,1024]{1,0:T(8,128)(2,1)} %tokens.5, bf16[1024,4096]{1,0:T(8,128)(2,1)} %w.3), custom_call_target="tpu_custom_call" | custom-call | tf_op jit(solution)/shard_map/project_query/pallas_call | solution.py:94
  3.1 5.9 %all-to-all-start = ((bf16[8,64,128]{2,1,0:T(8,128)(2,1)}), bf16[8,64,128]{2,1,0:T(8,128)(2,1)S(1)}, u32[]{:S(2)}, u32[]{:S(2)}) async-start(bf16[8,64,128]{2,1,0:T(8,128)(2,1)} %get-tuple-element.29), calls=%async_computation | async-start | bytes 262144 | tf_op jit(solution)/shard_map/all_to_all | solution.py:524
  9.0 0.5 pack_history.1
  9.6 1.8 %copy-done = bf16[16,2,14,32,128]{4,3,2,1,0:T(8,128)(2,1)} copy-done((bf16[16,2,14,32,128]{4,3,2,1,0:T(8,128)(2,1)}, bf16[16,2,14,32,128]{4,3,2,1,0:T(8,128)(2,1)S(1)}, u32[]{:S(2)}) %copy-start) | copy-done | bytes 3670040
  11.4 2.9 %all-to-all-done = bf16[8,64,128]{2,1,0:T(8,128)(2,1)S(1)} async-done(((bf16[8,64,128]{2,1,0:T(8,128)(2,1)}), bf16[8,64,128]{2,1,0:T(8,128)(2,1)S(1)}, u32[]{:S(2)}, u32[]{:S(2)}) %all-to-all-start) | async-done | bytes 131104 | tf_op jit(solution)/shard_map/all_to_all | solution.py:524
  14.3 5.9 %all-to-all-start.1 = ((bf16[16,2,14,32,128]{4,3,2,1,0:T(8,128)(2,1)}), bf16[16,2,14,32,128]{4,3,2,1,0:T(8,128)(2,1)}, u32[]{:S(2)}, u32[]{:S(2)}) async-start(bf16[16,2,14,32,128]{4,3,2,1,0:T(8,128)(2,1)} %copy-done), calls=%async_computation.1 | async-start | bytes 7340032 | tf_op jit(solution)/shard_map/all_to_all | solution.py:527
  20.9 0.1 copy.13
  21.0 0.1 concatenate.20
  21.2 0.1 copy.14
  21.3 0.1 concatenate.21
  21.4 0.1 concatenate.24
  21.5 4.7 %collective-permute-start = (bf16[528,128]{1,0:T(8,128)(2,1)S(1)}, bf16[528,128]{1,0:T(8,128)(2,1)S(1)}, u32[]{:S(2)}, u32[]{:S(2)}) collective-permute-start(bf16[528,128]{1,0:T(8,128)(2,1)S(1)} %pad_maximum_fusion.own), channel_id=1, source_target_pairs={{0,96},{32,192},{64,160},{96,0},{128,224},{160,64},{192,32},{224,1... | collective-permute-start | bytes 405512 | tf_op jit(solution)/shard_map/ppermute | solution.py:482
  26.2 2.2 %collective-permute-start.1 = (bf16[528,128]{1,0:T(8,128)(2,1)S(1)}, bf16[528,128]{1,0:T(8,128)(2,1)S(1)}, u32[]{:S(2)}, u32[]{:S(2)}) collective-permute-start(bf16[528,128]{1,0:T(8,128)(2,1)S(1)} %pad_maximum_fusion.own), channel_id=1, source_target_pairs={{0,160},{32,128},{64,224},{96,192},{128,32},{160,0},{192,96},{224,... | collective-permute-start | bytes 405512 | tf_op jit(solution)/shard_map/ppermute | solution.py:482
  28.4 0.1 pad_add_fusion.where
  28.5 2.2 %collective-permute-done.far_a = bf16[528,128]{1,0:T(8,128)(2,1)S(1)} collective-permute-done((bf16[528,128]{1,0:T(8,128)(2,1)S(1)}, bf16[528,128]{1,0:T(8,128)(2,1)S(1)}, u32[]{:S(2)}, u32[]{:S(2)}) %collective-permute-start) | collective-permute-done | bytes 135200 | tf_op jit(solution)/shard_map/ppermute | solution.py:482
  30.7 6.3 %collective-permute-done.1.far_b = bf16[528,128]{1,0:T(8,128)(2,1)S(1)} collective-permute-done((bf16[528,128]{1,0:T(8,128)(2,1)S(1)}, bf16[528,128]{1,0:T(8,128)(2,1)S(1)}, u32[]{:S(2)}, u32[]{:S(2)}) %collective-permute-start.1) | collective-permute-done | bytes 135200 | tf_op jit(solution)/shard_map/ppermute | solution.py:482
  37.0 0.6 bundle_queries.1
  37.7 1.6 %collective-permute-start.2 = (bf16[1328,128]{1,0:T(8,128)(2,1)S(1)}, bf16[1328,128]{1,0:T(8,128)(2,1)S(1)}, u32[]{:S(2)}, u32[]{:S(2)}) collective-permute-start(bf16[1328,128]{1,0:T(8,128)(2,1)S(1)} %get-tuple-element.36), channel_id=1, source_target_pairs={{0,32},{32,0},{64,96},{96,64},{128,160},{160,128},{192,224},{224,1... | collective-permute-start | bytes 1019912 | tf_op jit(solution)/shard_map/ppermute | solution.py:482
  39.3 2.4 %collective-permute-start.3 = (bf16[1328,128]{1,0:T(8,128)(2,1)S(1)}, bf16[1328,128]{1,0:T(8,128)(2,1)S(1)}, u32[]{:S(2)}, u32[]{:S(2)}) collective-permute-start(bf16[1328,128]{1,0:T(8,128)(2,1)S(1)} %get-tuple-element.37), channel_id=1, source_target_pairs={{0,224},{32,64},{64,32},{96,128},{128,96},{160,192},{192,160},{224... | collective-permute-start | bytes 1019912 | tf_op jit(solution)/shard_map/ppermute | solution.py:482
  41.6 5.7 %collective-permute-done.2.near_a = bf16[1328,128]{1,0:T(8,128)(2,1)S(1)} collective-permute-done((bf16[1328,128]{1,0:T(8,128)(2,1)S(1)}, bf16[1328,128]{1,0:T(8,128)(2,1)S(1)}, u32[]{:S(2)}, u32[]{:S(2)}) %collective-permute-start.2) | collective-permute-done | bytes 340000 | tf_op jit(solution)/shard_map/ppermute | solution.py:482
  47.4 2.7 %collective-permute-done.3.near_b = bf16[1328,128]{1,0:T(8,128)(2,1)S(1)} collective-permute-done((bf16[1328,128]{1,0:T(8,128)(2,1)S(1)}, bf16[1328,128]{1,0:T(8,128)(2,1)S(1)}, u32[]{:S(2)}, u32[]{:S(2)}) %collective-permute-start.3) | collective-permute-done | bytes 340000 | tf_op jit(solution)/shard_map/ppermute | solution.py:482
  50.1 0.6 stack_queries.1.q_own.q
  50.7 0.1 collective-permute-start.4
  50.8 6.1 %project_rest.1 = (bf16[64,1024]{1,0:T(8,128)(2,1)S(1)}, f32[64,1024]{1,0:T(8,128)S(1)}, bf16[1024,1024]{1,0:T(8,128)(2,1)S(1)}) custom-call(bf16[64,1024]{1,0:T(8,128)(2,1)S(1)} %copy-done.4, bf16[1024,4096]{1,0:T(8,128)(2,1)} %w.3, bf16[64,1024]{1,0:T(8,128)(2,1)S(1)} %get-tuple-element.30.after.q, f32[8]{0:T(128)S(1)} %copy-done.6, bf16[1024,1024]{1,0:T(8,128)(2,1)} %w2.1), custom_call_target="tpu_custom_call" | custom-call | tf_op jit(solution)/shard_map/project_rest/pallas_call | solution.py:145
  56.9 1.4 %copy-done.1 = bf16[1024,1024]{1,0:T(8,128)(2,1)} copy-done((bf16[1024,1024]{1,0:T(8,128)(2,1)}, bf16[1024,1024]{1,0:T(8,128)(2,1)S(1)}, u32[]{:S(2)}) %copy-start.1) | copy-done | bytes 2097176
  58.4 2.3 %read_tables.1.plan = s32[4,16]{1,0:T(4,128)S(1)} custom-call(s32[4]{0:T(128)S(1)} %pad_add_fusion.where, bf16[8,528,128]{2,1,0:T(8,128)(2,1)S(1)} %stack_queries.1.q_own.q, bf16[8,528,128]{2,1,0:T(8,128)(2,1)S(1)} %collective-permute-done.4.q_other), custom_call_target="tpu_custom_call" | custom-call | tf_op jit(solution)/shard_map/read_tables/pallas_call | solution.py:271
  60.6 3.5 %all-to-all-done.1.kv = bf16[16,2,14,32,128]{4,3,2,1,0:T(8,128)(2,1)} async-done(((bf16[16,2,14,32,128]{4,3,2,1,0:T(8,128)(2,1)}), bf16[16,2,14,32,128]{4,3,2,1,0:T(8,128)(2,1)}, u32[]{:S(2)}, u32[]{:S(2)}) %all-to-all-start.1) | async-done | bytes 3670048 | tf_op jit(solution)/shard_map/all_to_all | solution.py:527
  64.1 6.8 %attend_first.1 = (f32[8,512,128]{2,1,0:T(8,128)S(1)}, bf16[8,512,128]{2,1,0:T(8,128)(2,1)S(1)}, bf16[14,16,2,32,128]{4,3,2,1,0:T(8,128)(2,1)S(1)}) custom-call(s32[4,16]{1,0:T(4,128)S(1)} %read_tables.1.plan, s32[4]{0:T(128)S(1)} %pad_add_fusion.where, f32[8,14]{1,0:T(8,128)S(1)} %copy-done.5, bf16[8,528,128]{2,1,0:T(8,128)(2,1)S(1)} %stack_queries.1.q_own.q, ...), custom_call_target="tpu_custom_call" | custom-call | tf_op jit(solution)/shard_map/attend_first/pallas_call | solution.py:337
  70.9 0.1 collective-permute-start.5
  71.0 2.4 %attend_second.1.a.own = bf16[8,512,128]{2,1,0:T(8,128)(2,1)S(1)} custom-call(s32[4,16]{1,0:T(4,128)S(1)} %read_tables.1.plan, s32[4]{0:T(128)S(1)} %pad_add_fusion.where, f32[8,14]{1,0:T(8,128)S(1)} %copy-done.5, bf16[8,528,128]{2,1,0:T(8,128)(2,1)S(1)} %stack_queries.1.q_own.q, bf16[14,16,2,32,128]{4,3,2,1,0:T(8,128)(2,1)S(1)} %get-tuple-element.40.blocks, ...), custom_call_target="tpu_custom_call" | custom-call | tf_op jit(solution)/shard_map/attend_second/pallas_call | solution.py:353
  73.4 0.2 collective-permute-done.5.b.other
  73.6 0.6 add_far.1
  74.3 4.2 %collective-permute-start.10 = (bf16[512,128]{1,0:T(8,128)(2,1)S(1)}, bf16[512,128]{1,0:T(8,128)(2,1)S(1)}, u32[]{:S(2)}, u32[]{:S(2)}) collective-permute-start(bf16[512,128]{1,0:T(8,128)(2,1)S(1)} %get-tuple-element.47), channel_id=1, source_target_pairs={{0,64},{16,208},{32,96},{48,240},{64,0},{80,144},{96,32},{112,176}... | collective-permute-start | bytes 393224 | tf_op jit(solution)/shard_map/ppermute | solution.py:490
  78.5 1.9 %collective-permute-start.8 = (bf16[512,128]{1,0:T(8,128)(2,1)S(1)}, bf16[512,128]{1,0:T(8,128)(2,1)S(1)}, u32[]{:S(2)}, u32[]{:S(2)}) collective-permute-start(bf16[512,128]{1,0:T(8,128)(2,1)S(1)} %get-tuple-element.43.after), channel_id=1, source_target_pairs={{0,32},{32,0},{64,96},{96,64},{128,160},{160,128},{192,224},{224,1... | collective-permute-start | bytes 393224 | tf_op jit(solution)/shard_map/ppermute | solution.py:482
  80.4 3.0 %collective-permute-start.9 = (bf16[512,128]{1,0:T(8,128)(2,1)S(1)}, bf16[512,128]{1,0:T(8,128)(2,1)S(1)}, u32[]{:S(2)}, u32[]{:S(2)}) collective-permute-start(bf16[512,128]{1,0:T(8,128)(2,1)S(1)} %get-tuple-element.46), channel_id=1, source_target_pairs={{0,224},{32,64},{64,32},{96,128},{128,96},{160,192},{192,160},{224... | collective-permute-start | bytes 393224 | tf_op jit(solution)/shard_map/ppermute | solution.py:482
  83.5 0.6 add_side.1
  84.1 0.1 collective-permute-start.6
  84.2 2.0 %collective-permute-start.7 = (bf16[512,128]{1,0:T(8,128)(2,1)S(1)}, bf16[512,128]{1,0:T(8,128)(2,1)S(1)}, u32[]{:S(2)}, u32[]{:S(2)}) collective-permute-start(bf16[512,128]{1,0:T(8,128)(2,1)S(1)} %get-tuple-element.45), channel_id=1, source_target_pairs={{0,224},{32,64},{64,32},{96,128},{128,96},{160,192},{192,160},{224... | collective-permute-start | bytes 393224 | tf_op jit(solution)/shard_map/ppermute | solution.py:482
  86.3 1.8 %collective-permute-done.9.near_b = bf16[512,128]{1,0:T(8,128)(2,1)S(1)} collective-permute-done((bf16[512,128]{1,0:T(8,128)(2,1)S(1)}, bf16[512,128]{1,0:T(8,128)(2,1)S(1)}, u32[]{:S(2)}, u32[]{:S(2)}) %collective-permute-start.9) | collective-permute-done | bytes 131104 | tf_op jit(solution)/shard_map/ppermute | solution.py:482
  88.0 0.7 add_near.1
  88.7 1.1 collective-permute-start.11
  89.8 4.0 %collective-permute-start.12 = (bf16[512,128]{1,0:T(8,128)(2,1)S(1)}, bf16[512,128]{1,0:T(8,128)(2,1)S(1)}, u32[]{:S(2)}, u32[]{:S(2)}) collective-permute-start(bf16[512,128]{1,0:T(8,128)(2,1)S(1)} %get-tuple-element.49), channel_id=1, source_target_pairs={{0,192},{32,224},{64,128},{96,160},{128,64},{160,96},{192,0},{224,... | collective-permute-start | bytes 393224 | tf_op jit(solution)/shard_map/ppermute | solution.py:482
  93.8 3.3 %collective-permute-done.11.refs_2_ = bf16[512,128]{1,0:T(8,128)(2,1)S(1)} collective-permute-done((bf16[512,128]{1,0:T(8,128)(2,1)S(1)}, bf16[512,128]{1,0:T(8,128)(2,1)S(1)}, u32[]{:S(2)}, u32[]{:S(2)}) %collective-permute-start.11) | collective-permute-done | bytes 131104 | tf_op jit(solution)/shard_map/ppermute | solution.py:482
  97.1 2.0 %collective-permute-done.12.refs_3_ = bf16[512,128]{1,0:T(8,128)(2,1)S(1)} collective-permute-done((bf16[512,128]{1,0:T(8,128)(2,1)S(1)}, bf16[512,128]{1,0:T(8,128)(2,1)S(1)}, u32[]{:S(2)}, u32[]{:S(2)}) %collective-permute-start.12) | collective-permute-done | bytes 131104 | tf_op jit(solution)/shard_map/ppermute | solution.py:482
  99.1 0.8 add_groups.1
  99.9 7.2 %all-to-all-start.2 = ((bf16[8,64,128]{2,1,0:T(8,128)(2,1)}), bf16[8,64,128]{2,1,0:T(8,128)(2,1)S(1)}, u32[]{:S(2)}, u32[]{:S(2)}) async-start(bf16[8,64,128]{2,1,0:T(8,128)(2,1)} %add_groups.1), calls=%async_computation.2 | async-start | bytes 262144 | tf_op jit(solution)/shard_map/all_to_all | solution.py:544
  107.8 4.6 %all-to-all-done.2.hist = bf16[8,64,128]{2,1,0:T(8,128)(2,1)S(1)} async-done(((bf16[8,64,128]{2,1,0:T(8,128)(2,1)}), bf16[8,64,128]{2,1,0:T(8,128)(2,1)S(1)}, u32[]{:S(2)}, u32[]{:S(2)}) %all-to-all-start.2) | async-done | bytes 131104 | tf_op jit(solution)/shard_map/all_to_all | solution.py:544
  112.4 1.8 %output.1 = bf16[64,1024]{1,0:T(8,128)(2,1)} custom-call(bf16[8,64,128]{2,1,0:T(8,128)(2,1)S(1)} %all-to-all-done.2.hist, f32[64,1024]{1,0:T(8,128)S(1)} %get-tuple-element.50.self_term, bf16[64,1024]{1,0:T(8,128)(2,1)S(1)} %get-tuple-element.51.gate, bf16[64,1024]{1,0:T(8,128)(2,1)S(1)} %copy-done.4, bf16[1024,1024]{1,0:T(8,128)(2,1)S(1)} %copy-done.2, ...), custom_call_target="tpu_custom_call" | custom-call | tf_op jit(solution)/shard_map/output/pallas_call | solution.py:470
  (26 shorter events, 0.1 us)
Async XLA Ops:
  0.0 9.0 %copy-start.3 = (bf16[14,32,2048]{2,1,0:T(8,128)(2,1)S(1)}, bf16[14,32,2048]{2,1,0:T(8,128)(2,1)}, u32[]{:S(2)}) copy-start(bf16[14,32,2048]{2,1,0:T(8,128)(2,1)} %pool.1) | copy-start | bytes 5505028
  3.1 11.2 %all-to-all-start = ((bf16[8,64,128]{2,1,0:T(8,128)(2,1)}), bf16[8,64,128]{2,1,0:T(8,128)(2,1)S(1)}, u32[]{:S(2)}, u32[]{:S(2)}) async-start(bf16[8,64,128]{2,1,0:T(8,128)(2,1)} %get-tuple-element.29), calls=%async_computation | async-start | bytes 262144 | tf_op jit(solution)/shard_map/all_to_all | solution.py:524
  9.5 1.8 %copy-start = (bf16[16,2,14,32,128]{4,3,2,1,0:T(8,128)(2,1)}, bf16[16,2,14,32,128]{4,3,2,1,0:T(8,128)(2,1)S(1)}, u32[]{:S(2)}) copy-start(bf16[16,2,14,32,128]{4,3,2,1,0:T(8,128)(2,1)S(1)} %pack_history.1) | copy-start | bytes 11010052
  11.4 9.5 %copy-start.7 = (s32[1,16,2]{1,2,0:T(2,128)S(1)}, s32[1,16,2]{1,2,0:T(2,128)}, u32[]{:S(2)}) copy-start(s32[1,16,2]{1,2,0:T(2,128)} %param.18) | copy-start | bytes 388
  11.4 9.8 %copy-start.8 = (s32[1,16,2]{1,2,0:T(2,128)S(1)}, s32[1,16,2]{1,2,0:T(2,128)}, u32[]{:S(2)}) copy-start(s32[1,16,2]{1,2,0:T(2,128)} %param.19) | copy-start | bytes 388
  14.3 49.8 %all-to-all-start.1 = ((bf16[16,2,14,32,128]{4,3,2,1,0:T(8,128)(2,1)}), bf16[16,2,14,32,128]{4,3,2,1,0:T(8,128)(2,1)}, u32[]{:S(2)}, u32[]{:S(2)}) async-start(bf16[16,2,14,32,128]{4,3,2,1,0:T(8,128)(2,1)} %copy-done), calls=%async_computation.1 | async-start | bytes 7340032 | tf_op jit(solution)/shard_map/all_to_all | solution.py:527
  20.2 30.6 %copy-start.4 = (bf16[64,1024]{1,0:T(8,128)(2,1)S(1)}, bf16[64,1024]{1,0:T(8,128)(2,1)}, u32[]{:S(2)}) copy-start(bf16[64,1024]{1,0:T(8,128)(2,1)} %tokens.5) | copy-start | bytes 393220
  20.2 30.6 %copy-start.6 = (f32[8]{0:T(128)S(1)}, f32[8]{0:T(128)}, u32[]{:S(2)}) copy-start(f32[8]{0:T(128)} %self_bias.1) | copy-start | bytes 100
  21.5 9.2 %collective-permute-start = (bf16[528,128]{1,0:T(8,128)(2,1)S(1)}, bf16[528,128]{1,0:T(8,128)(2,1)S(1)}, u32[]{:S(2)}, u32[]{:S(2)}) collective-permute-start(bf16[528,128]{1,0:T(8,128)(2,1)S(1)} %pad_maximum_fusion.own), channel_id=1, source_target_pairs={{0,96},{32,192},{64,160},{96,0},{128,224},{160,64},{192,32},{224,1... | collective-permute-start | bytes 405512 | tf_op jit(solution)/shard_map/ppermute | solution.py:482
  26.2 10.8 %collective-permute-start.1 = (bf16[528,128]{1,0:T(8,128)(2,1)S(1)}, bf16[528,128]{1,0:T(8,128)(2,1)S(1)}, u32[]{:S(2)}, u32[]{:S(2)}) collective-permute-start(bf16[528,128]{1,0:T(8,128)(2,1)S(1)} %pad_maximum_fusion.own), channel_id=1, source_target_pairs={{0,160},{32,128},{64,224},{96,192},{128,32},{160,0},{192,96},{224,... | collective-permute-start | bytes 405512 | tf_op jit(solution)/shard_map/ppermute | solution.py:482
  37.7 9.7 %collective-permute-start.2 = (bf16[1328,128]{1,0:T(8,128)(2,1)S(1)}, bf16[1328,128]{1,0:T(8,128)(2,1)S(1)}, u32[]{:S(2)}, u32[]{:S(2)}) collective-permute-start(bf16[1328,128]{1,0:T(8,128)(2,1)S(1)} %get-tuple-element.36), channel_id=1, source_target_pairs={{0,32},{32,0},{64,96},{96,64},{128,160},{160,128},{192,224},{224,1... | collective-permute-start | bytes 1019912 | tf_op jit(solution)/shard_map/ppermute | solution.py:482
  39.3 10.8 %collective-permute-start.3 = (bf16[1328,128]{1,0:T(8,128)(2,1)S(1)}, bf16[1328,128]{1,0:T(8,128)(2,1)S(1)}, u32[]{:S(2)}, u32[]{:S(2)}) collective-permute-start(bf16[1328,128]{1,0:T(8,128)(2,1)S(1)} %get-tuple-element.37), channel_id=1, source_target_pairs={{0,224},{32,64},{64,32},{96,128},{128,96},{160,192},{192,160},{224... | collective-permute-start | bytes 1019912 | tf_op jit(solution)/shard_map/ppermute | solution.py:482
  50.7 7.7 %collective-permute-start.4 = (bf16[8,528,128]{2,1,0:T(8,128)(2,1)S(1)}, bf16[8,528,128]{2,1,0:T(8,128)(2,1)S(1)}, u32[]{:S(2)}, u32[]{:S(2)}) collective-permute-start(bf16[8,528,128]{2,1,0:T(8,128)(2,1)S(1)} %stack_queries.1.q_own.q), channel_id=1, source_target_pairs={{0,16},{16,0},{1,17},{17,1},{2,18},{18,2},{3,19},{19,3},{4,20},{20... | collective-permute-start | bytes 3244040 | tf_op jit(solution)/shard_map/ppermute | solution.py:494
  56.9 1.4 %copy-start.1 = (bf16[1024,1024]{1,0:T(8,128)(2,1)}, bf16[1024,1024]{1,0:T(8,128)(2,1)S(1)}, u32[]{:S(2)}) copy-start(bf16[1024,1024]{1,0:T(8,128)(2,1)S(1)} %get-tuple-element.52.w) | copy-start | bytes 6291460
  58.4 5.7 %copy-start.5 = (f32[8,14]{1,0:T(8,128)S(1)}, f32[8,14]{1,0:T(8,128)}, u32[]{:S(2)}) copy-start(f32[8,14]{1,0:T(8,128)} %bias.3) | copy-start | bytes 1348
  70.9 2.7 %collective-permute-start.5 = (bf16[8,512,128]{2,1,0:T(8,128)(2,1)S(1)}, bf16[8,512,128]{2,1,0:T(8,128)(2,1)S(1)}, u32[]{:S(2)}, u32[]{:S(2)}) collective-permute-start(bf16[8,512,128]{2,1,0:T(8,128)(2,1)S(1)} %get-tuple-element.42), channel_id=1, source_target_pairs={{0,16},{16,0},{1,17},{17,1},{2,18},{18,2},{3,19},{19,3},{4,20},{20... | collective-permute-start | bytes 3145736 | tf_op jit(solution)/shard_map/ppermute | solution.py:494
  74.3 12.0 %collective-permute-start.10 = (bf16[512,128]{1,0:T(8,128)(2,1)S(1)}, bf16[512,128]{1,0:T(8,128)(2,1)S(1)}, u32[]{:S(2)}, u32[]{:S(2)}) collective-permute-start(bf16[512,128]{1,0:T(8,128)(2,1)S(1)} %get-tuple-element.47), channel_id=1, source_target_pairs={{0,64},{16,208},{32,96},{48,240},{64,0},{80,144},{96,32},{112,176}... | collective-permute-start | bytes 393224 | tf_op jit(solution)/shard_map/ppermute | solution.py:490
  78.5 7.8 %collective-permute-start.8 = (bf16[512,128]{1,0:T(8,128)(2,1)S(1)}, bf16[512,128]{1,0:T(8,128)(2,1)S(1)}, u32[]{:S(2)}, u32[]{:S(2)}) collective-permute-start(bf16[512,128]{1,0:T(8,128)(2,1)S(1)} %get-tuple-element.43.after), channel_id=1, source_target_pairs={{0,32},{32,0},{64,96},{96,64},{128,160},{160,128},{192,224},{224,1... | collective-permute-start | bytes 393224 | tf_op jit(solution)/shard_map/ppermute | solution.py:482
  80.4 7.6 %collective-permute-start.9 = (bf16[512,128]{1,0:T(8,128)(2,1)S(1)}, bf16[512,128]{1,0:T(8,128)(2,1)S(1)}, u32[]{:S(2)}, u32[]{:S(2)}) collective-permute-start(bf16[512,128]{1,0:T(8,128)(2,1)S(1)} %get-tuple-element.46), channel_id=1, source_target_pairs={{0,224},{32,64},{64,32},{96,128},{128,96},{160,192},{192,160},{224... | collective-permute-start | bytes 393224 | tf_op jit(solution)/shard_map/ppermute | solution.py:482
  84.1 9.7 %collective-permute-start.6 = (bf16[512,128]{1,0:T(8,128)(2,1)S(1)}, bf16[512,128]{1,0:T(8,128)(2,1)S(1)}, u32[]{:S(2)}, u32[]{:S(2)}) collective-permute-start(bf16[512,128]{1,0:T(8,128)(2,1)S(1)} %get-tuple-element.44), channel_id=1, source_target_pairs={{0,32},{32,0},{64,96},{96,64},{128,160},{160,128},{192,224},{224,1... | collective-permute-start | bytes 393224 | tf_op jit(solution)/shard_map/ppermute | solution.py:482
  84.2 9.6 %collective-permute-start.7 = (bf16[512,128]{1,0:T(8,128)(2,1)S(1)}, bf16[512,128]{1,0:T(8,128)(2,1)S(1)}, u32[]{:S(2)}, u32[]{:S(2)}) collective-permute-start(bf16[512,128]{1,0:T(8,128)(2,1)S(1)} %get-tuple-element.45), channel_id=1, source_target_pairs={{0,224},{32,64},{64,32},{96,128},{128,96},{160,192},{192,160},{224... | collective-permute-start | bytes 393224 | tf_op jit(solution)/shard_map/ppermute | solution.py:482
  88.7 23.7 %copy-start.2 = (bf16[1024,1024]{1,0:T(8,128)(2,1)S(1)}, bf16[1024,1024]{1,0:T(8,128)(2,1)}, u32[]{:S(2)}) copy-start(bf16[1024,1024]{1,0:T(8,128)(2,1)} %copy-done.1) | copy-start | bytes 6291460
  88.7 8.4 %collective-permute-start.11 = (bf16[512,128]{1,0:T(8,128)(2,1)S(1)}, bf16[512,128]{1,0:T(8,128)(2,1)S(1)}, u32[]{:S(2)}, u32[]{:S(2)}) collective-permute-start(bf16[512,128]{1,0:T(8,128)(2,1)S(1)} %get-tuple-element.48), channel_id=1, source_target_pairs={{0,64},{32,96},{64,0},{96,32},{128,192},{160,224},{192,128},{224,1... | collective-permute-start | bytes 393224 | tf_op jit(solution)/shard_map/ppermute | solution.py:482
  89.8 9.4 %collective-permute-start.12 = (bf16[512,128]{1,0:T(8,128)(2,1)S(1)}, bf16[512,128]{1,0:T(8,128)(2,1)S(1)}, u32[]{:S(2)}, u32[]{:S(2)}) collective-permute-start(bf16[512,128]{1,0:T(8,128)(2,1)S(1)} %get-tuple-element.49), channel_id=1, source_target_pairs={{0,192},{32,224},{64,128},{96,160},{128,64},{160,96},{192,0},{224,... | collective-permute-start | bytes 393224 | tf_op jit(solution)/shard_map/ppermute | solution.py:482
  99.9 12.5 %all-to-all-start.2 = ((bf16[8,64,128]{2,1,0:T(8,128)(2,1)}), bf16[8,64,128]{2,1,0:T(8,128)(2,1)S(1)}, u32[]{:S(2)}, u32[]{:S(2)}) async-start(bf16[8,64,128]{2,1,0:T(8,128)(2,1)} %add_groups.1), calls=%async_computation.2 | async-start | bytes 262144 | tf_op jit(solution)/shard_map/all_to_all | solution.py:544

commit v8 on v7

--- a/solution.py
+++ b/solution.py
@@ -442,16 +442,30 @@
     )(*args)
 
 
-def total_kernel(own, other, *refs):
-    total = add(own[0], other[0], *(r[...] for r in refs[:-1]))
-    refs[-1][...] = total.astype(jnp.bfloat16).reshape(HEADS, ROWS, HEAD)
+def here_kernel(own, other, side_a, side_b, out):
+    out[...] = add(own[0], other[0], side_a[...], side_b[...])
+
+
+def here_sum(*parts):
+    return pl.pallas_call(
+        here_kernel,
+        out_shape=jax.ShapeDtypeStruct((HALF, HEAD), jnp.float32),
+        in_specs=[VM] * 4,
+        out_specs=VM,
+        compiler_params=params(12),
+        name="add_here",
+    )(*parts)
+
+
+def total_kernel(here, a, b, out):
+    out[...] = add(here[...], a[...], b[...]).astype(jnp.bfloat16).reshape(HEADS, ROWS, HEAD)
 
 
 def total(*parts):
     return pl.pallas_call(
         total_kernel,
         out_shape=jax.ShapeDtypeStruct((HEADS, ROWS, HEAD), jnp.bfloat16),
-        in_specs=[VM] * 6,
+        in_specs=[VM] * 3,
         out_specs=VM,
         compiler_params=params(12),
         name="add_groups",
@@ -540,7 +554,7 @@
     side_a, side_b = side(where, own, other, out_a)
     side_a, side_b = move(side_a, 1), move(side_b, -1)
     out_a, out_b = near(where, own, other, move(out_a, 1), move(out_b, -1), cross(across))
-    hist = total(own, other, side_a, side_b, move(out_a, 2, 2), move(out_b, -2, 2))
+    hist = total(here_sum(own, other, side_a, side_b), move(out_a, 2, 2), move(out_b, -2, 2))
     hist = lax.all_to_all(hist, W, split_axis=0, concat_axis=0, tiled=True)
     return tail(hist, self_term, gate, tokens, w2, where, candidate_count)
 

time: 115 us -> 115 us (level)
  transfers between devices with their start and end apart: 16 -> 16, of which waited for: 11 -> 10; matrix products, arithmetic and copies ran while one was open for 1% -> 1% of each run, Pallas kernels for 12% -> 13%
where the time goes in v8:
time: 115 us; the launch traced here: 114 us
  starting transfers between devices  46 us (40%)
  waiting for transfers between devices  35.3 us (31%)
  Pallas kernels  27.5 us (24%)
  local copies, waits for them, and re-layouts  3.75 us (3%)
  between operations  1.62 us (1%)
    ppermute x10, waiting for transfers between devices, move(): return lax.ppermute(value, 'z', pairs)  24.3 us
    ppermute x10, starting transfers between devices, move(): return lax.ppermute(value, 'z', pairs)  23.2 us
    all_to_all x1, starting transfers between devices, local(): hist = lax.all_to_all(hist, W, split_axis=0, concat_axis=0, tiled=True)  7.24 us
    pallas_call x1, Pallas kernels, attend_first(): pl.pallas_call(first_kernel, out_shape=(jax.ShapeDtypeStruct((NZ, HALF, H...  6.75 us
    pallas_call x1, Pallas kernels, rest(): pl.pallas_call(rest_kernel, out_shape=(jax.ShapeDtypeStruct((ROWS, D), jn...  6.12 us
    all_to_all x1, starting transfers between devices, local(): q_mine = lax.all_to_all(q_send, W, split_axis=0, concat_axis=0, tiled=True)  5.94 us
    all_to_all x1, starting transfers between devices, local(): kv = lax.all_to_all(packed, M, split_axis=0, concat_axis=0, tiled=True)  5.91 us
    all_to_all x1, waiting for transfers between devices, local(): hist = lax.all_to_all(hist, W, split_axis=0, concat_axis=0, tiled=True)  4.6 us
  transfers between devices with their start and end apart: 16, of which 10 were waited for; matrix products, arithmetic and copies ran while one was open for 1% of the time, Pallas kernels for 13%

profile of v8, /device:TPU:2, one launch (start us, length us, event | category | flops | bytes accessed | tf_op | source)
XLA Modules:
  0.0 114.2 jit_solution(2130013456837883474)
XLA Ops:
  0.0 3.1 %project_query.1 = (bf16[64,1024]{1,0:T(8,128)(2,1)S(1)}, bf16[8,64,128]{2,1,0:T(8,128)(2,1)}) custom-call(bf16[64,1024]{1,0:T(8,128)(2,1)} %tokens.5, bf16[1024,4096]{1,0:T(8,128)(2,1)} %w.3), custom_call_target="tpu_custom_call" | custom-call | tf_op jit(solution)/shard_map/project_query/pallas_call | solution.py:94
  3.1 5.9 %all-to-all-start = ((bf16[8,64,128]{2,1,0:T(8,128)(2,1)}), bf16[8,64,128]{2,1,0:T(8,128)(2,1)S(1)}, u32[]{:S(2)}, u32[]{:S(2)}) async-start(bf16[8,64,128]{2,1,0:T(8,128)(2,1)} %get-tuple-element.29), calls=%async_computation | async-start | bytes 262144 | tf_op jit(solution)/shard_map/all_to_all | solution.py:538
  9.0 0.5 pack_history.1
  9.6 1.8 %copy-done = bf16[16,2,14,32,128]{4,3,2,1,0:T(8,128)(2,1)} copy-done((bf16[16,2,14,32,128]{4,3,2,1,0:T(8,128)(2,1)}, bf16[16,2,14,32,128]{4,3,2,1,0:T(8,128)(2,1)S(1)}, u32[]{:S(2)}) %copy-start) | copy-done | bytes 3670040
  11.4 2.9 %all-to-all-done = bf16[8,64,128]{2,1,0:T(8,128)(2,1)S(1)} async-done(((bf16[8,64,128]{2,1,0:T(8,128)(2,1)}), bf16[8,64,128]{2,1,0:T(8,128)(2,1)S(1)}, u32[]{:S(2)}, u32[]{:S(2)}) %all-to-all-start) | async-done | bytes 131104 | tf_op jit(solution)/shard_map/all_to_all | solution.py:538
  14.3 5.9 %all-to-all-start.1 = ((bf16[16,2,14,32,128]{4,3,2,1,0:T(8,128)(2,1)}), bf16[16,2,14,32,128]{4,3,2,1,0:T(8,128)(2,1)}, u32[]{:S(2)}, u32[]{:S(2)}) async-start(bf16[16,2,14,32,128]{4,3,2,1,0:T(8,128)(2,1)} %copy-done), calls=%async_computation.1 | async-start | bytes 7340032 | tf_op jit(solution)/shard_map/all_to_all | solution.py:541
  20.9 0.1 copy.13
  21.0 0.1 concatenate.20
  21.2 0.1 copy.14
  21.3 0.1 concatenate.21
  21.4 0.1 concatenate.24
  21.5 4.7 %collective-permute-start = (bf16[528,128]{1,0:T(8,128)(2,1)S(1)}, bf16[528,128]{1,0:T(8,128)(2,1)S(1)}, u32[]{:S(2)}, u32[]{:S(2)}) collective-permute-start(bf16[528,128]{1,0:T(8,128)(2,1)S(1)} %pad_maximum_fusion.own), channel_id=1, source_target_pairs={{0,96},{32,192},{64,160},{96,0},{128,224},{160,64},{192,32},{224,1... | collective-permute-start | bytes 405512 | tf_op jit(solution)/shard_map/ppermute | solution.py:496
  26.2 2.2 %collective-permute-start.1 = (bf16[528,128]{1,0:T(8,128)(2,1)S(1)}, bf16[528,128]{1,0:T(8,128)(2,1)S(1)}, u32[]{:S(2)}, u32[]{:S(2)}) collective-permute-start(bf16[528,128]{1,0:T(8,128)(2,1)S(1)} %pad_maximum_fusion.own), channel_id=1, source_target_pairs={{0,160},{32,128},{64,224},{96,192},{128,32},{160,0},{192,96},{224,... | collective-permute-start | bytes 405512 | tf_op jit(solution)/shard_map/ppermute | solution.py:496
  28.4 0.1 pad_add_fusion.where
  28.5 2.2 %collective-permute-done.far_a = bf16[528,128]{1,0:T(8,128)(2,1)S(1)} collective-permute-done((bf16[528,128]{1,0:T(8,128)(2,1)S(1)}, bf16[528,128]{1,0:T(8,128)(2,1)S(1)}, u32[]{:S(2)}, u32[]{:S(2)}) %collective-permute-start) | collective-permute-done | bytes 135200 | tf_op jit(solution)/shard_map/ppermute | solution.py:496
  30.7 6.3 %collective-permute-done.1.far_b = bf16[528,128]{1,0:T(8,128)(2,1)S(1)} collective-permute-done((bf16[528,128]{1,0:T(8,128)(2,1)S(1)}, bf16[528,128]{1,0:T(8,128)(2,1)S(1)}, u32[]{:S(2)}, u32[]{:S(2)}) %collective-permute-start.1) | collective-permute-done | bytes 135200 | tf_op jit(solution)/shard_map/ppermute | solution.py:496
  37.0 0.6 bundle_queries.1
  37.7 1.6 %collective-permute-start.2 = (bf16[1328,128]{1,0:T(8,128)(2,1)S(1)}, bf16[1328,128]{1,0:T(8,128)(2,1)S(1)}, u32[]{:S(2)}, u32[]{:S(2)}) collective-permute-start(bf16[1328,128]{1,0:T(8,128)(2,1)S(1)} %get-tuple-element.36), channel_id=1, source_target_pairs={{0,32},{32,0},{64,96},{96,64},{128,160},{160,128},{192,224},{224,1... | collective-permute-start | bytes 1019912 | tf_op jit(solution)/shard_map/ppermute | solution.py:496
  39.3 2.4 %collective-permute-start.3 = (bf16[1328,128]{1,0:T(8,128)(2,1)S(1)}, bf16[1328,128]{1,0:T(8,128)(2,1)S(1)}, u32[]{:S(2)}, u32[]{:S(2)}) collective-permute-start(bf16[1328,128]{1,0:T(8,128)(2,1)S(1)} %get-tuple-element.37), channel_id=1, source_target_pairs={{0,224},{32,64},{64,32},{96,128},{128,96},{160,192},{192,160},{224... | collective-permute-start | bytes 1019912 | tf_op jit(solution)/shard_map/ppermute | solution.py:496
  41.6 5.7 %collective-permute-done.2.near_a = bf16[1328,128]{1,0:T(8,128)(2,1)S(1)} collective-permute-done((bf16[1328,128]{1,0:T(8,128)(2,1)S(1)}, bf16[1328,128]{1,0:T(8,128)(2,1)S(1)}, u32[]{:S(2)}, u32[]{:S(2)}) %collective-permute-start.2) | collective-permute-done | bytes 340000 | tf_op jit(solution)/shard_map/ppermute | solution.py:496
  47.4 2.7 %collective-permute-done.3.near_b = bf16[1328,128]{1,0:T(8,128)(2,1)S(1)} collective-permute-done((bf16[1328,128]{1,0:T(8,128)(2,1)S(1)}, bf16[1328,128]{1,0:T(8,128)(2,1)S(1)}, u32[]{:S(2)}, u32[]{:S(2)}) %collective-permute-start.3) | collective-permute-done | bytes 340000 | tf_op jit(solution)/shard_map/ppermute | solution.py:496
  50.1 0.6 stack_queries.1.q_own.q
  50.7 0.1 collective-permute-start.4
  50.8 6.1 %project_rest.1 = (bf16[64,1024]{1,0:T(8,128)(2,1)S(1)}, f32[64,1024]{1,0:T(8,128)S(1)}, bf16[1024,1024]{1,0:T(8,128)(2,1)S(1)}) custom-call(bf16[64,1024]{1,0:T(8,128)(2,1)S(1)} %copy-done.4, bf16[1024,4096]{1,0:T(8,128)(2,1)} %w.3, bf16[64,1024]{1,0:T(8,128)(2,1)S(1)} %get-tuple-element.30.after.q, f32[8]{0:T(128)S(1)} %copy-done.6, bf16[1024,1024]{1,0:T(8,128)(2,1)} %w2.1), custom_call_target="tpu_custom_call" | custom-call | tf_op jit(solution)/shard_map/project_rest/pallas_call | solution.py:145
  56.9 1.4 %copy-done.1 = bf16[1024,1024]{1,0:T(8,128)(2,1)} copy-done((bf16[1024,1024]{1,0:T(8,128)(2,1)}, bf16[1024,1024]{1,0:T(8,128)(2,1)S(1)}, u32[]{:S(2)}) %copy-start.1) | copy-done | bytes 2097176
  58.4 2.3 %read_tables.1.plan = s32[4,16]{1,0:T(4,128)S(1)} custom-call(s32[4]{0:T(128)S(1)} %pad_add_fusion.where, bf16[8,528,128]{2,1,0:T(8,128)(2,1)S(1)} %stack_queries.1.q_own.q, bf16[8,528,128]{2,1,0:T(8,128)(2,1)S(1)} %collective-permute-done.4.q_other), custom_call_target="tpu_custom_call" | custom-call | tf_op jit(solution)/shard_map/read_tables/pallas_call | solution.py:271
  60.6 3.5 %all-to-all-done.1.kv = bf16[16,2,14,32,128]{4,3,2,1,0:T(8,128)(2,1)} async-done(((bf16[16,2,14,32,128]{4,3,2,1,0:T(8,128)(2,1)}), bf16[16,2,14,32,128]{4,3,2,1,0:T(8,128)(2,1)}, u32[]{:S(2)}, u32[]{:S(2)}) %all-to-all-start.1) | async-done | bytes 3670048 | tf_op jit(solution)/shard_map/all_to_all | solution.py:541
  64.1 6.8 %attend_first.1 = (f32[8,512,128]{2,1,0:T(8,128)S(1)}, bf16[8,512,128]{2,1,0:T(8,128)(2,1)S(1)}, bf16[14,16,2,32,128]{4,3,2,1,0:T(8,128)(2,1)S(1)}) custom-call(s32[4,16]{1,0:T(4,128)S(1)} %read_tables.1.plan, s32[4]{0:T(128)S(1)} %pad_add_fusion.where, f32[8,14]{1,0:T(8,128)S(1)} %copy-done.5, bf16[8,528,128]{2,1,0:T(8,128)(2,1)S(1)} %stack_queries.1.q_own.q, ...), custom_call_target="tpu_custom_call" | custom-call | tf_op jit(solution)/shard_map/attend_first/pallas_call | solution.py:337
  70.9 0.1 collective-permute-start.5
  71.0 2.9 %attend_second.1.a.own = bf16[8,512,128]{2,1,0:T(8,128)(2,1)S(1)} custom-call(s32[4,16]{1,0:T(4,128)S(1)} %read_tables.1.plan, s32[4]{0:T(128)S(1)} %pad_add_fusion.where, f32[8,14]{1,0:T(8,128)S(1)} %copy-done.5, bf16[8,528,128]{2,1,0:T(8,128)(2,1)S(1)} %stack_queries.1.q_own.q, bf16[14,16,2,32,128]{4,3,2,1,0:T(8,128)(2,1)S(1)} %get-tuple-element.40.blocks, ...), custom_call_target="tpu_custom_call" | custom-call | tf_op jit(solution)/shard_map/attend_second/pallas_call | solution.py:353
  73.9 0.6 add_far.1
  74.6 3.5 %collective-permute-start.10 = (bf16[512,128]{1,0:T(8,128)(2,1)S(1)}, bf16[512,128]{1,0:T(8,128)(2,1)S(1)}, u32[]{:S(2)}, u32[]{:S(2)}) collective-permute-start(bf16[512,128]{1,0:T(8,128)(2,1)S(1)} %get-tuple-element.47), channel_id=1, source_target_pairs={{0,64},{16,208},{32,96},{48,240},{64,0},{80,144},{96,32},{112,176}... | collective-permute-start | bytes 393224 | tf_op jit(solution)/shard_map/ppermute | solution.py:504
  78.1 2.3 %collective-permute-start.8 = (bf16[512,128]{1,0:T(8,128)(2,1)S(1)}, bf16[512,128]{1,0:T(8,128)(2,1)S(1)}, u32[]{:S(2)}, u32[]{:S(2)}) collective-permute-start(bf16[512,128]{1,0:T(8,128)(2,1)S(1)} %get-tuple-element.43.after), channel_id=1, source_target_pairs={{0,32},{32,0},{64,96},{96,64},{128,160},{160,128},{192,224},{224,1... | collective-permute-start | bytes 393224 | tf_op jit(solution)/shard_map/ppermute | solution.py:496
  80.4 2.3 %collective-permute-start.9 = (bf16[512,128]{1,0:T(8,128)(2,1)S(1)}, bf16[512,128]{1,0:T(8,128)(2,1)S(1)}, u32[]{:S(2)}, u32[]{:S(2)}) collective-permute-start(bf16[512,128]{1,0:T(8,128)(2,1)S(1)} %get-tuple-element.46), channel_id=1, source_target_pairs={{0,224},{32,64},{64,32},{96,128},{128,96},{160,192},{192,160},{224... | collective-permute-start | bytes 393224 | tf_op jit(solution)/shard_map/ppermute | solution.py:496
  82.7 0.6 add_side.1
  83.3 0.1 collective-permute-start.6
  83.5 2.3 %collective-permute-start.7 = (bf16[512,128]{1,0:T(8,128)(2,1)S(1)}, bf16[512,128]{1,0:T(8,128)(2,1)S(1)}, u32[]{:S(2)}, u32[]{:S(2)}) collective-permute-start(bf16[512,128]{1,0:T(8,128)(2,1)S(1)} %get-tuple-element.45), channel_id=1, source_target_pairs={{0,224},{32,64},{64,32},{96,128},{128,96},{160,192},{192,160},{224... | collective-permute-start | bytes 393224 | tf_op jit(solution)/shard_map/ppermute | solution.py:496
  85.8 2.2 %collective-permute-done.9.near_b = bf16[512,128]{1,0:T(8,128)(2,1)S(1)} collective-permute-done((bf16[512,128]{1,0:T(8,128)(2,1)S(1)}, bf16[512,128]{1,0:T(8,128)(2,1)S(1)}, u32[]{:S(2)}, u32[]{:S(2)}) %collective-permute-start.9) | collective-permute-done | bytes 131104 | tf_op jit(solution)/shard_map/ppermute | solution.py:496
  88.0 0.7 add_near.1
  88.7 0.3 collective-permute-start.11
  89.0 5.0 %collective-permute-start.12 = (bf16[512,128]{1,0:T(8,128)(2,1)S(1)}, bf16[512,128]{1,0:T(8,128)(2,1)S(1)}, u32[]{:S(2)}, u32[]{:S(2)}) collective-permute-start(bf16[512,128]{1,0:T(8,128)(2,1)S(1)} %get-tuple-element.49), channel_id=1, source_target_pairs={{0,192},{32,224},{64,128},{96,160},{128,64},{160,96},{192,0},{224,... | collective-permute-start | bytes 393224 | tf_op jit(solution)/shard_map/ppermute | solution.py:496
  94.0 0.1 add_here.1.here
  94.0 3.3 %collective-permute-done.11.a = bf16[512,128]{1,0:T(8,128)(2,1)S(1)} collective-permute-done((bf16[512,128]{1,0:T(8,128)(2,1)S(1)}, bf16[512,128]{1,0:T(8,128)(2,1)S(1)}, u32[]{:S(2)}, u32[]{:S(2)}) %collective-permute-start.11) | collective-permute-done | bytes 131104 | tf_op jit(solution)/shard_map/ppermute | solution.py:496
  97.3 1.8 %collective-permute-done.12.b = bf16[512,128]{1,0:T(8,128)(2,1)S(1)} collective-permute-done((bf16[512,128]{1,0:T(8,128)(2,1)S(1)}, bf16[512,128]{1,0:T(8,128)(2,1)S(1)}, u32[]{:S(2)}, u32[]{:S(2)}) %collective-permute-start.12) | collective-permute-done | bytes 131104 | tf_op jit(solution)/shard_map/ppermute | solution.py:496
  99.2 0.7 add_groups.1
  99.9 7.2 %all-to-all-start.2 = ((bf16[8,64,128]{2,1,0:T(8,128)(2,1)}), bf16[8,64,128]{2,1,0:T(8,128)(2,1)S(1)}, u32[]{:S(2)}, u32[]{:S(2)}) async-start(bf16[8,64,128]{2,1,0:T(8,128)(2,1)} %add_groups.1), calls=%async_computation.2 | async-start | bytes 262144 | tf_op jit(solution)/shard_map/all_to_all | solution.py:558
  107.8 4.6 %all-to-all-done.2.hist = bf16[8,64,128]{2,1,0:T(8,128)(2,1)S(1)} async-done(((bf16[8,64,128]{2,1,0:T(8,128)(2,1)}), bf16[8,64,128]{2,1,0:T(8,128)(2,1)S(1)}, u32[]{:S(2)}, u32[]{:S(2)}) %all-to-all-start.2) | async-done | bytes 131104 | tf_op jit(solution)/shard_map/all_to_all | solution.py:558
  112.4 1.8 %output.1 = bf16[64,1024]{1,0:T(8,128)(2,1)} custom-call(bf16[8,64,128]{2,1,0:T(8,128)(2,1)S(1)} %all-to-all-done.2.hist, f32[64,1024]{1,0:T(8,128)S(1)} %get-tuple-element.50.self_term, bf16[64,1024]{1,0:T(8,128)(2,1)S(1)} %get-tuple-element.51.gate, bf16[64,1024]{1,0:T(8,128)(2,1)S(1)} %copy-done.4, bf16[1024,1024]{1,0:T(8,128)(2,1)S(1)} %copy-done.2, ...), custom_call_target="tpu_custom_call" | custom-call | tf_op jit(solution)/shard_map/output/pallas_call | solution.py:484
  (27 shorter events, 0.1 us)
Async XLA Ops:
  0.0 9.0 %copy-start.3 = (bf16[14,32,2048]{2,1,0:T(8,128)(2,1)S(1)}, bf16[14,32,2048]{2,1,0:T(8,128)(2,1)}, u32[]{:S(2)}) copy-start(bf16[14,32,2048]{2,1,0:T(8,128)(2,1)} %pool.1) | copy-start | bytes 5505028
  3.1 11.2 %all-to-all-start = ((bf16[8,64,128]{2,1,0:T(8,128)(2,1)}), bf16[8,64,128]{2,1,0:T(8,128)(2,1)S(1)}, u32[]{:S(2)}, u32[]{:S(2)}) async-start(bf16[8,64,128]{2,1,0:T(8,128)(2,1)} %get-tuple-element.29), calls=%async_computation | async-start | bytes 262144 | tf_op jit(solution)/shard_map/all_to_all | solution.py:538
  9.5 1.8 %copy-start = (bf16[16,2,14,32,128]{4,3,2,1,0:T(8,128)(2,1)}, bf16[16,2,14,32,128]{4,3,2,1,0:T(8,128)(2,1)S(1)}, u32[]{:S(2)}) copy-start(bf16[16,2,14,32,128]{4,3,2,1,0:T(8,128)(2,1)S(1)} %pack_history.1) | copy-start | bytes 11010052
  11.4 9.5 %copy-start.7 = (s32[1,16,2]{1,2,0:T(2,128)S(1)}, s32[1,16,2]{1,2,0:T(2,128)}, u32[]{:S(2)}) copy-start(s32[1,16,2]{1,2,0:T(2,128)} %param.18) | copy-start | bytes 388
  11.4 9.8 %copy-start.8 = (s32[1,16,2]{1,2,0:T(2,128)S(1)}, s32[1,16,2]{1,2,0:T(2,128)}, u32[]{:S(2)}) copy-start(s32[1,16,2]{1,2,0:T(2,128)} %param.19) | copy-start | bytes 388
  14.3 49.8 %all-to-all-start.1 = ((bf16[16,2,14,32,128]{4,3,2,1,0:T(8,128)(2,1)}), bf16[16,2,14,32,128]{4,3,2,1,0:T(8,128)(2,1)}, u32[]{:S(2)}, u32[]{:S(2)}) async-start(bf16[16,2,14,32,128]{4,3,2,1,0:T(8,128)(2,1)} %copy-done), calls=%async_computation.1 | async-start | bytes 7340032 | tf_op jit(solution)/shard_map/all_to_all | solution.py:541
  20.2 30.6 %copy-start.4 = (bf16[64,1024]{1,0:T(8,128)(2,1)S(1)}, bf16[64,1024]{1,0:T(8,128)(2,1)}, u32[]{:S(2)}) copy-start(bf16[64,1024]{1,0:T(8,128)(2,1)} %tokens.5) | copy-start | bytes 393220
  20.2 30.6 %copy-start.6 = (f32[8]{0:T(128)S(1)}, f32[8]{0:T(128)}, u32[]{:S(2)}) copy-start(f32[8]{0:T(128)} %self_bias.1) | copy-start | bytes 100
  21.5 9.2 %collective-permute-start = (bf16[528,128]{1,0:T(8,128)(2,1)S(1)}, bf16[528,128]{1,0:T(8,128)(2,1)S(1)}, u32[]{:S(2)}, u32[]{:S(2)}) collective-permute-start(bf16[528,128]{1,0:T(8,128)(2,1)S(1)} %pad_maximum_fusion.own), channel_id=1, source_target_pairs={{0,96},{32,192},{64,160},{96,0},{128,224},{160,64},{192,32},{224,1... | collective-permute-start | bytes 405512 | tf_op jit(solution)/shard_map/ppermute | solution.py:496
  26.2 10.8 %collective-permute-start.1 = (bf16[528,128]{1,0:T(8,128)(2,1)S(1)}, bf16[528,128]{1,0:T(8,128)(2,1)S(1)}, u32[]{:S(2)}, u32[]{:S(2)}) collective-permute-start(bf16[528,128]{1,0:T(8,128)(2,1)S(1)} %pad_maximum_fusion.own), channel_id=1, source_target_pairs={{0,160},{32,128},{64,224},{96,192},{128,32},{160,0},{192,96},{224,... | collective-permute-start | bytes 405512 | tf_op jit(solution)/shard_map/ppermute | solution.py:496
  37.7 9.7 %collective-permute-start.2 = (bf16[1328,128]{1,0:T(8,128)(2,1)S(1)}, bf16[1328,128]{1,0:T(8,128)(2,1)S(1)}, u32[]{:S(2)}, u32[]{:S(2)}) collective-permute-start(bf16[1328,128]{1,0:T(8,128)(2,1)S(1)} %get-tuple-element.36), channel_id=1, source_target_pairs={{0,32},{32,0},{64,96},{96,64},{128,160},{160,128},{192,224},{224,1... | collective-permute-start | bytes 1019912 | tf_op jit(solution)/shard_map/ppermute | solution.py:496
  39.3 10.8 %collective-permute-start.3 = (bf16[1328,128]{1,0:T(8,128)(2,1)S(1)}, bf16[1328,128]{1,0:T(8,128)(2,1)S(1)}, u32[]{:S(2)}, u32[]{:S(2)}) collective-permute-start(bf16[1328,128]{1,0:T(8,128)(2,1)S(1)} %get-tuple-element.37), channel_id=1, source_target_pairs={{0,224},{32,64},{64,32},{96,128},{128,96},{160,192},{192,160},{224... | collective-permute-start | bytes 1019912 | tf_op jit(solution)/shard_map/ppermute | solution.py:496
  50.7 7.7 %collective-permute-start.4 = (bf16[8,528,128]{2,1,0:T(8,128)(2,1)S(1)}, bf16[8,528,128]{2,1,0:T(8,128)(2,1)S(1)}, u32[]{:S(2)}, u32[]{:S(2)}) collective-permute-start(bf16[8,528,128]{2,1,0:T(8,128)(2,1)S(1)} %stack_queries.1.q_own.q), channel_id=1, source_target_pairs={{0,16},{16,0},{1,17},{17,1},{2,18},{18,2},{3,19},{19,3},{4,20},{20... | collective-permute-start | bytes 3244040 | tf_op jit(solution)/shard_map/ppermute | solution.py:508
  56.9 1.4 %copy-start.1 = (bf16[1024,1024]{1,0:T(8,128)(2,1)}, bf16[1024,1024]{1,0:T(8,128)(2,1)S(1)}, u32[]{:S(2)}) copy-start(bf16[1024,1024]{1,0:T(8,128)(2,1)S(1)} %get-tuple-element.52.w) | copy-start | bytes 6291460
  58.4 5.7 %copy-start.5 = (f32[8,14]{1,0:T(8,128)S(1)}, f32[8,14]{1,0:T(8,128)}, u32[]{:S(2)}) copy-start(f32[8,14]{1,0:T(8,128)} %bias.3) | copy-start | bytes 1348
  70.9 3.1 %collective-permute-start.5 = (bf16[8,512,128]{2,1,0:T(8,128)(2,1)S(1)}, bf16[8,512,128]{2,1,0:T(8,128)(2,1)S(1)}, u32[]{:S(2)}, u32[]{:S(2)}) collective-permute-start(bf16[8,512,128]{2,1,0:T(8,128)(2,1)S(1)} %get-tuple-element.42), channel_id=1, source_target_pairs={{0,16},{16,0},{1,17},{17,1},{2,18},{18,2},{3,19},{19,3},{4,20},{20... | collective-permute-start | bytes 3145736 | tf_op jit(solution)/shard_map/ppermute | solution.py:508
  74.6 11.2 %collective-permute-start.10 = (bf16[512,128]{1,0:T(8,128)(2,1)S(1)}, bf16[512,128]{1,0:T(8,128)(2,1)S(1)}, u32[]{:S(2)}, u32[]{:S(2)}) collective-permute-start(bf16[512,128]{1,0:T(8,128)(2,1)S(1)} %get-tuple-element.47), channel_id=1, source_target_pairs={{0,64},{16,208},{32,96},{48,240},{64,0},{80,144},{96,32},{112,176}... | collective-permute-start | bytes 393224 | tf_op jit(solution)/shard_map/ppermute | solution.py:504
  78.1 7.7 %collective-permute-start.8 = (bf16[512,128]{1,0:T(8,128)(2,1)S(1)}, bf16[512,128]{1,0:T(8,128)(2,1)S(1)}, u32[]{:S(2)}, u32[]{:S(2)}) collective-permute-start(bf16[512,128]{1,0:T(8,128)(2,1)S(1)} %get-tuple-element.43.after), channel_id=1, source_target_pairs={{0,32},{32,0},{64,96},{96,64},{128,160},{160,128},{192,224},{224,1... | collective-permute-start | bytes 393224 | tf_op jit(solution)/shard_map/ppermute | solution.py:496
  80.4 7.6 %collective-permute-start.9 = (bf16[512,128]{1,0:T(8,128)(2,1)S(1)}, bf16[512,128]{1,0:T(8,128)(2,1)S(1)}, u32[]{:S(2)}, u32[]{:S(2)}) collective-permute-start(bf16[512,128]{1,0:T(8,128)(2,1)S(1)} %get-tuple-element.46), channel_id=1, source_target_pairs={{0,224},{32,64},{64,32},{96,128},{128,96},{160,192},{192,160},{224... | collective-permute-start | bytes 393224 | tf_op jit(solution)/shard_map/ppermute | solution.py:496
  83.3 10.6 %collective-permute-start.6 = (bf16[512,128]{1,0:T(8,128)(2,1)S(1)}, bf16[512,128]{1,0:T(8,128)(2,1)S(1)}, u32[]{:S(2)}, u32[]{:S(2)}) collective-permute-start(bf16[512,128]{1,0:T(8,128)(2,1)S(1)} %get-tuple-element.44), channel_id=1, source_target_pairs={{0,32},{32,0},{64,96},{96,64},{128,160},{160,128},{192,224},{224,1... | collective-permute-start | bytes 393224 | tf_op jit(solution)/shard_map/ppermute | solution.py:496
  83.5 10.5 %collective-permute-start.7 = (bf16[512,128]{1,0:T(8,128)(2,1)S(1)}, bf16[512,128]{1,0:T(8,128)(2,1)S(1)}, u32[]{:S(2)}, u32[]{:S(2)}) collective-permute-start(bf16[512,128]{1,0:T(8,128)(2,1)S(1)} %get-tuple-element.45), channel_id=1, source_target_pairs={{0,224},{32,64},{64,32},{96,128},{128,96},{160,192},{192,160},{224... | collective-permute-start | bytes 393224 | tf_op jit(solution)/shard_map/ppermute | solution.py:496
  88.7 23.7 %copy-start.2 = (bf16[1024,1024]{1,0:T(8,128)(2,1)S(1)}, bf16[1024,1024]{1,0:T(8,128)(2,1)}, u32[]{:S(2)}) copy-start(bf16[1024,1024]{1,0:T(8,128)(2,1)} %copy-done.1) | copy-start | bytes 6291460
  88.7 8.7 %collective-permute-start.11 = (bf16[512,128]{1,0:T(8,128)(2,1)S(1)}, bf16[512,128]{1,0:T(8,128)(2,1)S(1)}, u32[]{:S(2)}, u32[]{:S(2)}) collective-permute-start(bf16[512,128]{1,0:T(8,128)(2,1)S(1)} %get-tuple-element.48), channel_id=1, source_target_pairs={{0,64},{32,96},{64,0},{96,32},{128,192},{160,224},{192,128},{224,1... | collective-permute-start | bytes 393224 | tf_op jit(solution)/shard_map/ppermute | solution.py:496
  89.0 10.2 %collective-permute-start.12 = (bf16[512,128]{1,0:T(8,128)(2,1)S(1)}, bf16[512,128]{1,0:T(8,128)(2,1)S(1)}, u32[]{:S(2)}, u32[]{:S(2)}) collective-permute-start(bf16[512,128]{1,0:T(8,128)(2,1)S(1)} %get-tuple-element.49), channel_id=1, source_target_pairs={{0,192},{32,224},{64,128},{96,160},{128,64},{160,96},{192,0},{224,... | collective-permute-start | bytes 393224 | tf_op jit(solution)/shard_map/ppermute | solution.py:496
  99.9 12.5 %all-to-all-start.2 = ((bf16[8,64,128]{2,1,0:T(8,128)(2,1)}), bf16[8,64,128]{2,1,0:T(8,128)(2,1)S(1)}, u32[]{:S(2)}, u32[]{:S(2)}) async-start(bf16[8,64,128]{2,1,0:T(8,128)(2,1)} %add_groups.1), calls=%async_computation.2 | async-start | bytes 262144 | tf_op jit(solution)/shard_map/all_to_all | solution.py:558
